TPU v7x, 1024 devices: a whole 4x4x32 slice. The times are simulated.
1024 devices in a mesh: dp: 16 (over z_lo), row: 4 (over z_hi, core), col: 16 (over x, y).
Axes of the slice: x: 4, y: 4, z: 32 (z_hi: 2, z_lo: 16; z = z_hi * 16 + z_lo), core: 2. Of those that a mesh axis runs over, the one named last changes fastest.
Arguments:
- tokens: bfloat16 [2048, 4096], P(('dp', 'col'), 'row'), may hold values from -6 to 6
- gate_weight: bfloat16 [4096, 14336], P('row', 'col'), may hold values from -0.09375 to 0.09375
- up_weight: bfloat16 [4096, 14336], P('row', 'col'), may hold values from -0.09375 to 0.09375
- mask_gate: int32 [32, 112], P('row', 'col'), may hold values 0 or 1
- mask_up: int32 [32, 112], P('row', 'col'), may hold values 0 or 1
- grad_hidden: bfloat16 [2048, 14336], P(('dp', 'row'), 'col'), may hold values from -6 to 6
Outputs:
- hidden: bfloat16 [2048, 14336], P(('dp', 'row'), 'col')
- grad_tokens: bfloat16 [2048, 4096], P(('dp', 'col'), 'row')
- grad_gate: float32 [4096, 14336], P(('row', 'dp'), 'col')
- grad_up: float32 [4096, 14336], P(('row', 'dp'), 'col')
All inputs are finite; a program needn't handle non-finite values. No bound on the sum of `mask_gate` or of `mask_up` on one device may be relied on, other than what follows from the above.
Results may differ from a plain program's by a relative error of at most 0.0049.
Values may be sent and summed in bfloat16 or wider, within the bound.
No kernel may reach another device: no remote copies, remote signals or barrier semaphores. Data moves between devices by JAX's collectives and lax.ppermute only.
A program may use at most 64 MiB of HBM per device.

v0:
```python
import jax
import jax.numpy as jnp
from jax import lax
from jax.sharding import PartitionSpec as P

BLK = 128


def spread(mask_blocks):
    return jnp.repeat(jnp.repeat(mask_blocks, BLK, axis=0), BLK, axis=1)


def activate(gate_proj, up_proj, cotangent_rows):
    sigmoid_gate = jax.nn.sigmoid(gate_proj)
    activation = gate_proj * sigmoid_gate
    hidden_rows = (activation * up_proj).astype(jnp.bfloat16)
    cotangent = cotangent_rows.astype(jnp.float32)
    grad_gate_act = (
        cotangent * up_proj * sigmoid_gate * (1.0 + gate_proj * (1.0 - sigmoid_gate))
    ).astype(jnp.bfloat16)
    grad_up_act = (cotangent * activation).astype(jnp.bfloat16)
    return (hidden_rows, grad_gate_act, grad_up_act)


def body(tokens, gate_weight, up_weight, mask_gate, mask_up, grad_hidden):
    keep_gate = spread(mask_gate).astype(jnp.bfloat16)
    keep_up = spread(mask_up).astype(jnp.bfloat16)
    masked_gate = gate_weight * keep_gate
    masked_up = up_weight * keep_up
    whole_rows = lax.all_gather(tokens, "col", axis=0, tiled=True)
    part_gate = jnp.dot(whole_rows, masked_gate, preferred_element_type=jnp.float32)
    part_up = jnp.dot(whole_rows, masked_up, preferred_element_type=jnp.float32)
    gate_proj, up_proj = (
        lax.psum_scatter(part_gate, "row", scatter_dimension=0, tiled=True),
        lax.psum_scatter(part_up, "row", scatter_dimension=0, tiled=True),
    )
    hidden, gate_mine, up_mine = activate(gate_proj, up_proj, grad_hidden)
    grad_gate_act, grad_up_act = (
        lax.all_gather(gate_mine, "row", axis=0, tiled=True),
        lax.all_gather(up_mine, "row", axis=0, tiled=True),
    )
    contract = (((1,), (1,)), ((), ()))
    grad_tokens = lax.psum_scatter(
        lax.dot_general(grad_gate_act, masked_gate, contract, preferred_element_type=jnp.float32)
        + lax.dot_general(grad_up_act, masked_up, contract, preferred_element_type=jnp.float32),
        "col",
        scatter_dimension=0,
        tiled=True,
    ).astype(jnp.bfloat16)
    joined = jnp.concatenate([grad_gate_act, grad_up_act], axis=1)
    keep_both = jnp.concatenate([keep_gate, keep_up], axis=1).astype(jnp.float32)
    product = lax.dot_general(
        whole_rows, joined, (((0,), (0,)), ((), ())), preferred_element_type=jnp.float32
    )
    summed = lax.psum_scatter(product * keep_both, "dp", scatter_dimension=0, tiled=True)
    hidden_units = gate_weight.shape[1]
    return (hidden, grad_tokens, summed[:, :hidden_units], summed[:, hidden_units:])


def solution(mesh):
    placed = (
        P(("dp", "col"), "row"),
        P("row", "col"),
        P("row", "col"),
        P("row", "col"),
        P("row", "col"),
        P(("dp", "row"), "col"),
    )
    return jax.shard_map(
        body,
        mesh=mesh,
        in_specs=placed,
        out_specs=(
            P(("dp", "row"), "col"),
            P(("dp", "col"), "row"),
            P(("row", "dp"), "col"),
            P(("row", "dp"), "col"),
        ),
        check_vma=False,
    )
```

profile of v0, /device:TPU:6, one launch (start us, length us, event | category | flops | bytes accessed | tf_op | source)
XLA Modules:
  0.0 513.9 jit_solution(14432711254252319596)
XLA Ops:
  7.2 0.0 reduce-scatter.10.cloned.1.call-start
  7.2 0.7 convert_element_type.40
  7.9 0.1 copy.28
  8.0 0.1 broadcast_bitcast_fusion.1
  8.1 33.8 %all_gather.9 = bf16[128,1024]{1,0:T(8,128)(2,1)S(1)} all-gather(bf16[8,1024]{1,0:T(8,128)(2,1)} %param.6), channel_id=1, replica_groups=mesh['dp'=16,'row'=4,'col'=16] {'col'}, dimensions={0}, use_global_device_ids=true | all-gather | bytes 278528 | tf_op jit(solution)/shard_map/all_gather | solution.py:30
  41.9 3.8 copy.29
  45.7 1.6 bitcast_multiply_fusion.2
  47.4 0.0 copy-start.3
  47.4 0.6 convolution_bitcast_fusion.1
  48.0 1.0 copy.39
  49.0 0.0 reduce-scatter.10.cloned.1.call-update
  49.0 0.0 reduce-scatter.12.cloned.1.call-start
  49.1 0.0 copy-done.3
  49.1 0.1 copy.32
  49.2 0.1 broadcast_bitcast_fusion
  49.3 3.8 copy.33
  53.1 1.6 bitcast_multiply_fusion.1
  54.7 0.0 copy-start
  54.7 1.2 copy-done
  56.0 0.0 copy-start.2
  56.0 0.6 convolution_bitcast_fusion
  56.6 1.0 copy.41
  57.6 0.0 reduce-scatter.12.cloned.1.call-update
  57.6 0.0 reduce-scatter.14.cloned.1.call-start
  57.7 86.2 %reduce-scatter.10.cloned.1.call-done = f32[32,896]{1,0:T(8,128)} async-done(((f32[128,896]{1,0:T(8,128)}), f32[32,896]{1,0:T(8,128)}) %reduce-scatter.10.cloned.1.call-update) | async-done | bytes 114704 | tf_op jit(solution)/shard_map/reduce_scatter | solution.py:34
  143.9 84.4 %reduce-scatter.12.cloned.1.call-done = f32[32,896]{1,0:T(8,128)} async-done(((f32[128,896]{1,0:T(8,128)}), f32[32,896]{1,0:T(8,128)}) %reduce-scatter.12.cloned.1.call-update) | async-done | bytes 114704 | tf_op jit(solution)/shard_map/reduce_scatter | solution.py:35
  228.3 0.0 copy-done.2
  228.3 1.7 fusion.5
  230.0 24.1 %all_gather.10 = bf16[128,896]{1,0:T(8,128)(2,1)S(1)} all-gather(bf16[32,896]{1,0:T(8,128)(2,1)S(1)} %get-tuple-element.18), channel_id=1, replica_groups=mesh['dp'=16,'row'=4,'col'=16] {'row'}, dimensions={0}, use_global_device_ids=true | all-gather | bytes 286720 | tf_op jit(solution)/shard_map/all_gather | solution.py:39
  254.1 24.1 %all_gather.11 = bf16[128,896]{1,0:T(8,128)(2,1)S(1)} all-gather(bf16[32,896]{1,0:T(8,128)(2,1)S(1)} %get-tuple-element.20), channel_id=1, replica_groups=mesh['dp'=16,'row'=4,'col'=16] {'row'}, dimensions={0}, use_global_device_ids=true | all-gather | bytes 286720 | tf_op jit(solution)/shard_map/all_gather | solution.py:40
  278.2 0.2 broadcast_in_dim.13
  278.4 0.2 broadcast_in_dim.15
  278.6 4.2 bitcast_multiply_fusion
  282.8 8.4 %copy.43 = f32[1024,1792]{1,0:T(8,128)} copy(f32[1024,1792]{0,1:T(8,128)} %bitcast_multiply_fusion) | data formatting | bytes 14680064
  291.2 0.0 reduce-scatter.14.cloned.1.call-update
  291.2 1.3 dynamic-slice
  293.2 0.0 copy-start.1
  293.2 0.4 fusion.10
  293.6 1.0 copy-done.1
  294.7 0.4 convolution_add_fusion
  295.1 73.6 %all-reduce.2 = bf16[128,1024]{1,0:T(8,128)(2,1)S(1)} all-reduce(f32[128,1024]{1,0:T(8,128)S(1)} %convolution_add_fusion), channel_id=4, replica_groups=mesh['dp'=16,'row'=4,'col'=16] {'col'}, use_global_device_ids=true, to_apply=%region_2.0.clone | all-reduce | flops 131072 | bytes 786432
  368.7 0.6 dynamic-slice_convert_fusion
  369.3 136.2 %reduce-scatter.14.cloned.1.call-done = f32[64,1792]{1,0:T(8,128)} async-done(((f32[1024,1792]{1,0:T(8,128)}), f32[64,1792]{1,0:T(8,128)}) %reduce-scatter.14.cloned.1.call-update) | async-done | bytes 458768
  505.5 1.8 fusion.9
  (3 shorter events, 0.0 us)
Async XLA Ops:
  7.2 136.7 %reduce-scatter.10.cloned.1.call-start = ((), (), s32[]{:S(2)}) async-start(), calls=%async_computation.3 | async-start | bytes 573440 | tf_op jit(solution)/shard_map/reduce_scatter | solution.py:34
  47.4 1.7 copy-start.3
  49.0 179.3 %reduce-scatter.12.cloned.1.call-start = ((), (), s32[]{:S(2)}) async-start(), calls=%async_computation.4 | async-start | bytes 573440 | tf_op jit(solution)/shard_map/reduce_scatter | solution.py:35
  54.7 1.2 copy-start
  56.0 172.4 %copy-start.2 = (bf16[32,896]{1,0:T(8,128)(2,1)S(1)}, bf16[32,896]{1,0:T(8,128)(2,1)}, u32[]{:S(2)}) copy-start(bf16[32,896]{1,0:T(8,128)(2,1)} %param.11) | copy-start | bytes 172036
  57.6 447.9 %reduce-scatter.14.cloned.1.call-start = ((), (), s32[]{:S(2)}) async-start(), calls=%async_computation.5 | async-start | bytes 7798784
  293.2 1.5 copy-start.1
Sparse Core Ops, SparseCore 0:
  49.2 94.6 reduce-scatter.9
  147.5 80.7 reduce-scatter.11
  291.4 214.1 reduce-scatter.13
where the time goes:
time: 515 us; the launch traced here: 514 us
  waiting for transfers between devices  307 us (60%)
  blocking collectives  156 us (30%)
  local copies, waits for them, and re-layouts  24.8 us (5%)
  between operations  14.5 us (3%)
  matrix products  6.32 us (1%)
  other arithmetic  5.59 us (1%)
    unnamed x4, waiting for transfers between devices  136 us
    reduce_scatter x1, waiting for transfers between devices, body(): lax.psum_scatter(part_gate, 'row', scatter_dimension=0, tiled=True)  86.2 us
    reduce_scatter x1, waiting for transfers between devices, body(): lax.psum_scatter(part_up, 'row', scatter_dimension=0, tiled=True)  84.4 us
    unnamed x1, blocking collectives  73.6 us
    all_gather x1, blocking collectives, body(): whole_rows = lax.all_gather(tokens, 'col', axis=0, tiled=True)  33.8 us
    all_gather x1, blocking collectives, body(): lax.all_gather(gate_mine, 'row', axis=0, tiled=True)  24.1 us
    all_gather x1, blocking collectives, body(): lax.all_gather(up_mine, 'row', axis=0, tiled=True)  24.1 us
    unnamed x18, local copies, waits for them, and re-layouts  21.7 us
  transfers between devices with their start and end apart: 3, of which 3 were waited for; matrix products, arithmetic and copies ran while one was open for 2% of the time, Pallas kernels for 0%

commit v1 on v0

v1 whole, which is shorter than its diff:
```python
import jax
import jax.numpy as jnp
from jax import lax
from jax.sharding import Mesh, PartitionSpec as P

BF16 = jnp.bfloat16
F32 = jnp.float32

DP = ("pair", "side")
Z = ("pair", "side", "row")


def z_index(place, side, core):
    return ((place % 8) * 2 + side) * 4 + (place // 8) * 2 + core


RING = [
    (z_index(place, side, core), z_index((place + (1, -1)[core]) % 16, side, core))
    for place in range(16)
    for side in range(2)
    for core in range(2)
]
OTHER_CORE = [(row, row ^ 1) for row in range(4)]
OTHER_HALF = [(row, row ^ 2) for row in range(4)]
OTHER_SIDE = [(side, side ^ 1) for side in range(2)]


def ordered(first_is_mine, mine, theirs, axis=0):
    return jnp.concatenate(
        [jnp.where(first_is_mine, mine, theirs), jnp.where(first_is_mine, theirs, mine)], axis=axis
    )


def masked(weight, mask):
    blocks, across = mask.shape
    rows, units = weight.shape
    keep = jnp.repeat(mask.astype(BF16), units // across, axis=1)
    return (weight.reshape(blocks, rows // blocks, units) * keep[:, None, :]).reshape(rows, units)


def gather_col(x, count):
    return lax.all_to_all(jnp.broadcast_to(x[None], (count, *x.shape)), "col", 0, 0)


def body(tokens, gate_weight, up_weight, mask_gate, mask_up, grad_hidden):
    columns = lax.axis_size("col")
    pair, side = lax.axis_index("pair"), lax.axis_index("side")
    row, col = lax.axis_index("row"), lax.axis_index("col")
    half, core = row // 2, row % 2
    place = half * 8 + pair
    held, features = tokens.shape
    units = gate_weight.shape[1]
    block = features // 8

    masked_gate = masked(gate_weight, mask_gate)
    masked_up = masked(up_weight, mask_up)
    masked_side = jnp.where(side == 0, masked_gate, masked_up)

    replica = gather_col(tokens, columns).reshape(2, 2, columns // 4 * held, features)
    replica = jnp.where(half == 0, replica, replica[::-1])
    replica = jnp.where(core == 0, replica, replica[:, ::-1])
    rows = replica.shape[2]

    def project(x):
        x = x.reshape(2 * rows, features)
        return jnp.concatenate(
            [jnp.dot(x, masked_gate, preferred_element_type=F32), jnp.dot(x, masked_up, preferred_element_type=F32)],
            axis=1,
        )

    others = lax.ppermute(project(replica[:, 1]), "row", OTHER_CORE)
    summed = project(replica[:, 0]) + others
    arrived = lax.ppermute(summed[rows:].astype(BF16), "row", OTHER_HALF)
    proj = summed[:rows] + arrived.astype(F32)
    gate_proj, up_proj = proj[:, :units], proj[:, units:]

    sigmoid_gate = jax.nn.sigmoid(gate_proj)
    activation = gate_proj * sigmoid_gate
    hidden = (activation * up_proj).astype(BF16)
    cotangent = grad_hidden.astype(F32)
    grad_gate_act = (cotangent * up_proj * sigmoid_gate * (1.0 + gate_proj * (1.0 - sigmoid_gate))).astype(BF16)
    grad_up_act = (cotangent * activation).astype(BF16)

    mine = jnp.where(side == 0, grad_gate_act, grad_up_act)
    theirs = lax.ppermute(jnp.where(side == 0, grad_up_act, grad_gate_act), "side", OTHER_SIDE)
    both = ordered(side == 0, mine, theirs)
    own = ordered(core == 0, both, lax.ppermute(both, "row", OTHER_CORE))

    spread = jnp.repeat(tokens.reshape(held, 8, block).transpose(1, 0, 2), 2, axis=0)
    spread = lax.all_to_all(spread, DP, 0, 0)
    everyone = gather_col(spread, columns).reshape(2, 2, columns // 4, 8, 2, held, block)
    everyone = everyone.transpose(0, 3, 1, 4, 2, 5, 6).reshape(16, 4 * rows, block)
    twice = jnp.concatenate([everyone, everyone], axis=0)
    before = lax.dynamic_slice_in_dim(twice, place + 8, 8, axis=0)[::-1]
    after = lax.dynamic_slice_in_dim(twice, place, 8, axis=0)
    after = jnp.concatenate([after[1:], after[:1]], axis=0)
    mine_rows = jnp.where(core == 0, before, after)
    their_rows = lax.ppermute(jnp.where(core == 0, after, before), "row", OTHER_CORE)
    features_of = ordered(core == 0, mine_rows, their_rows, axis=2)

    contract_rows = (((0,), (0,)), ((), ()))
    total = None
    moving = own
    fourth = None
    for step in range(8):
        moving = lax.ppermute(moving, Z, RING)
        if step == 3:
            fourth = moving
        met = moving if step < 7 else jnp.where(core == 0, moving, own)
        term = lax.dot_general(features_of[step], met, contract_rows, preferred_element_type=F32)
        total = term if total is None else total + term

    across = lax.ppermute(fourth, "row", OTHER_CORE)
    far = jnp.where((pair < 4) == (core == 0), fourth, across)
    part = lax.dot_general(
        jnp.concatenate([own, far], axis=0),
        masked_side,
        (((1,), (1,)), ((), ())),
        preferred_element_type=F32,
    ).astype(BF16)
    part = part.reshape(2, 2, 2, columns // 4, held, features)
    part = jnp.where(half == 0, part, part[::-1]).transpose(2, 0, 1, 3, 4, 5)
    part = part.reshape(2 * columns, held, features)
    reduced = lax.all_to_all(part, ("side", "col"), 0, 0)
    reduced = jnp.sum(reduced.astype(F32), axis=0).astype(BF16)
    swapped = lax.ppermute(reduced, "pair", [(i, i ^ 4) for i in range(8)])
    grad_tokens = jnp.where((col < columns // 2) == (half == 0), reduced, swapped)

    keep = jnp.where(core == 0, total[block:], total[:block])
    got = lax.ppermute(keep, "row", OTHER_CORE)
    full = jnp.where(core == 0, total[:block], total[block:]) + got
    low, high = full[: block // 2], full[block // 2 :]
    kept = jnp.where(side == 0, low, high)
    traded = lax.ppermute(jnp.where(side == 0, high, low), "side", OTHER_SIDE)
    grad_gate = jnp.where(side == 0, kept, traded)
    grad_up = jnp.where(side == 0, traded, kept)

    def kept_blocks(mask):
        line = lax.dynamic_slice_in_dim(mask, pair, 1, axis=0).astype(F32)
        return jnp.repeat(line, units // mask.shape[1], axis=1)

    return (hidden, grad_tokens, grad_gate * kept_blocks(mask_gate), grad_up * kept_blocks(mask_up))


def solution(mesh):
    replicas, rows, columns = (mesh.shape[name] for name in ("dp", "row", "col"))
    assert replicas == 16 and rows == 4
    split = Mesh(mesh.devices.reshape(8, 2, rows, columns), ("pair", "side", "row", "col"))
    placed = (
        P(("pair", "side", "col"), "row"),
        P("row", "col"),
        P("row", "col"),
        P("row", "col"),
        P("row", "col"),
        P(("pair", "side", "row"), "col"),
    )
    return jax.shard_map(
        body,
        mesh=split,
        in_specs=placed,
        out_specs=(
            P(("pair", "side", "row"), "col"),
            P(("pair", "side", "col"), "row"),
            P(("row", "pair", "side"), "col"),
            P(("row", "pair", "side"), "col"),
        ),
        check_vma=False,
    )
```

time: 515 us -> 248 us (0.48)
  waiting for transfers between devices: 307 us -> 95.7 us
  blocking collectives: 156 us -> 0 us
  starting transfers between devices: 0.12 us -> 129 us
  local copies, waits for them, and re-layouts: 24.8 us -> 4.92 us
  between operations: 14.5 us -> 1.2 us
    reduce_scatter x2 -> x0, waiting for transfers between devices: 171 us -> none  [the longest x1 86.2 us: body(): lax.psum_scatter(part_gate, 'row', scatter_dimension=0, tiled=True)]
    unnamed x4 -> x0, waiting for transfers between devices: 136 us -> none
    all_gather x3 -> x0, blocking collectives: 82 us -> none  [the longest x1 33.8 us: body(): whole_rows = lax.all_gather(tokens, 'col', axis=0, tiled=True)]
    ppermute x0 -> x17, waiting for transfers between devices: none -> 79.3 us  [the longest x8 56.5 us: body(): moving = lax.ppermute(moving, Z, RING)]
    ppermute x0 -> x17, starting transfers between devices: none -> 73.7 us  [the longest x1 19.9 us: body(): arrived = lax.ppermute(summed[rows:].astype(BF16), 'row', OTHER_HALF)]
    unnamed x1 -> x0, blocking collectives: 73.6 us -> none
    all_to_all x0 -> x4, starting transfers between devices: none -> 55.5 us  [the longest x1 23.2 us: body(): spread = lax.all_to_all(spread, DP, 0, 0)]
    unnamed x18 -> x16, local copies, waits for them, and re-layouts: 21.7 us -> 1.26 us
  transfers between devices with their start and end apart: 3 -> 21, of which waited for: 3 -> 15; matrix products, arithmetic and copies ran while one was open for 2% -> 6% of each run, Pallas kernels for 0% -> 0%
where the time goes in v1:
time: 248 us; the launch traced here: 247 us
  starting transfers between devices  129 us (52%)
  waiting for transfers between devices  95.7 us (39%)
  other arithmetic  10.6 us (4%)
  matrix products  5.01 us (2%)
  local copies, waits for them, and re-layouts  4.92 us (2%)
    ppermute x8, waiting for transfers between devices, body(): moving = lax.ppermute(moving, Z, RING)  56.5 us
    all_to_all x1, starting transfers between devices, body(): spread = lax.all_to_all(spread, DP, 0, 0)  23.2 us
    all_to_all x2, starting transfers between devices, gather_col(): lax.all_to_all(jnp.broadcast_to(x[None], (count, *x.shape)), 'col', 0, 0)  22.7 us
    ppermute x1, starting transfers between devices, body(): arrived = lax.ppermute(summed[rows:].astype(BF16), 'row', OTHER_HALF)  19.9 us
    ppermute x8, starting transfers between devices, body(): moving = lax.ppermute(moving, Z, RING)  18.9 us
    ppermute x1, starting transfers between devices, body(): lax.ppermute(jnp.where(side == 0, grad_up_act, grad_gate_act), 'side', OT...  17.9 us
    all_to_all x1, waiting for transfers between devices, body(): spread = lax.all_to_all(spread, DP, 0, 0)  15.3 us
    all_to_all x1, starting transfers between devices, body(): reduced = lax.all_to_all(part, ('side', 'col'), 0, 0)  9.53 us
  transfers between devices with their start and end apart: 21, of which 15 were waited for; matrix products, arithmetic and copies ran while one was open for 6% of the time, Pallas kernels for 0%

profile of v1, /device:TPU:6, one launch (start us, length us, event | category | flops | bytes accessed | tf_op | source)
XLA Modules:
  0.0 246.6 jit_solution(11685221821003079295)
XLA Ops:
  0.6 1.5 broadcast_in_dim.31
  2.1 16.5 %all-to-all-start = ((bf16[16,8,1024]{2,1,0:T(8,128)(2,1)}), bf16[16,8,1024]{2,1,0:T(8,128)(2,1)S(1)}, u32[]{:S(2)}, u32[]{:S(2)}) async-start(bf16[16,8,1024]{2,1,0:T(8,128)(2,1)} %broadcast_in_dim.31), calls=%async_computation | async-start | bytes 524288 | tf_op jit(solution)/shard_map/all_to_all | solution.py:42
  18.6 0.7 convert_element_type.38
  19.5 0.7 convert_element_type.37
  20.3 3.7 %bitcast_multiply_fusion = (bf16[1024,896]{1,0:T(8,128)(2,1)S(1)}, bf16[1024,896]{1,0:T(8,128)(2,1)}) fusion(bf16[1024,896]{1,0:T(8,128)(2,1)} %param.8, bf16[8,896]{1,0:T(8,128)(2,1)S(1)} %broadcast_bitcast_fusion, bf16[1024,896]{1,0:T(8,128)(2,1)} %param.7, bf16[8,896]{1,0:T(8,128)(2,1)S(1)} %broadcast_bitcast_fusion.1), kind=kLoop, calls=%fused_computation | loop fusion | flops 1835008 | bytes 7368704 | tf_op jit(solution)/shard_map/mul | solution.py:38
  24.0 1.0 all-to-all-done
  25.1 0.4 fusion.64
  25.6 0.9 copy-done
  26.5 0.4 fusion.63
  27.0 1.9 collective-permute-start
  28.9 0.4 fusion.62
  29.3 0.4 fusion.61
  29.8 0.9 collective-permute-done
  30.8 19.9 %collective-permute-start.1 = (bf16[32,1792]{1,0:T(8,128)(2,1)S(1)}, bf16[32,1792]{1,0:T(8,128)(2,1)S(1)}, u32[]{:S(2)}, u32[]{:S(2)}) collective-permute-start(bf16[32,1792]{1,0:T(8,128)(2,1)S(1)} %slice.219), channel_id=1, source_target_pairs={{0,32},{16,48},{32,0},{48,16},{1,33},{17,49},{33,1},{49,17},{2,34}... | collective-permute-start | bytes 344072 | tf_op jit(solution)/shard_map/ppermute | solution.py:73
  50.7 5.9 %collective-permute-done.1 = bf16[32,1792]{1,0:T(8,128)(2,1)S(1)} collective-permute-done((bf16[32,1792]{1,0:T(8,128)(2,1)S(1)}, bf16[32,1792]{1,0:T(8,128)(2,1)S(1)}, u32[]{:S(2)}, u32[]{:S(2)}) %collective-permute-start.1) | collective-permute-done | bytes 114720 | tf_op jit(solution)/shard_map/ppermute | solution.py:73
  56.7 17.9 %collective-permute-start.2 = (bf16[32,896]{1,0:T(8,128)(2,1)S(1)}, bf16[32,896]{1,0:T(8,128)(2,1)S(1)}, u32[]{:S(2)}, u32[]{:S(2)}) collective-permute-start(bf16[32,896]{1,0:T(8,128)(2,1)S(1)} %get-tuple-element.4), channel_id=1, source_target_pairs={{0,64},{64,0},{1,65},{65,1},{2,66},{66,2},{3,67},{67,3},{4,68},{68... | collective-permute-start | bytes 172040 | tf_op jit(solution)/shard_map/ppermute | solution.py:85
  74.6 2.1 collective-permute-done.2
  76.8 1.9 collective-permute-start.3
  78.7 1.3 collective-permute-done.3
  80.0 1.9 collective-permute-start.4
  82.0 0.6 broadcast_in_dim.34
  82.6 23.2 %all-to-all-start.2 = ((bf16[16,8,128]{2,1,0:T(8,128)(2,1)}), bf16[16,8,128]{2,1,0:T(8,128)(2,1)S(1)}, u32[]{:S(2)}, u32[]{:S(2)}) async-start(bf16[16,8,128]{2,1,0:T(8,128)(2,1)} %bitcast.12), calls=%async_computation.2 | async-start | bytes 65536 | tf_op jit(solution)/shard_map/all_to_all | solution.py:90
  105.9 4.7 %collective-permute-start.5 = (bf16[128,896]{1,0:T(8,128)(2,1)S(1)}, bf16[128,896]{1,0:T(8,128)(2,1)S(1)}, u32[]{:S(2)}, u32[]{:S(2)}) collective-permute-start(bf16[128,896]{1,0:T(8,128)(2,1)S(1)} %collective-permute-done.4), channel_id=1, source_target_pairs={{0,128},{16,944},{64,192},{80,1008},{128,256},{144,16},{192,320},{... | collective-permute-start | bytes 688136 | tf_op jit(solution)/shard_map/ppermute | solution.py:106
  110.6 15.3 %all-to-all-done.2 = bf16[16,8,128]{2,1,0:T(8,128)(2,1)S(1)} async-done(((bf16[16,8,128]{2,1,0:T(8,128)(2,1)}), bf16[16,8,128]{2,1,0:T(8,128)(2,1)S(1)}, u32[]{:S(2)}, u32[]{:S(2)}) %all-to-all-start.2) | async-done | bytes 32800 | tf_op jit(solution)/shard_map/all_to_all | solution.py:90
  125.9 0.9 broadcast_in_dim.35
  126.8 6.2 %all-to-all-start.3 = ((bf16[16,16,8,128]{3,2,1,0:T(8,128)(2,1)}), bf16[16,16,8,128]{3,2,1,0:T(8,128)(2,1)S(1)}, u32[]{:S(2)}, u32[]{:S(2)}) async-start(bf16[16,16,8,128]{3,2,1,0:T(8,128)(2,1)} %broadcast_in_dim.35), calls=%async_computation.3 | async-start | bytes 1048576 | tf_op jit(solution)/shard_map/all_to_all | solution.py:42
  133.0 2.5 %collective-permute-start.6 = (bf16[128,896]{1,0:T(8,128)(2,1)S(1)}, bf16[128,896]{1,0:T(8,128)(2,1)S(1)}, u32[]{:S(2)}, u32[]{:S(2)}) collective-permute-start(bf16[128,896]{1,0:T(8,128)(2,1)S(1)} %collective-permute-done.5), channel_id=1, source_target_pairs={{0,128},{16,944},{64,192},{80,1008},{128,256},{144,16},{192,320},{... | collective-permute-start | bytes 688136 | tf_op jit(solution)/shard_map/ppermute | solution.py:106
  135.6 7.6 %collective-permute-done.6 = bf16[128,896]{1,0:T(8,128)(2,1)S(1)} collective-permute-done((bf16[128,896]{1,0:T(8,128)(2,1)S(1)}, bf16[128,896]{1,0:T(8,128)(2,1)S(1)}, u32[]{:S(2)}, u32[]{:S(2)}) %collective-permute-start.6) | collective-permute-done | bytes 229408 | tf_op jit(solution)/shard_map/ppermute | solution.py:106
  143.2 2.1 collective-permute-start.7
  145.5 10.2 %collective-permute-done.7 = bf16[128,896]{1,0:T(8,128)(2,1)S(1)} collective-permute-done((bf16[128,896]{1,0:T(8,128)(2,1)S(1)}, bf16[128,896]{1,0:T(8,128)(2,1)S(1)}, u32[]{:S(2)}, u32[]{:S(2)}) %collective-permute-start.7) | collective-permute-done | bytes 229408 | tf_op jit(solution)/shard_map/ppermute | solution.py:106
  155.7 1.9 collective-permute-start.8
  157.6 0.2 fusion.11
  157.9 0.8 broadcast_select_fusion.2
  158.7 2.4 collective-permute-start.10
  161.1 0.8 fusion.3
  162.0 0.9 reverse_select_fusion
  162.9 9.5 %all-to-all-start.1 = ((bf16[32,8,1024]{2,1,0:T(8,128)(2,1)}), bf16[32,8,1024]{2,1,0:T(8,128)(2,1)S(1)}, u32[]{:S(2)}, u32[]{:S(2)}) async-start(bf16[32,8,1024]{2,1,0:T(8,128)(2,1)} %bitcast.9), calls=%async_computation.1 | async-start | bytes 1048576 | tf_op jit(solution)/shard_map/all_to_all | solution.py:124
  172.7 0.3 fusion.36
  173.0 0.3 convolution_add_fusion.6
  173.3 0.3 copy-done.3
  173.6 0.3 convolution_add_fusion.5
  173.9 1.9 collective-permute-start.11
  175.8 0.3 convolution_add_fusion.4
  176.2 9.7 %collective-permute-done.11 = bf16[128,896]{1,0:T(8,128)(2,1)S(1)} collective-permute-done((bf16[128,896]{1,0:T(8,128)(2,1)S(1)}, bf16[128,896]{1,0:T(8,128)(2,1)S(1)}, u32[]{:S(2)}, u32[]{:S(2)}) %collective-permute-start.11) | collective-permute-done | bytes 229408 | tf_op jit(solution)/shard_map/ppermute | solution.py:106
  185.8 1.9 collective-permute-start.12
  187.7 0.3 convolution_add_fusion.3
  188.1 10.2 %collective-permute-done.12 = bf16[128,896]{1,0:T(8,128)(2,1)S(1)} collective-permute-done((bf16[128,896]{1,0:T(8,128)(2,1)S(1)}, bf16[128,896]{1,0:T(8,128)(2,1)S(1)}, u32[]{:S(2)}, u32[]{:S(2)}) %collective-permute-start.12) | collective-permute-done | bytes 229408 | tf_op jit(solution)/shard_map/ppermute | solution.py:106
  198.3 1.9 collective-permute-start.13
  200.2 0.3 convolution_add_fusion.2
  200.5 10.0 %collective-permute-done.13 = bf16[128,896]{1,0:T(8,128)(2,1)S(1)} collective-permute-done((bf16[128,896]{1,0:T(8,128)(2,1)S(1)}, bf16[128,896]{1,0:T(8,128)(2,1)S(1)}, u32[]{:S(2)}, u32[]{:S(2)}) %collective-permute-start.13) | collective-permute-done | bytes 229408 | tf_op jit(solution)/shard_map/ppermute | solution.py:106
  210.6 1.9 collective-permute-start.14
  212.5 0.3 convolution_add_fusion.1
  212.8 8.8 %collective-permute-done.14 = bf16[128,896]{1,0:T(8,128)(2,1)S(1)} collective-permute-done((bf16[128,896]{1,0:T(8,128)(2,1)S(1)}, bf16[128,896]{1,0:T(8,128)(2,1)S(1)}, u32[]{:S(2)}, u32[]{:S(2)}) %collective-permute-start.14) | collective-permute-done | bytes 229408 | tf_op jit(solution)/shard_map/ppermute | solution.py:106
  221.6 0.3 convolution_add_fusion
  221.9 1.9 collective-permute-start.15
  223.9 0.7 fusion.46
  224.7 1.0 collective-permute-done.15
  225.8 5.0 %collective-permute-start.16 = (f32[64,896]{1,0:T(8,128)S(1)}, f32[64,896]{1,0:T(8,128)S(1)}, u32[]{:S(2)}, u32[]{:S(2)}) collective-permute-start(f32[64,896]{1,0:T(8,128)S(1)} %slice_select_fusion.1), channel_id=1, source_target_pairs={{0,64},{64,0},{1,65},{65,1},{2,66},{66,2},{3,67},{67,3},{4,68},{68... | collective-permute-start | bytes 688136 | tf_op jit(solution)/shard_map/ppermute | solution.py:134
  230.9 0.7 multiply_convert_fusion
  231.6 1.9 collective-permute-start.9
  233.6 3.1 %collective-permute-done.16 = f32[64,896]{1,0:T(8,128)S(1)} collective-permute-done((f32[64,896]{1,0:T(8,128)S(1)}, f32[64,896]{1,0:T(8,128)S(1)}, u32[]{:S(2)}, u32[]{:S(2)}) %collective-permute-start.16) | collective-permute-done | bytes 229408 | tf_op jit(solution)/shard_map/ppermute | solution.py:134
  236.7 0.8 select_multiply_fusion
  237.5 8.5 %collective-permute-done.9 = bf16[8,1024]{1,0:T(8,128)(2,1)S(1)} collective-permute-done((bf16[8,1024]{1,0:T(8,128)(2,1)S(1)}, bf16[8,1024]{1,0:T(8,128)(2,1)S(1)}, u32[]{:S(2)}, u32[]{:S(2)}) %collective-permute-start.9) | collective-permute-done | bytes 16416 | tf_op jit(solution)/shard_map/ppermute | solution.py:126
  246.0 0.6 broadcast_select_fusion.11
  (48 shorter events, 1.6 us)
Async XLA Ops:
  2.1 22.9 %all-to-all-start = ((bf16[16,8,1024]{2,1,0:T(8,128)(2,1)}), bf16[16,8,1024]{2,1,0:T(8,128)(2,1)S(1)}, u32[]{:S(2)}, u32[]{:S(2)}) async-start(bf16[16,8,1024]{2,1,0:T(8,128)(2,1)} %broadcast_in_dim.31), calls=%async_computation | async-start | bytes 524288 | tf_op jit(solution)/shard_map/all_to_all | solution.py:42
  25.0 1.5 copy-start
  27.0 3.7 %collective-permute-start = (f32[64,1792]{1,0:T(8,128)S(1)}, f32[64,1792]{1,0:T(8,128)S(1)}, u32[]{:S(2)}, u32[]{:S(2)}) collective-permute-start(f32[64,1792]{1,0:T(8,128)S(1)} %pad_maximum_fusion), channel_id=1, source_target_pairs={{0,16},{16,0},{32,48},{48,32},{1,17},{17,1},{33,49},{49,33},{2,18}... | collective-permute-start | bytes 1376264 | tf_op jit(solution)/shard_map/ppermute | solution.py:71
  29.3 27.2 %copy-start.7 = (bf16[32,896]{1,0:T(8,128)(2,1)S(1)}, bf16[32,896]{1,0:T(8,128)(2,1)}, u32[]{:S(2)}) copy-start(bf16[32,896]{1,0:T(8,128)(2,1)} %param.11) | copy-start | bytes 172036
  29.8 52.2 %copy-start.6 = (bf16[8,1024]{1,0:T(8,128)(2,1)S(1)}, bf16[8,1024]{1,0:T(8,128)(2,1)}, u32[]{:S(2)}) copy-start(bf16[8,1024]{1,0:T(8,128)(2,1)} %param.6) | copy-start | bytes 49156
  30.8 25.8 %collective-permute-start.1 = (bf16[32,1792]{1,0:T(8,128)(2,1)S(1)}, bf16[32,1792]{1,0:T(8,128)(2,1)S(1)}, u32[]{:S(2)}, u32[]{:S(2)}) collective-permute-start(bf16[32,1792]{1,0:T(8,128)(2,1)S(1)} %slice.219), channel_id=1, source_target_pairs={{0,32},{16,48},{32,0},{48,16},{1,33},{17,49},{33,1},{49,17},{2,34}... | collective-permute-start | bytes 344072 | tf_op jit(solution)/shard_map/ppermute | solution.py:73
  56.7 20.0 %collective-permute-start.2 = (bf16[32,896]{1,0:T(8,128)(2,1)S(1)}, bf16[32,896]{1,0:T(8,128)(2,1)S(1)}, u32[]{:S(2)}, u32[]{:S(2)}) collective-permute-start(bf16[32,896]{1,0:T(8,128)(2,1)S(1)} %get-tuple-element.4), channel_id=1, source_target_pairs={{0,64},{64,0},{1,65},{65,1},{2,66},{66,2},{3,67},{67,3},{4,68},{68... | collective-permute-start | bytes 172040 | tf_op jit(solution)/shard_map/ppermute | solution.py:85
  76.8 3.2 %collective-permute-start.3 = (bf16[64,896]{1,0:T(8,128)(2,1)S(1)}, bf16[64,896]{1,0:T(8,128)(2,1)S(1)}, u32[]{:S(2)}, u32[]{:S(2)}) collective-permute-start(bf16[64,896]{1,0:T(8,128)(2,1)S(1)} %pad_maximum_fusion.3), channel_id=1, source_target_pairs={{0,16},{16,0},{32,48},{48,32},{1,17},{17,1},{33,49},{49,33},{2,18}... | collective-permute-start | bytes 344072 | tf_op jit(solution)/shard_map/ppermute | solution.py:87
  80.0 25.8 %collective-permute-start.4 = (bf16[128,896]{1,0:T(8,128)(2,1)S(1)}, bf16[128,896]{1,0:T(8,128)(2,1)S(1)}, u32[]{:S(2)}, u32[]{:S(2)}) collective-permute-start(bf16[128,896]{1,0:T(8,128)(2,1)S(1)} %pad_maximum_fusion.2), channel_id=1, source_target_pairs={{0,128},{16,944},{64,192},{80,1008},{128,256},{144,16},{192,320},{... | collective-permute-start | bytes 688136 | tf_op jit(solution)/shard_map/ppermute | solution.py:106
  82.6 43.3 %all-to-all-start.2 = ((bf16[16,8,128]{2,1,0:T(8,128)(2,1)}), bf16[16,8,128]{2,1,0:T(8,128)(2,1)S(1)}, u32[]{:S(2)}, u32[]{:S(2)}) async-start(bf16[16,8,128]{2,1,0:T(8,128)(2,1)} %bitcast.12), calls=%async_computation.2 | async-start | bytes 65536 | tf_op jit(solution)/shard_map/all_to_all | solution.py:90
  105.8 29.7 %copy-start.4 = (bf16[128,896]{1,0:T(8,128)(2,1)}, bf16[128,896]{1,0:T(8,128)(2,1)S(1)}, u32[]{:S(2)}) copy-start(bf16[128,896]{1,0:T(8,128)(2,1)S(1)} %collective-permute-done.4) | copy-start | bytes 688132
  105.9 27.2 %collective-permute-start.5 = (bf16[128,896]{1,0:T(8,128)(2,1)S(1)}, bf16[128,896]{1,0:T(8,128)(2,1)S(1)}, u32[]{:S(2)}, u32[]{:S(2)}) collective-permute-start(bf16[128,896]{1,0:T(8,128)(2,1)S(1)} %collective-permute-done.4), channel_id=1, source_target_pairs={{0,128},{16,944},{64,192},{80,1008},{128,256},{144,16},{192,320},{... | collective-permute-start | bytes 688136 | tf_op jit(solution)/shard_map/ppermute | solution.py:106
  126.8 18.5 %all-to-all-start.3 = ((bf16[16,16,8,128]{3,2,1,0:T(8,128)(2,1)}), bf16[16,16,8,128]{3,2,1,0:T(8,128)(2,1)S(1)}, u32[]{:S(2)}, u32[]{:S(2)}) async-start(bf16[16,16,8,128]{3,2,1,0:T(8,128)(2,1)} %broadcast_in_dim.35), calls=%async_computation.3 | async-start | bytes 1048576 | tf_op jit(solution)/shard_map/all_to_all | solution.py:42
  133.0 10.1 %collective-permute-start.6 = (bf16[128,896]{1,0:T(8,128)(2,1)S(1)}, bf16[128,896]{1,0:T(8,128)(2,1)S(1)}, u32[]{:S(2)}, u32[]{:S(2)}) collective-permute-start(bf16[128,896]{1,0:T(8,128)(2,1)S(1)} %collective-permute-done.5), channel_id=1, source_target_pairs={{0,128},{16,944},{64,192},{80,1008},{128,256},{144,16},{192,320},{... | collective-permute-start | bytes 688136 | tf_op jit(solution)/shard_map/ppermute | solution.py:106
  143.2 14.7 %copy-start.2 = (bf16[128,896]{1,0:T(8,128)(2,1)}, bf16[128,896]{1,0:T(8,128)(2,1)S(1)}, u32[]{:S(2)}) copy-start(bf16[128,896]{1,0:T(8,128)(2,1)S(1)} %collective-permute-done.6) | copy-start | bytes 688132
  143.2 12.5 %collective-permute-start.7 = (bf16[128,896]{1,0:T(8,128)(2,1)S(1)}, bf16[128,896]{1,0:T(8,128)(2,1)S(1)}, u32[]{:S(2)}, u32[]{:S(2)}) collective-permute-start(bf16[128,896]{1,0:T(8,128)(2,1)S(1)} %collective-permute-done.6), channel_id=1, source_target_pairs={{0,128},{16,944},{64,192},{80,1008},{128,256},{144,16},{192,320},{... | collective-permute-start | bytes 688136 | tf_op jit(solution)/shard_map/ppermute | solution.py:106
  145.3 15.8 %copy-start.1 = (bf16[1024,896]{1,0:T(8,128)(2,1)S(1)}, bf16[1024,896]{1,0:T(8,128)(2,1)}, u32[]{:S(2)}) copy-start(bf16[1024,896]{1,0:T(8,128)(2,1)} %get-tuple-element.20) | copy-start | bytes 5505028
  155.7 5.4 %collective-permute-start.8 = (bf16[128,896]{1,0:T(8,128)(2,1)S(1)}, bf16[128,896]{1,0:T(8,128)(2,1)S(1)}, u32[]{:S(2)}, u32[]{:S(2)}) collective-permute-start(bf16[128,896]{1,0:T(8,128)(2,1)S(1)} %collective-permute-done.7), channel_id=1, source_target_pairs={{0,16},{16,0},{32,48},{48,32},{1,17},{17,1},{33,49},{49,33},{2,18}... | collective-permute-start | bytes 688136 | tf_op jit(solution)/shard_map/ppermute | solution.py:113
  158.7 13.8 %collective-permute-start.10 = (bf16[8,128,128]{2,1,0:T(8,128)(2,1)}, bf16[8,128,128]{2,1,0:T(8,128)(2,1)S(1)}, u32[]{:S(2)}, u32[]{:S(2)}) collective-permute-start(bf16[8,128,128]{2,1,0:T(8,128)(2,1)} %broadcast_select_fusion.2), channel_id=1, source_target_pairs={{0,16},{16,0},{32,48},{48,32},{1,17},{17,1},{33,49},{49,33},{2,18}... | collective-permute-start | bytes 786440 | tf_op jit(solution)/shard_map/ppermute | solution.py:98
  162.0 10.7 %copy-start.5 = (bf16[128,896]{1,0:T(8,128)(2,1)S(1)}, bf16[128,896]{1,0:T(8,128)(2,1)}, u32[]{:S(2)}) copy-start(bf16[128,896]{1,0:T(8,128)(2,1)} %copy-done.4) | copy-start | bytes 688132
  162.9 68.7 %all-to-all-start.1 = ((bf16[32,8,1024]{2,1,0:T(8,128)(2,1)}), bf16[32,8,1024]{2,1,0:T(8,128)(2,1)S(1)}, u32[]{:S(2)}, u32[]{:S(2)}) async-start(bf16[32,8,1024]{2,1,0:T(8,128)(2,1)} %bitcast.9), calls=%async_computation.1 | async-start | bytes 1048576 | tf_op jit(solution)/shard_map/all_to_all | solution.py:124
  172.6 0.9 copy-start.3
  173.9 11.9 %collective-permute-start.11 = (bf16[128,896]{1,0:T(8,128)(2,1)S(1)}, bf16[128,896]{1,0:T(8,128)(2,1)S(1)}, u32[]{:S(2)}, u32[]{:S(2)}) collective-permute-start(bf16[128,896]{1,0:T(8,128)(2,1)S(1)} %collective-permute-done.7), channel_id=1, source_target_pairs={{0,128},{16,944},{64,192},{80,1008},{128,256},{144,16},{192,320},{... | collective-permute-start | bytes 688136 | tf_op jit(solution)/shard_map/ppermute | solution.py:106
  185.8 12.5 %collective-permute-start.12 = (bf16[128,896]{1,0:T(8,128)(2,1)S(1)}, bf16[128,896]{1,0:T(8,128)(2,1)S(1)}, u32[]{:S(2)}, u32[]{:S(2)}) collective-permute-start(bf16[128,896]{1,0:T(8,128)(2,1)S(1)} %collective-permute-done.11), channel_id=1, source_target_pairs={{0,128},{16,944},{64,192},{80,1008},{128,256},{144,16},{192,320},{... | collective-permute-start | bytes 688136 | tf_op jit(solution)/shard_map/ppermute | solution.py:106
  198.3 12.3 %collective-permute-start.13 = (bf16[128,896]{1,0:T(8,128)(2,1)S(1)}, bf16[128,896]{1,0:T(8,128)(2,1)S(1)}, u32[]{:S(2)}, u32[]{:S(2)}) collective-permute-start(bf16[128,896]{1,0:T(8,128)(2,1)S(1)} %collective-permute-done.12), channel_id=1, source_target_pairs={{0,128},{16,944},{64,192},{80,1008},{128,256},{144,16},{192,320},{... | collective-permute-start | bytes 688136 | tf_op jit(solution)/shard_map/ppermute | solution.py:106
  210.6 11.0 %collective-permute-start.14 = (bf16[128,896]{1,0:T(8,128)(2,1)S(1)}, bf16[128,896]{1,0:T(8,128)(2,1)S(1)}, u32[]{:S(2)}, u32[]{:S(2)}) collective-permute-start(bf16[128,896]{1,0:T(8,128)(2,1)S(1)} %collective-permute-done.13), channel_id=1, source_target_pairs={{0,128},{16,944},{64,192},{80,1008},{128,256},{144,16},{192,320},{... | collective-permute-start | bytes 688136 | tf_op jit(solution)/shard_map/ppermute | solution.py:106
  221.9 3.7 %collective-permute-start.15 = (f32[128,896]{1,0:T(8,128)S(1)}, f32[128,896]{1,0:T(8,128)S(1)}, u32[]{:S(2)}, u32[]{:S(2)}) collective-permute-start(f32[128,896]{1,0:T(8,128)S(1)} %slice_select_fusion), channel_id=1, source_target_pairs={{0,16},{16,0},{32,48},{48,32},{1,17},{17,1},{33,49},{49,33},{2,18}... | collective-permute-start | bytes 1376264 | tf_op jit(solution)/shard_map/ppermute | solution.py:130
  225.8 10.9 %collective-permute-start.16 = (f32[64,896]{1,0:T(8,128)S(1)}, f32[64,896]{1,0:T(8,128)S(1)}, u32[]{:S(2)}, u32[]{:S(2)}) collective-permute-start(f32[64,896]{1,0:T(8,128)S(1)} %slice_select_fusion.1), channel_id=1, source_target_pairs={{0,64},{64,0},{1,65},{65,1},{2,66},{66,2},{3,67},{67,3},{4,68},{68... | collective-permute-start | bytes 688136 | tf_op jit(solution)/shard_map/ppermute | solution.py:134
  231.6 14.3 %collective-permute-start.9 = (bf16[8,1024]{1,0:T(8,128)(2,1)S(1)}, bf16[8,1024]{1,0:T(8,128)(2,1)S(1)}, u32[]{:S(2)}, u32[]{:S(2)}) collective-permute-start(bf16[8,1024]{1,0:T(8,128)(2,1)S(1)} %reduce_sum.12), channel_id=1, source_target_pairs={{0,512},{128,640},{256,768},{384,896},{512,0},{640,128},{768,256},... | collective-permute-start | bytes 49160 | tf_op jit(solution)/shard_map/ppermute | solution.py:126

commit v2 on v1

v2 whole, which is shorter than its diff:
```python
import jax
import jax.numpy as jnp
from jax import lax
from jax.sharding import Mesh, PartitionSpec as P

BF16 = jnp.bfloat16
F32 = jnp.float32

TEAM = 4
GROUPS = 16 // TEAM
PLACES = 2 * GROUPS
STEPS = PLACES // 2
DP = ("group", "member")
Z = ("group", "member", "row")


def z_index(place, member, core):
    return ((place % GROUPS) * TEAM + member) * 4 + (place // GROUPS) * 2 + core


RING = [
    (z_index(place, member, core), z_index((place + (1, -1)[core]) % PLACES, member, core))
    for place in range(PLACES)
    for member in range(TEAM)
    for core in range(2)
]
OTHER_CORE = [(row, row ^ 1) for row in range(4)]
OTHER_HALF = [(row, row ^ 2) for row in range(4)]
FAR_GROUP = [(group, group ^ (PLACES // 4)) for group in range(GROUPS)]


def ordered(first_is_mine, mine, theirs, axis=0):
    return jnp.concatenate(
        [jnp.where(first_is_mine, mine, theirs), jnp.where(first_is_mine, theirs, mine)], axis=axis
    )


def masked(weight, mask):
    blocks, across = mask.shape
    rows, units = weight.shape
    keep = jnp.repeat(mask.astype(BF16), units // across, axis=1)
    return (weight.reshape(blocks, rows // blocks, units) * keep[:, None, :]).reshape(rows, units)


def gather_col(x, count):
    return lax.all_to_all(jnp.broadcast_to(x[None], (count, *x.shape)), "col", 0, 0)


def body(tokens, gate_weight, up_weight, mask_gate, mask_up, grad_hidden):
    columns = lax.axis_size("col")
    group, member = lax.axis_index("group"), lax.axis_index("member")
    row, col = lax.axis_index("row"), lax.axis_index("col")
    half, core = row // 2, row % 2
    place = half * GROUPS + group
    held, features = tokens.shape
    units = gate_weight.shape[1]
    share = 2 * units // TEAM
    block = features // GROUPS

    replica = gather_col(tokens, columns).reshape(2, 2, columns // 4 * held, features)

    spread = tokens.reshape(held, GROUPS, block).transpose(1, 0, 2)
    spread = jnp.broadcast_to(spread[:, None], (GROUPS, TEAM, held, block)).reshape(16, held, block)
    spread = lax.all_to_all(spread, DP, 0, 0)

    masked_gate = masked(gate_weight, mask_gate)
    masked_up = masked(up_weight, mask_up)
    both_weights = jnp.concatenate([masked_gate, masked_up], axis=1)
    masked_share = lax.dynamic_slice_in_dim(both_weights, member * share, share, axis=1)

    replica = jnp.where(half == 0, replica, replica[::-1])
    replica = jnp.where(core == 0, replica, replica[:, ::-1])
    rows = replica.shape[2]

    def project(x):
        return jnp.dot(x.reshape(2 * rows, features), both_weights, preferred_element_type=F32)

    others = lax.ppermute(project(replica[:, 1]), "row", OTHER_CORE)
    summed = project(replica[:, 0]) + others
    summed, spread, masked_share = lax.optimization_barrier((summed, spread, masked_share))
    arrived = lax.ppermute(summed[rows:].astype(BF16), "row", OTHER_HALF)
    everyone = gather_col(spread, columns)
    arrived, everyone = lax.optimization_barrier((arrived, everyone))
    proj = summed[:rows] + arrived.astype(F32)
    gate_proj, up_proj = proj[:, :units], proj[:, units:]

    sigmoid_gate = jax.nn.sigmoid(gate_proj)
    activation = gate_proj * sigmoid_gate
    hidden = (activation * up_proj).astype(BF16)
    cotangent = grad_hidden.astype(F32)
    grad_gate_act = (cotangent * up_proj * sigmoid_gate * (1.0 + gate_proj * (1.0 - sigmoid_gate))).astype(BF16)
    grad_up_act = (cotangent * activation).astype(BF16)

    shares = jnp.concatenate([grad_gate_act, grad_up_act], axis=1).reshape(rows, TEAM, share).transpose(1, 0, 2)
    mine = lax.all_to_all(shares, "member", 0, 0).reshape(TEAM * rows, share)
    own = ordered(core == 0, mine, lax.ppermute(mine, "row", OTHER_CORE))

    everyone = everyone.reshape(2, 2, columns // 4, GROUPS, TEAM, held, block)
    everyone = everyone.transpose(0, 3, 1, 4, 2, 5, 6).reshape(PLACES, 2 * TEAM * rows, block)
    twice = jnp.concatenate([everyone, everyone], axis=0)
    before = lax.dynamic_slice_in_dim(twice, place + STEPS, STEPS, axis=0)[::-1]
    after = lax.dynamic_slice_in_dim(twice, place, STEPS, axis=0)
    after = jnp.concatenate([after[1:], after[:1]], axis=0)
    mine_rows = jnp.where(core == 0, before, after)
    their_rows = lax.ppermute(jnp.where(core == 0, after, before), "row", OTHER_CORE)
    features_of = ordered(core == 0, mine_rows, their_rows, axis=2)

    contract_rows = (((0,), (0,)), ((), ()))
    total = None
    moving = own
    passing = None
    for step in range(STEPS):
        moving = lax.ppermute(moving, Z, RING)
        if step == PLACES // 4 - 1:
            passing = moving
        met = moving if step < STEPS - 1 else jnp.where(core == 0, moving, own)
        term = lax.dot_general(features_of[step], met, contract_rows, preferred_element_type=F32)
        total = term if total is None else total + term

    across = lax.ppermute(passing, "row", OTHER_CORE)
    far = jnp.where((group < PLACES // 4) == (core == 0), passing, across)
    part = lax.dot_general(
        jnp.concatenate([own, far], axis=0),
        masked_share,
        (((1,), (1,)), ((), ())),
        preferred_element_type=F32,
    ).astype(BF16)
    part = part.reshape(2, 2, TEAM, columns // 4, held, features)
    part = jnp.where(half == 0, part, part[::-1]).transpose(0, 1, 3, 2, 4, 5)
    part = part.reshape(columns, TEAM, held, features)
    reduced = jnp.sum(lax.all_to_all(part, "col", 0, 0).astype(F32), axis=0)
    reduced = jnp.sum(lax.all_to_all(reduced, "member", 0, 0), axis=0).astype(BF16)
    total, reduced = lax.optimization_barrier((total, reduced))
    swapped = lax.ppermute(reduced, "group", FAR_GROUP)
    grad_tokens = jnp.where((col < columns // 2) == (half == 0), reduced, swapped)

    got = lax.ppermute(jnp.where(core == 0, total[block:], total[:block]), "row", OTHER_CORE)
    full = jnp.where(core == 0, total[:block], total[block:]) + got
    traded = lax.all_to_all(full.astype(BF16).reshape(TEAM, block // TEAM, share), "member", 0, 0)
    grads = traded.transpose(1, 0, 2).reshape(block // TEAM, 2 * units).astype(F32)

    def kept_blocks(mask):
        line = (group * TEAM + member) * mask.shape[0] // 16
        line = lax.dynamic_slice_in_dim(mask, line, 1, axis=0).astype(F32)
        return jnp.repeat(line, units // mask.shape[1], axis=1)

    return (hidden, grad_tokens, grads[:, :units] * kept_blocks(mask_gate), grads[:, units:] * kept_blocks(mask_up))


def solution(mesh):
    replicas, rows, columns = (mesh.shape[name] for name in ("dp", "row", "col"))
    assert replicas == 16 and rows == 4
    split = Mesh(mesh.devices.reshape(GROUPS, TEAM, rows, columns), ("group", "member", "row", "col"))
    placed = (
        P(("group", "member", "col"), "row"),
        P("row", "col"),
        P("row", "col"),
        P("row", "col"),
        P("row", "col"),
        P(("group", "member", "row"), "col"),
    )
    return jax.shard_map(
        body,
        mesh=split,
        in_specs=placed,
        out_specs=(
            P(("group", "member", "row"), "col"),
            P(("group", "member", "col"), "row"),
            P(("row", "group", "member"), "col"),
            P(("row", "group", "member"), "col"),
        ),
        check_vma=False,
    )
```

time: 248 us -> 245 us (0.988)
  starting transfers between devices: 129 us -> 97.6 us
  blocking collectives: 0 us -> 15 us
  other arithmetic: 10.6 us -> 15.6 us
  waiting for transfers between devices: 95.7 us -> 98.9 us
  matrix products: 5.01 us -> 7.78 us
    ppermute x8 -> x4, waiting for transfers between devices: 56.5 us -> 35.6 us  [body(): moving = lax.ppermute(moving, Z, RING)]
    ppermute x6 -> x4, starting transfers between devices: 30.6 us -> 9.74 us  [the longest x1 3.99 us: body(): swapped = lax.ppermute(reduced, 'group', FAR_GROUP)]
    ppermute x1, waiting for transfers between devices: 5.9 us -> 21.2 us  [body(): arrived = lax.ppermute(summed[rows:].astype(BF16), 'row', OTHER_HALF)]
    all_to_all x0 -> x1, blocking collectives: none -> 15 us  [body(): mine = lax.all_to_all(shares, 'member', 0, 0).reshape(TEAM * rows, share)]
    all_to_all x1 -> x3, starting transfers between devices: 9.53 us -> 23.4 us  [the longest x1 11.6 us: body(): lax.all_to_all(full.astype(BF16).reshape(TEAM, block // TEAM, share), 'me...]
    all_to_all x1 -> x3, waiting for transfers between devices: 0.01 us -> 10.9 us  [the longest x1 10.9 us: body(): reduced = jnp.sum(lax.all_to_all(part, 'col', 0, 0).astype(F32), axis=0)]
    ppermute x8 -> x4, starting transfers between devices: 18.9 us -> 8.75 us  [body(): moving = lax.ppermute(moving, Z, RING)]
    ppermute x1, starting transfers between devices: 19.9 us -> 11.9 us  [body(): arrived = lax.ppermute(summed[rows:].astype(BF16), 'row', OTHER_HALF)]
  transfers between devices with their start and end apart: 21 -> 17, of which waited for: 15 -> 10; matrix products, arithmetic and copies ran while one was open for 6% -> 9% of each run, Pallas kernels for 0% -> 0%
where the time goes in v2:
time: 245 us; the launch traced here: 242 us
  waiting for transfers between devices  98.9 us (40%)
  starting transfers between devices  97.6 us (40%)
  other arithmetic  15.6 us (6%)
  blocking collectives  15 us (6%)
  matrix products  7.78 us (3%)
  local copies, waits for them, and re-layouts  5.97 us (2%)
    ppermute x4, waiting for transfers between devices, body(): moving = lax.ppermute(moving, Z, RING)  35.6 us
    all_to_all x2, starting transfers between devices, gather_col(): lax.all_to_all(jnp.broadcast_to(x[None], (count, *x.shape)), 'col', 0, 0)  22.8 us
    ppermute x1, waiting for transfers between devices, body(): arrived = lax.ppermute(summed[rows:].astype(BF16), 'row', OTHER_HALF)  21.2 us
    all_to_all x1, starting transfers between devices, body(): spread = lax.all_to_all(spread, DP, 0, 0)  16.8 us
    all_to_all x1, waiting for transfers between devices, body(): spread = lax.all_to_all(spread, DP, 0, 0)  16.6 us
    all_to_all x1, blocking collectives, body(): mine = lax.all_to_all(shares, 'member', 0, 0).reshape(TEAM * rows, share)  15 us
    ppermute x1, starting transfers between devices, body(): arrived = lax.ppermute(summed[rows:].astype(BF16), 'row', OTHER_HALF)  11.9 us
    all_to_all x1, starting transfers between devices, body(): lax.all_to_all(full.astype(BF16).reshape(TEAM, block // TEAM, share), 'me...  11.6 us
  transfers between devices with their start and end apart: 17, of which 10 were waited for; matrix products, arithmetic and copies ran while one was open for 9% of the time, Pallas kernels for 0%

profile of v2, /device:TPU:6, one launch (start us, length us, event | category | flops | bytes accessed | tf_op | source)
XLA Modules:
  0.0 242.0 jit_solution(17973359331942483148)
XLA Ops:
  0.6 1.5 broadcast_in_dim.34
  2.1 16.5 %all-to-all-start = ((bf16[16,8,1024]{2,1,0:T(8,128)(2,1)}), bf16[16,8,1024]{2,1,0:T(8,128)(2,1)S(1)}, u32[]{:S(2)}, u32[]{:S(2)}) async-start(bf16[16,8,1024]{2,1,0:T(8,128)(2,1)} %broadcast_in_dim.34), calls=%async_computation | async-start | bytes 524288 | tf_op jit(solution)/shard_map/all_to_all | solution.py:46
  18.6 0.7 convert_element_type.54
  19.3 0.1 copy.35
  19.4 0.1 broadcast_bitcast_fusion
  19.5 0.7 convert_element_type.53
  20.2 0.1 copy.34
  20.3 0.1 broadcast_bitcast_fusion.1
  20.3 3.7 %bitcast_multiply_fusion = (bf16[1024,896]{1,0:T(8,128)(2,1)S(1)}, bf16[1024,896]{1,0:T(8,128)(2,1)}) fusion(bf16[1024,896]{1,0:T(8,128)(2,1)} %param.8, bf16[8,896]{1,0:T(8,128)(2,1)S(1)} %broadcast_bitcast_fusion, bf16[1024,896]{1,0:T(8,128)(2,1)} %param.7, bf16[8,896]{1,0:T(8,128)(2,1)S(1)} %broadcast_bitcast_fusion.1), kind=kLoop, calls=%fused_computation.11 | loop fusion | flops 1835008 | bytes 7368704 | tf_op jit(solution)/shard_map/mul | solution.py:42
  24.0 1.0 all-to-all-done
  25.1 2.2 fusion
  27.4 1.9 collective-permute-start
  29.3 0.6 broadcast_in_dim.37
  30.0 16.8 %all-to-all-start.1 = ((bf16[16,8,256]{2,1,0:T(8,128)(2,1)}), bf16[16,8,256]{2,1,0:T(8,128)(2,1)S(1)}, u32[]{:S(2)}, u32[]{:S(2)}) async-start(bf16[16,8,256]{2,1,0:T(8,128)(2,1)} %bitcast.9), calls=%async_computation.1 | async-start | bytes 131072 | tf_op jit(solution)/shard_map/all_to_all | solution.py:64
  46.8 2.4 fusion.3
  49.2 1.8 fusion.2
  51.0 16.6 %all-to-all-done.1 = bf16[16,8,256]{2,1,0:T(8,128)(2,1)S(1)} async-done(((bf16[16,8,256]{2,1,0:T(8,128)(2,1)}), bf16[16,8,256]{2,1,0:T(8,128)(2,1)S(1)}, u32[]{:S(2)}, u32[]{:S(2)}) %all-to-all-start.1) | async-done | bytes 65568 | tf_op jit(solution)/shard_map/all_to_all | solution.py:64
  67.6 1.1 broadcast_in_dim.38
  68.7 6.2 %all-to-all-start.2 = ((bf16[16,16,8,256]{3,2,1,0:T(8,128)(2,1)}), bf16[16,16,8,256]{3,2,1,0:T(8,128)(2,1)S(1)}, u32[]{:S(2)}, u32[]{:S(2)}) async-start(bf16[16,16,8,256]{3,2,1,0:T(8,128)(2,1)} %broadcast_in_dim.38), calls=%async_computation.2 | async-start | bytes 2097152 | tf_op jit(solution)/shard_map/all_to_all | solution.py:46
  75.0 11.9 %collective-permute-start.1 = (bf16[32,1792]{1,0:T(8,128)(2,1)S(1)}, bf16[32,1792]{1,0:T(8,128)(2,1)S(1)}, u32[]{:S(2)}, u32[]{:S(2)}) collective-permute-start(bf16[32,1792]{1,0:T(8,128)(2,1)S(1)} %slice.128), channel_id=1, source_target_pairs={{0,32},{16,48},{32,0},{48,16},{1,33},{17,49},{33,1},{49,17},{2,34}... | collective-permute-start | bytes 344072 | tf_op jit(solution)/shard_map/ppermute | solution.py:81
  86.8 21.2 %collective-permute-done.1 = bf16[32,1792]{1,0:T(8,128)(2,1)S(1)} collective-permute-done((bf16[32,1792]{1,0:T(8,128)(2,1)S(1)}, bf16[32,1792]{1,0:T(8,128)(2,1)S(1)}, u32[]{:S(2)}, u32[]{:S(2)}) %collective-permute-start.1) | collective-permute-done | bytes 114720 | tf_op jit(solution)/shard_map/ppermute | solution.py:81
  108.1 0.7 fusion.28
  108.8 0.2 reshape.67
  109.0 15.0 %all_to_all.35 = bf16[4,32,448]{2,1,0:T(8,128)(2,1)S(1)} all-to-all(bf16[4,32,448]{2,1,0:T(8,128)(2,1)S(1)} %bitcast.60), channel_id=1, replica_groups=mesh['group'=4,'member'=4,'row'=4,'col'=16] {'member'}, dimensions={0} | all-to-all | bytes 229376 | tf_op jit(solution)/shard_map/all_to_all | solution.py:95
  124.1 0.1 copy.39
  124.2 1.9 collective-permute-start.3
  126.1 1.3 collective-permute-done.3
  127.5 1.9 collective-permute-start.4
  129.4 10.1 %collective-permute-done.4 = bf16[256,448]{0,1:T(8,128)(2,1)S(1)} collective-permute-done((bf16[256,448]{0,1:T(8,128)(2,1)S(1)}, bf16[256,448]{0,1:T(8,128)(2,1)S(1)}, u32[]{:S(2)}, u32[]{:S(2)}) %collective-permute-start.4) | collective-permute-done | bytes 229408 | tf_op jit(solution)/shard_map/ppermute | solution.py:113
  139.5 2.0 collective-permute-start.5
  141.5 0.1 copy.36
  141.7 17.4 %collective-permute-done.5 = bf16[256,448]{0,1:T(8,128)(2,1)} collective-permute-done((bf16[256,448]{0,1:T(8,128)(2,1)S(1)}, bf16[256,448]{0,1:T(8,128)(2,1)}, u32[]{:S(2)}, u32[]{:S(2)}) %collective-permute-start.5) | collective-permute-done | bytes 229408 | tf_op jit(solution)/shard_map/ppermute | solution.py:113
  159.1 1.9 collective-permute-start.8
  161.0 0.4 fusion.4
  161.4 0.1 broadcast_select_fusion.2
  161.6 2.4 collective-permute-start.2
  164.0 1.0 broadcast_select_fusion.4
  165.0 0.8 convolution_convert_fusion
  165.8 0.1 copy.42
  165.8 1.3 reverse_select_fusion
  167.1 7.2 %all-to-all-start.4 = ((bf16[16,4,8,1024]{3,2,1,0:T(8,128)(2,1)}), bf16[16,4,8,1024]{3,2,1,0:T(8,128)(2,1)S(1)}, u32[]{:S(2)}, u32[]{:S(2)}) async-start(bf16[16,4,8,1024]{3,2,1,0:T(8,128)(2,1)} %bitcast.21), calls=%async_computation.4 | async-start | bytes 2097152 | tf_op jit(solution)/shard_map/all_to_all | solution.py:131
  174.4 1.3 broadcast_select_fusion
  175.7 0.3 fusion.16
  176.0 1.9 collective-permute-start.6
  177.9 10.9 %all-to-all-done.4 = bf16[16,4,8,1024]{3,2,1,0:T(8,128)(2,1)S(1)} async-done(((bf16[16,4,8,1024]{3,2,1,0:T(8,128)(2,1)}), bf16[16,4,8,1024]{3,2,1,0:T(8,128)(2,1)S(1)}, u32[]{:S(2)}, u32[]{:S(2)}) %all-to-all-start.4) | async-done | bytes 1048608 | tf_op jit(solution)/shard_map/all_to_all | solution.py:131
  188.8 0.8 convert_reduce_fusion
  189.7 4.6 %all-to-all-start.5 = ((f32[4,8,1024]{2,1,0:T(8,128)}), f32[4,8,1024]{2,1,0:T(8,128)S(1)}, u32[]{:S(2)}, u32[]{:S(2)}) async-start(f32[4,8,1024]{2,1,0:T(8,128)} %convert_reduce_fusion), calls=%async_computation.5 | async-start | bytes 262144 | tf_op jit(solution)/shard_map/all_to_all | solution.py:132
  194.2 1.2 convolution_add_fusion.2
  195.5 2.9 %collective-permute-start.7 = (bf16[256,448]{0,1:T(8,128)(2,1)}, bf16[256,448]{0,1:T(8,128)(2,1)S(1)}, u32[]{:S(2)}, u32[]{:S(2)}) collective-permute-start(bf16[256,448]{0,1:T(8,128)(2,1)} %collective-permute-done.6), channel_id=1, source_target_pairs={{0,256},{16,816},{64,320},{80,880},{128,384},{144,944},{192,448},{... | collective-permute-start | bytes 688136 | tf_op jit(solution)/shard_map/ppermute | solution.py:113
  198.4 1.2 convolution_add_fusion.1
  199.6 8.1 %collective-permute-done.7 = bf16[256,448]{0,1:T(8,128)(2,1)S(1)} collective-permute-done((bf16[256,448]{0,1:T(8,128)(2,1)}, bf16[256,448]{0,1:T(8,128)(2,1)S(1)}, u32[]{:S(2)}, u32[]{:S(2)}) %collective-permute-start.7) | collective-permute-done | bytes 229408 | tf_op jit(solution)/shard_map/ppermute | solution.py:113
  207.8 0.3 convolution_add_fusion
  208.2 1.9 collective-permute-start.10
  210.1 1.8 collective-permute-done.10
  211.9 0.1 add_convert_fusion
  212.0 0.8 copy.43
  212.8 11.6 %all-to-all-start.6 = ((bf16[4,64,448]{2,1,0:T(8,128)(2,1)}), bf16[4,64,448]{2,1,0:T(8,128)(2,1)S(1)}, u32[]{:S(2)}, u32[]{:S(2)}) async-start(bf16[4,64,448]{2,1,0:T(8,128)(2,1)} %bitcast.22), calls=%async_computation.6 | async-start | bytes 524288 | tf_op jit(solution)/shard_map/all_to_all | solution.py:139
  224.4 0.7 fusion.32
  225.2 4.0 %collective-permute-start.9 = (bf16[8,1024]{1,0:T(8,128)(2,1)S(1)}, bf16[8,1024]{1,0:T(8,128)(2,1)S(1)}, u32[]{:S(2)}, u32[]{:S(2)}) collective-permute-start(bf16[8,1024]{1,0:T(8,128)(2,1)S(1)} %reduce_sum.19), channel_id=1, source_target_pairs={{0,512},{256,768},{512,0},{768,256},{1,513},{257,769},{513,1},{769... | collective-permute-start | bytes 49160 | tf_op jit(solution)/shard_map/ppermute | solution.py:134
  229.3 10.4 %collective-permute-done.9 = bf16[8,1024]{1,0:T(8,128)(2,1)S(1)} collective-permute-done((bf16[8,1024]{1,0:T(8,128)(2,1)S(1)}, bf16[8,1024]{1,0:T(8,128)(2,1)S(1)}, u32[]{:S(2)}, u32[]{:S(2)}) %collective-permute-start.9) | collective-permute-done | bytes 16416 | tf_op jit(solution)/shard_map/ppermute | solution.py:134
  239.7 0.6 broadcast_select_fusion.7
  240.4 0.3 copy.44
  240.7 0.5 reshape.72
  241.2 0.8 slice_multiply_fusion
  (33 shorter events, 0.6 us)
Async XLA Ops:
  2.1 22.9 %all-to-all-start = ((bf16[16,8,1024]{2,1,0:T(8,128)(2,1)}), bf16[16,8,1024]{2,1,0:T(8,128)(2,1)S(1)}, u32[]{:S(2)}, u32[]{:S(2)}) async-start(bf16[16,8,1024]{2,1,0:T(8,128)(2,1)} %broadcast_in_dim.34), calls=%async_computation | async-start | bytes 524288 | tf_op jit(solution)/shard_map/all_to_all | solution.py:46
  25.1 4.2 %copy-start.3 = (bf16[8,1024]{1,0:T(8,128)(2,1)S(1)}, bf16[8,1024]{1,0:T(8,128)(2,1)}, u32[]{:S(2)}) copy-start(bf16[8,1024]{1,0:T(8,128)(2,1)} %param.6) | copy-start | bytes 49156
  27.4 21.8 %collective-permute-start = (f32[64,1792]{1,0:T(8,128)S(1)}, f32[64,1792]{1,0:T(8,128)}, u32[]{:S(2)}, u32[]{:S(2)}) collective-permute-start(f32[64,1792]{1,0:T(8,128)S(1)} %fusion), channel_id=1, source_target_pairs={{0,16},{16,0},{32,48},{48,32},{1,17},{17,1},{33,49},{49,33},{2,18}... | collective-permute-start | bytes 1376264 | tf_op jit(solution)/shard_map/ppermute | solution.py:78
  30.0 37.6 %all-to-all-start.1 = ((bf16[16,8,256]{2,1,0:T(8,128)(2,1)}), bf16[16,8,256]{2,1,0:T(8,128)(2,1)S(1)}, u32[]{:S(2)}, u32[]{:S(2)}) async-start(bf16[16,8,256]{2,1,0:T(8,128)(2,1)} %bitcast.9), calls=%async_computation.1 | async-start | bytes 131072 | tf_op jit(solution)/shard_map/all_to_all | solution.py:64
  46.8 2.4 %copy-start = (bf16[1024,896]{1,0:T(8,128)(2,1)S(1)}, bf16[1024,896]{1,0:T(8,128)(2,1)}, u32[]{:S(2)}) copy-start(bf16[1024,896]{1,0:T(8,128)(2,1)} %get-tuple-element.32) | copy-start | bytes 5505028
  51.0 57.1 %copy-start.4 = (bf16[32,896]{1,0:T(8,128)(2,1)S(1)}, bf16[32,896]{1,0:T(8,128)(2,1)}, u32[]{:S(2)}) copy-start(bf16[32,896]{1,0:T(8,128)(2,1)} %param.11) | copy-start | bytes 172036
  68.7 39.4 %all-to-all-start.2 = ((bf16[16,16,8,256]{3,2,1,0:T(8,128)(2,1)}), bf16[16,16,8,256]{3,2,1,0:T(8,128)(2,1)S(1)}, u32[]{:S(2)}, u32[]{:S(2)}) async-start(bf16[16,16,8,256]{3,2,1,0:T(8,128)(2,1)} %broadcast_in_dim.38), calls=%async_computation.2 | async-start | bytes 2097152 | tf_op jit(solution)/shard_map/all_to_all | solution.py:46
  75.0 33.1 %collective-permute-start.1 = (bf16[32,1792]{1,0:T(8,128)(2,1)S(1)}, bf16[32,1792]{1,0:T(8,128)(2,1)S(1)}, u32[]{:S(2)}, u32[]{:S(2)}) collective-permute-start(bf16[32,1792]{1,0:T(8,128)(2,1)S(1)} %slice.128), channel_id=1, source_target_pairs={{0,32},{16,48},{32,0},{48,16},{1,33},{17,49},{33,1},{49,17},{2,34}... | collective-permute-start | bytes 344072 | tf_op jit(solution)/shard_map/ppermute | solution.py:81
  124.2 3.2 %collective-permute-start.3 = (bf16[128,448]{0,1:T(8,128)(2,1)S(1)}, bf16[128,448]{0,1:T(8,128)(2,1)S(1)}, u32[]{:S(2)}, u32[]{:S(2)}) collective-permute-start(bf16[128,448]{0,1:T(8,128)(2,1)S(1)} %copy.39), channel_id=1, source_target_pairs={{0,16},{16,0},{32,48},{48,32},{1,17},{17,1},{33,49},{49,33},{2,18}... | collective-permute-start | bytes 344072 | tf_op jit(solution)/shard_map/ppermute | solution.py:96
  127.5 12.0 %collective-permute-start.4 = (bf16[256,448]{0,1:T(8,128)(2,1)S(1)}, bf16[256,448]{0,1:T(8,128)(2,1)S(1)}, u32[]{:S(2)}, u32[]{:S(2)}) collective-permute-start(bf16[256,448]{0,1:T(8,128)(2,1)S(1)} %pad_maximum_fusion.7), channel_id=1, source_target_pairs={{0,256},{16,816},{64,320},{80,880},{128,384},{144,944},{192,448},{... | collective-permute-start | bytes 688136 | tf_op jit(solution)/shard_map/ppermute | solution.py:113
  139.5 21.9 %copy-start.1 = (bf16[256,448]{0,1:T(8,128)(2,1)}, bf16[256,448]{0,1:T(8,128)(2,1)S(1)}, u32[]{:S(2)}) copy-start(bf16[256,448]{0,1:T(8,128)(2,1)S(1)} %collective-permute-done.4) | copy-start | bytes 688132
  139.5 19.5 %collective-permute-start.5 = (bf16[256,448]{0,1:T(8,128)(2,1)S(1)}, bf16[256,448]{0,1:T(8,128)(2,1)}, u32[]{:S(2)}, u32[]{:S(2)}) collective-permute-start(bf16[256,448]{0,1:T(8,128)(2,1)S(1)} %collective-permute-done.4), channel_id=1, source_target_pairs={{0,256},{16,816},{64,320},{80,880},{128,384},{144,944},{192,448},{... | collective-permute-start | bytes 688136 | tf_op jit(solution)/shard_map/ppermute | solution.py:113
  159.1 4.9 %collective-permute-start.8 = (bf16[256,448]{0,1:T(8,128)(2,1)}, bf16[256,448]{0,1:T(8,128)(2,1)S(1)}, u32[]{:S(2)}, u32[]{:S(2)}) collective-permute-start(bf16[256,448]{0,1:T(8,128)(2,1)} %collective-permute-done.5), channel_id=1, source_target_pairs={{0,16},{16,0},{32,48},{48,32},{1,17},{17,1},{33,49},{49,33},{2,18}... | collective-permute-start | bytes 688136 | tf_op jit(solution)/shard_map/ppermute | solution.py:120
  161.6 12.8 %collective-permute-start.2 = (bf16[4,256,256]{2,1,0:T(8,128)(2,1)S(1)}, bf16[4,256,256]{2,1,0:T(8,128)(2,1)}, u32[]{:S(2)}, u32[]{:S(2)}) collective-permute-start(bf16[4,256,256]{2,1,0:T(8,128)(2,1)S(1)} %broadcast_select_fusion.2), channel_id=1, source_target_pairs={{0,16},{16,0},{32,48},{48,32},{1,17},{17,1},{33,49},{49,33},{2,18}... | collective-permute-start | bytes 1572872 | tf_op jit(solution)/shard_map/ppermute | solution.py:105
  167.1 21.7 %all-to-all-start.4 = ((bf16[16,4,8,1024]{3,2,1,0:T(8,128)(2,1)}), bf16[16,4,8,1024]{3,2,1,0:T(8,128)(2,1)S(1)}, u32[]{:S(2)}, u32[]{:S(2)}) async-start(bf16[16,4,8,1024]{3,2,1,0:T(8,128)(2,1)} %bitcast.21), calls=%async_computation.4 | async-start | bytes 2097152 | tf_op jit(solution)/shard_map/all_to_all | solution.py:131
  174.4 1.3 copy-start.2
  176.0 19.5 %collective-permute-start.6 = (bf16[256,448]{0,1:T(8,128)(2,1)}, bf16[256,448]{0,1:T(8,128)(2,1)}, u32[]{:S(2)}, u32[]{:S(2)}) collective-permute-start(bf16[256,448]{0,1:T(8,128)(2,1)} %collective-permute-done.5), channel_id=1, source_target_pairs={{0,256},{16,816},{64,320},{80,880},{128,384},{144,944},{192,448},{... | collective-permute-start | bytes 688136 | tf_op jit(solution)/shard_map/ppermute | solution.py:113
  189.7 18.4 %all-to-all-start.5 = ((f32[4,8,1024]{2,1,0:T(8,128)}), f32[4,8,1024]{2,1,0:T(8,128)S(1)}, u32[]{:S(2)}, u32[]{:S(2)}) async-start(f32[4,8,1024]{2,1,0:T(8,128)} %convert_reduce_fusion), calls=%async_computation.5 | async-start | bytes 262144 | tf_op jit(solution)/shard_map/all_to_all | solution.py:132
  195.5 12.3 %collective-permute-start.7 = (bf16[256,448]{0,1:T(8,128)(2,1)}, bf16[256,448]{0,1:T(8,128)(2,1)S(1)}, u32[]{:S(2)}, u32[]{:S(2)}) collective-permute-start(bf16[256,448]{0,1:T(8,128)(2,1)} %collective-permute-done.6), channel_id=1, source_target_pairs={{0,256},{16,816},{64,320},{80,880},{128,384},{144,944},{192,448},{... | collective-permute-start | bytes 688136 | tf_op jit(solution)/shard_map/ppermute | solution.py:113
  208.2 3.7 %collective-permute-start.10 = (f32[256,448]{0,1:T(8,128)S(1)}, f32[256,448]{0,1:T(8,128)S(1)}, u32[]{:S(2)}, u32[]{:S(2)}) collective-permute-start(f32[256,448]{0,1:T(8,128)S(1)} %slice_select_fusion), channel_id=1, source_target_pairs={{0,16},{16,0},{32,48},{48,32},{1,17},{17,1},{33,49},{49,33},{2,18}... | collective-permute-start | bytes 1376264 | tf_op jit(solution)/shard_map/ppermute | solution.py:137
  212.8 27.5 %all-to-all-start.6 = ((bf16[4,64,448]{2,1,0:T(8,128)(2,1)}), bf16[4,64,448]{2,1,0:T(8,128)(2,1)S(1)}, u32[]{:S(2)}, u32[]{:S(2)}) async-start(bf16[4,64,448]{2,1,0:T(8,128)(2,1)} %bitcast.22), calls=%async_computation.6 | async-start | bytes 524288 | tf_op jit(solution)/shard_map/all_to_all | solution.py:139
  225.2 14.5 %collective-permute-start.9 = (bf16[8,1024]{1,0:T(8,128)(2,1)S(1)}, bf16[8,1024]{1,0:T(8,128)(2,1)S(1)}, u32[]{:S(2)}, u32[]{:S(2)}) collective-permute-start(bf16[8,1024]{1,0:T(8,128)(2,1)S(1)} %reduce_sum.19), channel_id=1, source_target_pairs={{0,512},{256,768},{512,0},{768,256},{1,513},{257,769},{513,1},{769... | collective-permute-start | bytes 49160 | tf_op jit(solution)/shard_map/ppermute | solution.py:134

commit v3 on v2

v3 whole, which is shorter than its diff:
```python
import jax
import jax.numpy as jnp
from jax import lax
from jax.sharding import Mesh, PartitionSpec as P

BF16 = jnp.bfloat16
F32 = jnp.float32

TEAM = 4
GROUPS = 16 // TEAM
PLACES = 2 * GROUPS
STEPS = PLACES // 2
Z = ("group", "member", "half", "core")


def z_index(place, member, core):
    return ((place % GROUPS) * TEAM + member) * 4 + (place // GROUPS) * 2 + core


RING = [
    (z_index(place, member, core), z_index((place + (1, -1)[core]) % PLACES, member, core))
    for place in range(PLACES)
    for member in range(TEAM)
    for core in range(2)
]
SWAP = [(0, 1), (1, 0)]
FAR_GROUP = [(group, group ^ (PLACES // 4)) for group in range(GROUPS)]


def ordered(first_is_mine, mine, theirs, axis=0):
    return jnp.concatenate(
        [jnp.where(first_is_mine, mine, theirs), jnp.where(first_is_mine, theirs, mine)], axis=axis
    )


def masked(weight, mask):
    blocks, across = mask.shape
    rows, units = weight.shape
    keep = jnp.repeat(mask.astype(BF16), units // across, axis=1)
    return (weight.reshape(blocks, rows // blocks, units) * keep[:, None, :]).reshape(rows, units)


def gather_col(x, count):
    return lax.all_to_all(jnp.broadcast_to(x[None], (count, *x.shape)), "col", 0, 0)


def in_turns(x, after, turns=2):
    part = x.shape[0] // turns

    def turn(i, y):
        piece = lax.dynamic_slice_in_dim(x, i * part, part, axis=0)
        return lax.dynamic_update_slice_in_dim(y, piece, i * part, axis=0)

    return lax.fori_loop(0, turns, turn, jnp.broadcast_to(after.ravel()[0].astype(x.dtype), x.shape))


def add_term(total, rows, met, turns=2):
    part = met.shape[0] // turns

    def turn(i, total):
        return total + lax.dot_general(
            lax.dynamic_slice_in_dim(rows, i * part, part, axis=0),
            lax.dynamic_slice_in_dim(met, i * part, part, axis=0),
            (((0,), (0,)), ((), ())),
            preferred_element_type=F32,
        )

    return lax.fori_loop(0, turns, turn, total)


def spread_over_dp(x, group, member):
    blocks, held, block = x.shape
    x = x.reshape(blocks, 1, held, block)
    bit = blocks // 2
    while bit:
        up = (group & bit) != 0
        low, high = x[:bit], x[bit:]
        theirs = lax.ppermute(jnp.where(up, low, high), "group", [(i, i ^ bit) for i in range(GROUPS)])
        x = ordered(~up, jnp.where(up, high, low), theirs, axis=1)
        bit //= 2
    bits = GROUPS.bit_length() - 1
    x = x.reshape(*(2,) * bits, held, block).transpose(*range(bits - 1, -1, -1), bits, bits + 1)
    x = x.reshape(GROUPS, 1, held, block)
    bit = 1
    while bit < TEAM:
        theirs = lax.ppermute(x, "member", [(i, i ^ bit) for i in range(TEAM)])
        x = ordered((member & bit) == 0, x, theirs, axis=1)
        bit *= 2
    return x.reshape(16, held, block)


def body(tokens, gate_weight, up_weight, mask_gate, mask_up, grad_hidden):
    columns = lax.axis_size("col")
    group, member = lax.axis_index("group"), lax.axis_index("member")
    half, core, col = lax.axis_index("half"), lax.axis_index("core"), lax.axis_index("col")
    place = half * GROUPS + group
    held, features = tokens.shape
    units = gate_weight.shape[1]
    share = 2 * units // TEAM
    block = features // GROUPS

    replica = gather_col(tokens, columns).reshape(2, 2, columns // 4 * held, features)

    spread = tokens.reshape(held, GROUPS, block).transpose(1, 0, 2)
    spread = spread_over_dp(spread, group, member)

    both_weights = jnp.concatenate([masked(gate_weight, mask_gate), masked(up_weight, mask_up)], axis=1)
    replica = jnp.where(half == 0, replica, replica[::-1])
    replica = jnp.where(core == 0, replica, replica[:, ::-1])
    rows = replica.shape[2]

    def project(x):
        return jnp.dot(x.reshape(2 * rows, features), both_weights, preferred_element_type=F32)

    others = lax.ppermute(project(replica[:, 1]), "core", SWAP)
    summed = project(replica[:, 0]) + others
    summed, spread, both_weights = lax.optimization_barrier((summed, spread, both_weights))

    arrived = lax.ppermute(summed[rows:].astype(BF16), "half", SWAP)
    spread = in_turns(spread, summed[:1, :1])
    everyone = gather_col(spread, columns)
    masked_share = in_turns(lax.dynamic_slice_in_dim(both_weights, member * share, share, axis=1), summed[:1, :1], 16)
    arrived, everyone, masked_share = lax.optimization_barrier((arrived, everyone, masked_share))
    proj = summed[:rows] + arrived.astype(F32)
    gate_proj, up_proj = proj[:, :units], proj[:, units:]

    sigmoid_gate = jax.nn.sigmoid(gate_proj)
    activation = gate_proj * sigmoid_gate
    hidden = (activation * up_proj).astype(BF16)
    cotangent = grad_hidden.astype(F32)
    grad_gate_act = (cotangent * up_proj * sigmoid_gate * (1.0 + gate_proj * (1.0 - sigmoid_gate))).astype(BF16)
    grad_up_act = (cotangent * activation).astype(BF16)

    shares = jnp.concatenate([grad_gate_act, grad_up_act], axis=1).reshape(rows, TEAM, share).transpose(1, 0, 2)
    shares = jnp.broadcast_to(shares[:, None], (TEAM, 2, rows, share)).reshape(2 * TEAM, rows, share)
    own = lax.all_to_all(shares, ("member", "core"), 0, 0).reshape(TEAM, 2, rows, share)
    own = own.transpose(1, 0, 2, 3).reshape(2 * TEAM * rows, share)
    own, everyone = lax.optimization_barrier((own, everyone))

    first = lax.ppermute(own, Z, RING)
    everyone = everyone.reshape(2, 2, columns // 4, GROUPS, TEAM, held, block)
    everyone = everyone.transpose(0, 3, 1, 4, 2, 5, 6).reshape(PLACES, 2 * TEAM * rows, block)
    twice = jnp.concatenate([everyone, everyone], axis=0)
    before = lax.dynamic_slice_in_dim(twice, place + STEPS, STEPS, axis=0)[::-1]
    after = lax.dynamic_slice_in_dim(twice, place, STEPS, axis=0)
    after = jnp.concatenate([after[1:], after[:1]], axis=0)
    my_rows, their_rows = jnp.where(core == 0, before, after), jnp.where(core == 0, after, before)
    first, my_rows, their_rows = lax.optimization_barrier((first, my_rows, their_rows))

    def add(step, tokens_of, met, *total):
        start = total[0] if total else jnp.zeros((tokens_of.shape[2], share), F32)
        return add_term(start, tokens_of[step], met)

    second = lax.ppermute(first, Z, RING)
    low = add(0, my_rows[:1, :, : block // 2], first)
    low, their_rows = lax.optimization_barrier((low, their_rows))
    their_rows = lax.ppermute(their_rows, "core", SWAP)
    high = add(0, my_rows[:1, :, block // 2 :], first)
    second, low, high, their_rows = lax.optimization_barrier((second, low, high, their_rows))
    my_total = jnp.concatenate([low, high], axis=0)

    third = lax.ppermute(second, Z, RING)
    my_total = add(1, my_rows, second, my_total)
    my_total, passing = lax.optimization_barrier((my_total, second))
    across = lax.ppermute(passing, "core", SWAP)
    far = jnp.where((group < PLACES // 4) == (core == 0), passing, across)
    part = lax.dot_general(
        jnp.concatenate([own, far], axis=0),
        masked_share,
        (((1,), (1,)), ((), ())),
        preferred_element_type=F32,
    ).astype(BF16)
    part = part.reshape(2, 2, TEAM, columns // 4, held, features)
    part = jnp.where(half == 0, part, part[::-1]).transpose(0, 1, 3, 2, 4, 5)
    part = part.reshape(columns, TEAM, held, features)
    their_total = add(1, their_rows, second, add(0, their_rows, first))
    third, my_total, their_total = lax.optimization_barrier((third, my_total, their_total))

    fourth = lax.ppermute(third, Z, RING)
    my_total = add(2, my_rows, third, my_total)
    part = lax.all_to_all(part, "col", 0, 0)
    their_total = add(2, their_rows, third, their_total)
    fourth, my_total, their_total, part = lax.optimization_barrier((fourth, my_total, their_total, part))

    last = jnp.where(core == 0, fourth, own)
    got = lax.ppermute(add(3, their_rows, last, their_total), "core", SWAP)
    reduced = jnp.sum(part.astype(F32), axis=0)
    reduced = jnp.sum(lax.all_to_all(reduced, "member", 0, 0), axis=0).astype(BF16)
    full = add(3, my_rows, last, my_total) + got
    full, reduced = lax.optimization_barrier((full, reduced))
    swapped = lax.ppermute(reduced, "group", FAR_GROUP)
    grad_tokens = jnp.where((col < columns // 2) == (half == 0), reduced, swapped)
    traded = lax.all_to_all(full.astype(BF16).reshape(TEAM, block // TEAM, share), "member", 0, 0)
    grads = traded.transpose(1, 0, 2).reshape(block // TEAM, 2 * units).astype(F32)

    def kept_blocks(mask):
        line = (group * TEAM + member) * mask.shape[0] // 16
        line = lax.dynamic_slice_in_dim(mask, line, 1, axis=0).astype(F32)
        return jnp.repeat(line, units // mask.shape[1], axis=1)

    return (hidden, grad_tokens, grads[:, :units] * kept_blocks(mask_gate), grads[:, units:] * kept_blocks(mask_up))


def solution(mesh):
    replicas, rows, columns = (mesh.shape[name] for name in ("dp", "row", "col"))
    assert replicas == 16 and rows == 4
    split = Mesh(
        mesh.devices.reshape(GROUPS, TEAM, 2, 2, columns), ("group", "member", "half", "core", "col")
    )
    placed = (
        P(("group", "member", "col"), ("half", "core")),
        P(("half", "core"), "col"),
        P(("half", "core"), "col"),
        P(("half", "core"), "col"),
        P(("half", "core"), "col"),
        P(("group", "member", "half", "core"), "col"),
    )
    return jax.shard_map(
        body,
        mesh=split,
        in_specs=placed,
        out_specs=(
            P(("group", "member", "half", "core"), "col"),
            P(("group", "member", "col"), ("half", "core")),
            P(("half", "core", "group", "member"), "col"),
            P(("half", "core", "group", "member"), "col"),
        ),
        check_vma=False,
    )
```

time: 245 us -> 245 us (level)
  waiting for transfers between devices: 98.9 us -> 70 us
  matrix products: 7.78 us -> 24.7 us
  local copies, waits for them, and re-layouts: 5.97 us -> 21.3 us
  blocking collectives: 15 us -> 0 us
  starting transfers between devices: 97.6 us -> 109 us
    ppermute x10 -> x13, starting transfers between devices: 30.7 us -> 57 us  [the longest x1 20.2 us: body(): arrived = lax.ppermute(summed[rows:].astype(BF16), 'half', SWAP)]
    ppermute x10 -> x13, waiting for transfers between devices: 60 us -> 42.7 us  [the longest x1 16.4 us: body(): first = lax.ppermute(own, Z, RING)]
    dot_general x4 -> x18, matrix products: 2.99 us -> 18.4 us  [turn(): lax.dot_general(lax.dynamic_slice_in_dim(rows, i * part, part, axis=0), l...]
    all_to_all x1 -> x0, blocking collectives: 15 us -> none  [body(): mine = lax.all_to_all(shares, 'member', 0, 0).reshape(TEAM * rows, share)]
    all_to_all x2, starting transfers between devices: 24 us -> 10.9 us  [the longest x1 7.51 us: body(): part = lax.all_to_all(part, 'col', 0, 0)]
    dynamic_update_slice x0 -> x18, local copies, waits for them, and re-layouts: none -> 9.98 us  [turn(): return lax.dynamic_update_slice_in_dim(y, piece, i * part, axis=0)]
    all_to_all x1, starting transfers between devices: 11.6 us -> 4.5 us  [body(): lax.all_to_all(full.astype(BF16).reshape(TEAM, block // TEAM, share), 'me...]
    all_to_all x2, waiting for transfers between devices: 27.5 us -> 21.3 us  [the longest x1 11.7 us: body(): part = lax.all_to_all(part, 'col', 0, 0)]
  transfers between devices with their start and end apart: 17 -> 20, of which waited for: 10 -> 13; matrix products, arithmetic and copies ran while one was open for 9% -> 20% of each run, Pallas kernels for 0% -> 0%
where the time goes in v3:
time: 245 us; the launch traced here: 241 us
  starting transfers between devices  109 us (44%)
  waiting for transfers between devices  70 us (29%)
  matrix products  24.7 us (10%)
  local copies, waits for them, and re-layouts  21.3 us (9%)
  other arithmetic  15 us (6%)
    all_to_all x2, starting transfers between devices, gather_col(): lax.all_to_all(jnp.broadcast_to(x[None], (count, *x.shape)), 'col', 0, 0)  23.7 us
    ppermute x1, starting transfers between devices, body(): arrived = lax.ppermute(summed[rows:].astype(BF16), 'half', SWAP)  20.2 us
    dot_general x18, matrix products, turn(): lax.dot_general(lax.dynamic_slice_in_dim(rows, i * part, part, axis=0), l...  18.4 us
    ppermute x1, waiting for transfers between devices, body(): first = lax.ppermute(own, Z, RING)  16.4 us
    all_to_all x1, waiting for transfers between devices, body(): part = lax.all_to_all(part, 'col', 0, 0)  11.7 us
    dynamic_update_slice x18, local copies, waits for them, and re-layouts, turn(): return lax.dynamic_update_slice_in_dim(y, piece, i * part, axis=0)  9.98 us
    ppermute x2, waiting for transfers between devices, spread_over_dp(): lax.ppermute(jnp.where(up, low, high), 'group', [(i, i ^ bit) for i in ra...  9.77 us
    ppermute x2, starting transfers between devices, spread_over_dp(): lax.ppermute(jnp.where(up, low, high), 'group', [(i, i ^ bit) for i in ra...  9.75 us
  transfers between devices with their start and end apart: 20, of which 13 were waited for; matrix products, arithmetic and copies ran while one was open for 20% of the time, Pallas kernels for 0%

profile of v3, /device:TPU:6, one launch (start us, length us, event | category | flops | bytes accessed | tf_op | source)
XLA Modules:
  0.0 241.4 jit_solution(13358868341402899455)
XLA Ops:
  0.6 1.4 broadcast_in_dim.43
  2.1 16.5 %all-to-all-start = ((bf16[16,8,1024]{2,1,0:T(8,128)(2,1)}), bf16[16,8,1024]{2,1,0:T(8,128)(2,1)S(1)}, u32[]{:S(2)}, u32[]{:S(2)}) async-start(bf16[16,8,1024]{2,1,0:T(8,128)(2,1)} %broadcast_in_dim.43), calls=%async_computation | async-start | bytes 524288 | tf_op jit(solution)/shard_map/all_to_all | solution.py:44
  19.3 6.6 %collective-permute-start.1 = (bf16[2,1,8,256]{3,2,0,1:T(8,128)(2,1)S(1)}, bf16[2,1,8,256]{3,2,0,1:T(8,128)(2,1)S(1)}, u32[]{:S(2)}, u32[]{:S(2)}) collective-permute-start(bf16[2,1,8,256]{3,2,0,1:T(8,128)(2,1)S(1)} %select_bitcast_fusion), channel_id=1, source_target_pairs={{0,512},{256,768},{512,0},{768,256},{1,513},{257,769},{513,1},{769... | collective-permute-start | bytes 24584 | tf_op jit(solution)/shard_map/ppermute | solution.py:78
  27.6 6.0 %collective-permute-done.1 = bf16[2,1,8,256]{3,2,0,1:T(8,128)(2,1)S(1)} collective-permute-done((bf16[2,1,8,256]{3,2,0,1:T(8,128)(2,1)S(1)}, bf16[2,1,8,256]{3,2,0,1:T(8,128)(2,1)S(1)}, u32[]{:S(2)}, u32[]{:S(2)}) %collective-permute-start.1) | collective-permute-done | bytes 8224 | tf_op jit(solution)/shard_map/ppermute | solution.py:78
  34.3 3.1 %collective-permute-start.2 = (bf16[1,2,8,256]{3,2,0,1:T(8,128)(2,1)S(1)}, bf16[1,2,8,256]{3,2,0,1:T(8,128)(2,1)S(1)}, u32[]{:S(2)}, u32[]{:S(2)}) collective-permute-start(bf16[1,2,8,256]{3,2,0,1:T(8,128)(2,1)S(1)} %broadcast_select_fusion.10), channel_id=1, source_target_pairs={{0,256},{256,0},{512,768},{768,512},{1,257},{257,1},{513,769},{769... | collective-permute-start | bytes 24584 | tf_op jit(solution)/shard_map/ppermute | solution.py:78
  37.5 2.4 %bitcast_multiply_fusion = (bf16[1024,896]{1,0:T(8,128)(2,1)S(1)}, bf16[1024,896]{1,0:T(8,128)(2,1)S(1)}) fusion(bf16[1024,896]{1,0:T(8,128)(2,1)} %param.30, bf16[8,896]{1,0:T(8,128)(2,1)S(1)} %broadcast_bitcast_fusion, bf16[1024,896]{1,0:T(8,128)(2,1)} %param.29, bf16[8,896]{1,0:T(8,128)(2,1)S(1)} %broadcast_bitcast_fusion.1), kind=kLoop, calls=%fused_computation.45 | loop fusion | flops 1835008 | bytes 7368704 | tf_op jit(solution)/shard_map/mul | solution.py:40
  39.9 3.8 %collective-permute-done.2 = bf16[1,2,8,256]{3,2,0,1:T(8,128)(2,1)S(1)} collective-permute-done((bf16[1,2,8,256]{3,2,0,1:T(8,128)(2,1)S(1)}, bf16[1,2,8,256]{3,2,0,1:T(8,128)(2,1)S(1)}, u32[]{:S(2)}, u32[]{:S(2)}) %collective-permute-start.2) | collective-permute-done | bytes 8224 | tf_op jit(solution)/shard_map/ppermute | solution.py:78
  43.8 1.9 collective-permute-start.3
  45.7 2.1 pad_maximum_fusion
  47.8 1.6 collective-permute-done.3
  49.6 2.8 %fusion.44 = f32[64,1792]{1,0:T(8,128)S(1)} fusion(bf16[64,1024]{1,0:T(8,128)(2,1)S(1)} %bitcast.85, bf16[1024,1792]{1,0:T(8,128)(2,1)} %pad_maximum_fusion), kind=kOutput, calls=%fused_computation.118 | convolution fusion | flops 234881024 | bytes 4259840 | tf_op jit(solution)/shard_map/dot_general | solution.py:113
  52.3 1.9 collective-permute-start
  54.3 1.9 collective-permute-start.4
  56.2 5.2 %collective-permute-done.4 = bf16[4,2,8,256]{3,2,1,0:T(8,128)(2,1)S(1)} collective-permute-done((bf16[4,2,8,256]{3,2,1,0:T(8,128)(2,1)S(1)}, bf16[4,2,8,256]{3,2,1,0:T(8,128)(2,1)S(1)}, u32[]{:S(2)}, u32[]{:S(2)}) %collective-permute-start.4) | collective-permute-done | bytes 32800 | tf_op jit(solution)/shard_map/ppermute | solution.py:86
  61.4 2.8 %convolution_add_fusion.9 = f32[64,1792]{1,0:T(8,128)S(1)} fusion(f32[64,1792]{1,0:T(8,128)S(1)} %collective-permute-done, bf16[64,1024]{1,0:T(8,128)(2,1)S(1)} %bitcast.84, bf16[1024,1792]{1,0:T(8,128)(2,1)} %pad_maximum_fusion), kind=kOutput, calls=%fused_computation.43 | convolution fusion | flops 234995712 | bytes 4718592 | tf_op jit(solution)/shard_map/dot_general | solution.py:113
  64.8 20.2 %collective-permute-start.5 = (bf16[32,1792]{1,0:T(8,128)(2,1)S(1)}, bf16[32,1792]{1,0:T(8,128)(2,1)S(1)}, u32[]{:S(2)}, u32[]{:S(2)}) collective-permute-start(bf16[32,1792]{1,0:T(8,128)(2,1)S(1)} %slice.107), channel_id=1, source_target_pairs={{0,32},{32,0},{1,33},{33,1},{2,34},{34,2},{3,35},{35,3},{4,36},{36... | collective-permute-start | bytes 344072 | tf_op jit(solution)/shard_map/ppermute | solution.py:119
  85.7 1.1 broadcast_in_dim.47
  86.8 7.2 %all-to-all-start.1 = ((bf16[16,16,8,256]{3,2,1,0:T(8,128)(2,1)}), bf16[16,16,8,256]{3,2,1,0:T(8,128)(2,1)S(1)}, u32[]{:S(2)}, u32[]{:S(2)}) async-start(bf16[16,16,8,256]{3,2,1,0:T(8,128)(2,1)} %broadcast_in_dim.47), calls=%async_computation.1 | async-start | bytes 2097152 | tf_op jit(solution)/shard_map/all_to_all | solution.py:44
  94.0 1.8 constant_dynamic-slice_fusion.2
  95.8 1.7 broadcast_in_dim.48
  97.5 10.0 %while.147 = (s32[]{:T(128)}, bf16[1024,448]{1,0:T(8,128)(2,1)}, bf16[1024,448]{1,0:T(8,128)(2,1)S(1)}, s32[]{:T(128)}, s32[]{:T(128)}, /*index=5*/s32[]{:T(128)}, s32[]{:T(128)}) while((s32[]{:T(128)}, bf16[1024,448]{1,0:T(8,128)(2,1)}, bf16[1024,448]{1,0:T(8,128)(2,1)S(1)}, s32[]{:T(128)}, s32[]{:T(128)}, /*index=5*/s32[]{:T(128)}, ...), condition=%wide.region_3.4_spmd, body=%wide.region_2.3_spmd.sunk | while | flops 6 | bytes 123015 | solution.py:54
  109.5 3.4 %all-to-all-start.2 = ((bf16[8,32,448]{2,1,0:T(8,128)(2,1)}), bf16[8,32,448]{2,1,0:T(8,128)(2,1)S(1)}, u32[]{:S(2)}, u32[]{:S(2)}) async-start(bf16[8,32,448]{2,1,0:T(8,128)(2,1)} %bitcast.19), calls=%async_computation.2 | async-start | bytes 524288 | tf_op jit(solution)/shard_map/all_to_all | solution.py:136
  112.9 9.6 %all-to-all-done.2 = bf16[8,32,448]{2,1,0:T(8,128)(2,1)S(1)} async-done(((bf16[8,32,448]{2,1,0:T(8,128)(2,1)}), bf16[8,32,448]{2,1,0:T(8,128)(2,1)S(1)}, u32[]{:S(2)}, u32[]{:S(2)}) %all-to-all-start.2) | async-done | bytes 229408 | tf_op jit(solution)/shard_map/all_to_all | solution.py:136
  122.6 4.3 %collective-permute-start.6 = (bf16[256,448]{1,0:T(8,128)(2,1)S(1)}, bf16[256,448]{1,0:T(8,128)(2,1)}, u32[]{:S(2)}, u32[]{:S(2)}) collective-permute-start(bf16[256,448]{1,0:T(8,128)(2,1)S(1)} %bitcast.80), channel_id=1, source_target_pairs={{0,256},{16,816},{64,320},{80,880},{128,384},{144,944},{192,448},{... | collective-permute-start | bytes 688136 | tf_op jit(solution)/shard_map/ppermute | solution.py:140
  127.7 16.4 %collective-permute-done.6 = bf16[256,448]{1,0:T(8,128)(2,1)} collective-permute-done((bf16[256,448]{1,0:T(8,128)(2,1)S(1)}, bf16[256,448]{1,0:T(8,128)(2,1)}, u32[]{:S(2)}, u32[]{:S(2)}) %collective-permute-start.6) | collective-permute-done | bytes 229408 | tf_op jit(solution)/shard_map/ppermute | solution.py:140
  144.1 1.9 collective-permute-start.7
  146.0 2.4 %while.154 = (s32[]{:T(128)}, f32[128,448]{0,1:T(8,128)S(1)}, bf16[256,128]{1,0:T(8,128)(2,1)S(1)}, bf16[256,448]{1,0:T(8,128)(2,1)}, s32[]{:T(128)}, /*index=5*/s32[]{:T(128)}, s32[]{:T(128)}, s32[]{:T(128)}) while((s32[]{:T(128)}, f32[128,448]{0,1:T(8,128)S(1)}, bf16[256,128]{1,0:T(8,128)(2,1)S(1)}, bf16[256,448]{1,0:T(8,128)(2,1)}, ...), condition=%wide.region_5.6_spmd.clone, body=%wide.region_4.5_spmd.clone.sunk | while | flops 14794759 | bytes 624276 | solution.py:68
  146.0 1.2 convolution_add_fusion.25
  147.2 1.2 convolution_add_fusion.25
  148.4 3.9 %collective-permute-start.8 = (bf16[4,256,256]{2,1,0:T(8,128)(2,1)S(1)}, bf16[4,256,256]{2,1,0:T(8,128)(2,1)}, u32[]{:S(2)}, u32[]{:S(2)}) collective-permute-start(bf16[4,256,256]{2,1,0:T(8,128)(2,1)S(1)} %get-tuple-element.886), channel_id=1, source_target_pairs={{0,16},{16,0},{1,17},{17,1},{2,18},{18,2},{3,19},{19,3},{4,20},{20... | collective-permute-start | bytes 1572872 | tf_op jit(solution)/shard_map/ppermute | solution.py:157
  152.3 2.4 %while.155 = (s32[]{:T(128)}, f32[128,448]{0,1:T(8,128)S(1)}, bf16[256,128]{1,0:T(8,128)(2,1)S(1)}, bf16[256,448]{1,0:T(8,128)(2,1)}, s32[]{:T(128)}, /*index=5*/s32[]{:T(128)}, s32[]{:T(128)}, s32[]{:T(128)}) while((s32[]{:T(128)}, f32[128,448]{0,1:T(8,128)S(1)}, bf16[256,128]{1,0:T(8,128)(2,1)S(1)}, bf16[256,448]{1,0:T(8,128)(2,1)}, ...), condition=%wide.region_7.8_spmd.clone, body=%wide.region_6.7_spmd.clone.sunk | while | flops 14794759 | bytes 624276 | solution.py:68
  152.3 1.2 convolution_add_fusion.26
  153.5 1.2 convolution_add_fusion.26
  154.8 7.2 %collective-permute-done.7 = bf16[256,448]{1,0:T(8,128)(2,1)} collective-permute-done((bf16[256,448]{1,0:T(8,128)(2,1)}, bf16[256,448]{1,0:T(8,128)(2,1)}, u32[]{:S(2)}, u32[]{:S(2)}) %collective-permute-start.7) | collective-permute-done | bytes 229408 | tf_op jit(solution)/shard_map/ppermute | solution.py:154
  162.0 1.9 collective-permute-start.9
  164.0 2.5 %while.148 = (s32[]{:T(128)}, f32[256,448]{0,1:T(8,128)S(1)}, bf16[256,256]{1,0:T(8,128)(2,1)S(1)}, bf16[256,448]{1,0:T(8,128)(2,1)}, s32[]{:T(128)}, /*index=5*/s32[]{:T(128)}, s32[]{:T(128)}, s32[]{:T(128)}) while((s32[]{:T(128)}, f32[256,448]{0,1:T(8,128)S(1)}, bf16[256,256]{1,0:T(8,128)(2,1)S(1)}, bf16[256,448]{1,0:T(8,128)(2,1)}, ...), condition=%wide.region_9.10_spmd, body=%wide.region_8.9_spmd.sunk | while | flops 29474820 | bytes 1115275 | solution.py:68
  164.0 1.2 convolution_add_fusion.19
  165.2 1.2 convolution_add_fusion.19
  166.5 1.1 slice_bitcast_fusion
  167.6 2.5 %while.156 = (s32[]{:T(128)}, f32[256,448]{0,1:T(8,128)S(1)}, bf16[256,256]{1,0:T(8,128)(2,1)S(1)}, bf16[256,448]{1,0:T(8,128)(2,1)}, s32[]{:T(128)}, /*index=5*/s32[]{:T(128)}, s32[]{:T(128)}, s32[]{:T(128)}) while((s32[]{:T(128)}, f32[256,448]{0,1:T(8,128)S(1)}, bf16[256,256]{1,0:T(8,128)(2,1)S(1)}, ...), condition=%wide.region_11.12_spmd.clone, body=%wide.region_10.11_spmd.clone.sunk | while | flops 29589512 | bytes 1115796 | solution.py:68
  167.6 1.2 convolution_add_fusion.27
  168.9 1.2 convolution_add_fusion.27
  170.2 1.9 collective-permute-start.11
  172.1 2.6 %while.149 = (s32[]{:T(128)}, f32[256,448]{0,1:T(8,128)S(1)}, bf16[256,256]{1,0:T(8,128)(2,1)S(1)}, bf16[256,448]{1,0:T(8,128)(2,1)}, s32[]{:T(128)}, /*index=5*/s32[]{:T(128)}, s32[]{:T(128)}, s32[]{:T(128)}) while((s32[]{:T(128)}, f32[256,448]{0,1:T(8,128)S(1)}, bf16[256,256]{1,0:T(8,128)(2,1)S(1)}, bf16[256,448]{1,0:T(8,128)(2,1)}, ...), condition=%wide.region_13.14_spmd, body=%wide.region_12.13_spmd.sunk | while | flops 29474820 | bytes 1115275 | solution.py:68
  172.1 1.3 convolution_add_fusion.20
  173.5 1.2 convolution_add_fusion.20
  174.7 1.5 collective-permute-done.9
  176.2 5.5 %collective-permute-start.10 = (bf16[256,448]{1,0:T(8,128)(2,1)}, bf16[256,448]{1,0:T(8,128)(2,1)S(1)}, u32[]{:S(2)}, u32[]{:S(2)}) collective-permute-start(bf16[256,448]{1,0:T(8,128)(2,1)} %collective-permute-done.9), channel_id=1, source_target_pairs={{0,256},{16,816},{64,320},{80,880},{128,384},{144,944},{192,448},{... | collective-permute-start | bytes 688136 | tf_op jit(solution)/shard_map/ppermute | solution.py:179
  181.7 1.0 broadcast_select_fusion.3
  183.6 1.3 reverse_select_fusion
  184.9 7.5 %all-to-all-start.3 = ((bf16[16,4,8,1024]{3,2,1,0:T(8,128)(2,1)}), bf16[16,4,8,1024]{3,2,1,0:T(8,128)(2,1)S(1)}, u32[]{:S(2)}, u32[]{:S(2)}) async-start(bf16[16,4,8,1024]{3,2,1,0:T(8,128)(2,1)} %bitcast.35), calls=%async_computation.3 | async-start | bytes 2097152 | tf_op jit(solution)/shard_map/all_to_all | solution.py:181
  192.4 2.5 %while.150 = (s32[]{:T(128)}, f32[256,448]{0,1:T(8,128)S(1)}, bf16[256,256]{1,0:T(8,128)(2,1)S(1)}, bf16[256,448]{1,0:T(8,128)(2,1)}, s32[]{:T(128)}, /*index=5*/s32[]{:T(128)}, s32[]{:T(128)}, s32[]{:T(128)}) while((s32[]{:T(128)}, f32[256,448]{0,1:T(8,128)S(1)}, bf16[256,256]{1,0:T(8,128)(2,1)S(1)}, bf16[256,448]{1,0:T(8,128)(2,1)}, ...), condition=%wide.region_15.16_spmd, body=%wide.region_14.15_spmd.sunk | while | flops 29474820 | bytes 1115275 | solution.py:68
  192.4 1.2 convolution_add_fusion.21
  193.6 1.2 convolution_add_fusion.21
  194.9 2.5 %while.151 = (s32[]{:T(128)}, f32[256,448]{0,1:T(8,128)S(1)}, bf16[256,256]{1,0:T(8,128)(2,1)S(1)}, bf16[256,448]{1,0:T(8,128)(2,1)}, s32[]{:T(128)}, /*index=5*/s32[]{:T(128)}, s32[]{:T(128)}, s32[]{:T(128)}) while((s32[]{:T(128)}, f32[256,448]{0,1:T(8,128)S(1)}, bf16[256,256]{1,0:T(8,128)(2,1)S(1)}, bf16[256,448]{1,0:T(8,128)(2,1)}, ...), condition=%wide.region_17.18_spmd, body=%wide.region_16.17_spmd.sunk | while | flops 29474820 | bytes 1115275 | solution.py:68
  194.9 1.2 convolution_add_fusion.22
  196.1 1.2 convolution_add_fusion.22
  197.4 11.7 %all-to-all-done.3 = bf16[16,4,8,1024]{3,2,1,0:T(8,128)(2,1)S(1)} async-done(((bf16[16,4,8,1024]{3,2,1,0:T(8,128)(2,1)}), bf16[16,4,8,1024]{3,2,1,0:T(8,128)(2,1)S(1)}, u32[]{:S(2)}, u32[]{:S(2)}) %all-to-all-start.3) | async-done | bytes 1048608 | tf_op jit(solution)/shard_map/all_to_all | solution.py:181
  210.0 3.3 %all-to-all-start.4 = ((f32[4,8,1024]{2,1,0:T(8,128)}), f32[4,8,1024]{2,1,0:T(8,128)S(1)}, u32[]{:S(2)}, u32[]{:S(2)}) async-start(f32[4,8,1024]{2,1,0:T(8,128)} %convert_reduce_fusion), calls=%async_computation.4 | async-start | bytes 262144 | tf_op jit(solution)/shard_map/all_to_all | solution.py:188
  214.2 1.9 collective-permute-start.12
  217.0 1.0 collective-permute-done.12
  219.3 4.5 %all-to-all-start.5 = ((bf16[4,64,448]{2,1,0:T(8,128)(2,1)}), bf16[4,64,448]{2,1,0:T(8,128)(2,1)S(1)}, u32[]{:S(2)}, u32[]{:S(2)}) async-start(bf16[4,64,448]{2,1,0:T(8,128)(2,1)} %bitcast.38), calls=%async_computation.5 | async-start | bytes 524288 | tf_op jit(solution)/shard_map/all_to_all | solution.py:193
  224.6 9.2 %collective-permute-start.13 = (bf16[8,1024]{1,0:T(8,128)(2,1)S(1)}, bf16[8,1024]{1,0:T(8,128)(2,1)S(1)}, u32[]{:S(2)}, u32[]{:S(2)}) collective-permute-start(bf16[8,1024]{1,0:T(8,128)(2,1)S(1)} %reduce_sum.19), channel_id=1, source_target_pairs={{0,512},{256,768},{512,0},{768,256},{1,513},{257,769},{513,1},{769... | collective-permute-start | bytes 49160 | tf_op jit(solution)/shard_map/ppermute | solution.py:191
  233.9 5.2 %collective-permute-done.13 = bf16[8,1024]{1,0:T(8,128)(2,1)S(1)} collective-permute-done((bf16[8,1024]{1,0:T(8,128)(2,1)S(1)}, bf16[8,1024]{1,0:T(8,128)(2,1)S(1)}, u32[]{:S(2)}, u32[]{:S(2)}) %collective-permute-start.13) | collective-permute-done | bytes 16416 | tf_op jit(solution)/shard_map/ppermute | solution.py:191
  (95 shorter events, 26.7 us)
Async XLA Ops:
  2.1 47.3 %all-to-all-start = ((bf16[16,8,1024]{2,1,0:T(8,128)(2,1)}), bf16[16,8,1024]{2,1,0:T(8,128)(2,1)S(1)}, u32[]{:S(2)}, u32[]{:S(2)}) async-start(bf16[16,8,1024]{2,1,0:T(8,128)(2,1)} %broadcast_in_dim.43), calls=%async_computation | async-start | bytes 524288 | tf_op jit(solution)/shard_map/all_to_all | solution.py:44
  19.3 14.2 %collective-permute-start.1 = (bf16[2,1,8,256]{3,2,0,1:T(8,128)(2,1)S(1)}, bf16[2,1,8,256]{3,2,0,1:T(8,128)(2,1)S(1)}, u32[]{:S(2)}, u32[]{:S(2)}) collective-permute-start(bf16[2,1,8,256]{3,2,0,1:T(8,128)(2,1)S(1)} %select_bitcast_fusion), channel_id=1, source_target_pairs={{0,512},{256,768},{512,0},{768,256},{1,513},{257,769},{513,1},{769... | collective-permute-start | bytes 24584 | tf_op jit(solution)/shard_map/ppermute | solution.py:78
  34.3 9.5 %collective-permute-start.2 = (bf16[1,2,8,256]{3,2,0,1:T(8,128)(2,1)S(1)}, bf16[1,2,8,256]{3,2,0,1:T(8,128)(2,1)S(1)}, u32[]{:S(2)}, u32[]{:S(2)}) collective-permute-start(bf16[1,2,8,256]{3,2,0,1:T(8,128)(2,1)S(1)} %broadcast_select_fusion.10), channel_id=1, source_target_pairs={{0,256},{256,0},{512,768},{768,512},{1,257},{257,1},{513,769},{769... | collective-permute-start | bytes 24584 | tf_op jit(solution)/shard_map/ppermute | solution.py:78
  43.8 5.6 %collective-permute-start.3 = (bf16[4,1,8,256]{3,2,1,0:T(8,128)(2,1)S(1)}, bf16[4,1,8,256]{3,2,1,0:T(8,128)(2,1)S(1)}, u32[]{:S(2)}, u32[]{:S(2)}) collective-permute-start(bf16[4,1,8,256]{3,2,1,0:T(8,128)(2,1)S(1)} %bitcast.90), channel_id=1, source_target_pairs={{0,64},{64,0},{128,192},{192,128},{1,65},{65,1},{129,193},{193,129... | collective-permute-start | bytes 49160 | tf_op jit(solution)/shard_map/ppermute | solution.py:86
  52.3 9.1 %collective-permute-start = (f32[64,1792]{1,0:T(8,128)S(1)}, f32[64,1792]{1,0:T(8,128)S(1)}, u32[]{:S(2)}, u32[]{:S(2)}) collective-permute-start(f32[64,1792]{1,0:T(8,128)S(1)} %fusion.44), channel_id=1, source_target_pairs={{0,16},{16,0},{1,17},{17,1},{2,18},{18,2},{3,19},{19,3},{4,20},{20... | collective-permute-start | bytes 1376264 | tf_op jit(solution)/shard_map/ppermute | solution.py:115
  54.3 7.1 %collective-permute-start.4 = (bf16[4,2,8,256]{3,2,1,0:T(8,128)(2,1)S(1)}, bf16[4,2,8,256]{3,2,1,0:T(8,128)(2,1)S(1)}, u32[]{:S(2)}, u32[]{:S(2)}) collective-permute-start(bf16[4,2,8,256]{3,2,1,0:T(8,128)(2,1)S(1)} %pad_maximum_fusion.5), channel_id=1, source_target_pairs={{0,128},{64,192},{128,0},{192,64},{1,129},{65,193},{129,1},{193,65... | collective-permute-start | bytes 98312 | tf_op jit(solution)/shard_map/ppermute | solution.py:86
  64.8 42.7 %collective-permute-start.5 = (bf16[32,1792]{1,0:T(8,128)(2,1)S(1)}, bf16[32,1792]{1,0:T(8,128)(2,1)S(1)}, u32[]{:S(2)}, u32[]{:S(2)}) collective-permute-start(bf16[32,1792]{1,0:T(8,128)(2,1)S(1)} %slice.107), channel_id=1, source_target_pairs={{0,32},{32,0},{1,33},{33,1},{2,34},{34,2},{3,35},{35,3},{4,36},{36... | collective-permute-start | bytes 344072 | tf_op jit(solution)/shard_map/ppermute | solution.py:119
  86.8 21.0 %all-to-all-start.1 = ((bf16[16,16,8,256]{3,2,1,0:T(8,128)(2,1)}), bf16[16,16,8,256]{3,2,1,0:T(8,128)(2,1)S(1)}, u32[]{:S(2)}, u32[]{:S(2)}) async-start(bf16[16,16,8,256]{3,2,1,0:T(8,128)(2,1)} %broadcast_in_dim.47), calls=%async_computation.1 | async-start | bytes 2097152 | tf_op jit(solution)/shard_map/all_to_all | solution.py:44
  94.0 13.8 %copy-start.1 = (bf16[32,896]{1,0:T(8,128)(2,1)S(1)}, bf16[32,896]{1,0:T(8,128)(2,1)}, u32[]{:S(2)}) copy-start(bf16[32,896]{1,0:T(8,128)(2,1)} %param.33) | copy-start | bytes 172036
  109.5 13.1 %all-to-all-start.2 = ((bf16[8,32,448]{2,1,0:T(8,128)(2,1)}), bf16[8,32,448]{2,1,0:T(8,128)(2,1)S(1)}, u32[]{:S(2)}, u32[]{:S(2)}) async-start(bf16[8,32,448]{2,1,0:T(8,128)(2,1)} %bitcast.19), calls=%async_computation.2 | async-start | bytes 524288 | tf_op jit(solution)/shard_map/all_to_all | solution.py:136
  122.6 21.5 %collective-permute-start.6 = (bf16[256,448]{1,0:T(8,128)(2,1)S(1)}, bf16[256,448]{1,0:T(8,128)(2,1)}, u32[]{:S(2)}, u32[]{:S(2)}) collective-permute-start(bf16[256,448]{1,0:T(8,128)(2,1)S(1)} %bitcast.80), channel_id=1, source_target_pairs={{0,256},{16,816},{64,320},{80,880},{128,384},{144,944},{192,448},{... | collective-permute-start | bytes 688136 | tf_op jit(solution)/shard_map/ppermute | solution.py:140
  144.1 17.9 %collective-permute-start.7 = (bf16[256,448]{1,0:T(8,128)(2,1)}, bf16[256,448]{1,0:T(8,128)(2,1)}, u32[]{:S(2)}, u32[]{:S(2)}) collective-permute-start(bf16[256,448]{1,0:T(8,128)(2,1)} %collective-permute-done.6), channel_id=1, source_target_pairs={{0,256},{16,816},{64,320},{80,880},{128,384},{144,944},{192,448},{... | collective-permute-start | bytes 688136 | tf_op jit(solution)/shard_map/ppermute | solution.py:154
  148.4 13.6 %collective-permute-start.8 = (bf16[4,256,256]{2,1,0:T(8,128)(2,1)S(1)}, bf16[4,256,256]{2,1,0:T(8,128)(2,1)}, u32[]{:S(2)}, u32[]{:S(2)}) collective-permute-start(bf16[4,256,256]{2,1,0:T(8,128)(2,1)S(1)} %get-tuple-element.886), channel_id=1, source_target_pairs={{0,16},{16,0},{1,17},{17,1},{2,18},{18,2},{3,19},{19,3},{4,20},{20... | collective-permute-start | bytes 1572872 | tf_op jit(solution)/shard_map/ppermute | solution.py:157
  162.0 14.2 %collective-permute-start.9 = (bf16[256,448]{1,0:T(8,128)(2,1)}, bf16[256,448]{1,0:T(8,128)(2,1)}, u32[]{:S(2)}, u32[]{:S(2)}) collective-permute-start(bf16[256,448]{1,0:T(8,128)(2,1)} %collective-permute-done.7), channel_id=1, source_target_pairs={{0,256},{16,816},{64,320},{80,880},{128,384},{144,944},{192,448},{... | collective-permute-start | bytes 688136 | tf_op jit(solution)/shard_map/ppermute | solution.py:162
  170.2 11.5 %collective-permute-start.11 = (bf16[256,448]{1,0:T(8,128)(2,1)}, bf16[256,448]{1,0:T(8,128)(2,1)}, u32[]{:S(2)}, u32[]{:S(2)}) collective-permute-start(bf16[256,448]{1,0:T(8,128)(2,1)} %collective-permute-done.7), channel_id=1, source_target_pairs={{0,16},{16,0},{1,17},{17,1},{2,18},{18,2},{3,19},{19,3},{4,20},{20... | collective-permute-start | bytes 688136 | tf_op jit(solution)/shard_map/ppermute | solution.py:165
  172.1 10.6 %copy-start = (bf16[1024,448]{1,0:T(8,128)(2,1)S(1)}, bf16[1024,448]{1,0:T(8,128)(2,1)}, u32[]{:S(2)}) copy-start(bf16[1024,448]{1,0:T(8,128)(2,1)} %get-tuple-element.901) | copy-start | bytes 2752516
  176.2 21.2 %collective-permute-start.10 = (bf16[256,448]{1,0:T(8,128)(2,1)}, bf16[256,448]{1,0:T(8,128)(2,1)S(1)}, u32[]{:S(2)}, u32[]{:S(2)}) collective-permute-start(bf16[256,448]{1,0:T(8,128)(2,1)} %collective-permute-done.9), channel_id=1, source_target_pairs={{0,256},{16,816},{64,320},{80,880},{128,384},{144,944},{192,448},{... | collective-permute-start | bytes 688136 | tf_op jit(solution)/shard_map/ppermute | solution.py:179
  184.9 24.2 %all-to-all-start.3 = ((bf16[16,4,8,1024]{3,2,1,0:T(8,128)(2,1)}), bf16[16,4,8,1024]{3,2,1,0:T(8,128)(2,1)S(1)}, u32[]{:S(2)}, u32[]{:S(2)}) async-start(bf16[16,4,8,1024]{3,2,1,0:T(8,128)(2,1)} %bitcast.35), calls=%async_computation.3 | async-start | bytes 2097152 | tf_op jit(solution)/shard_map/all_to_all | solution.py:181
  210.0 9.4 %all-to-all-start.4 = ((f32[4,8,1024]{2,1,0:T(8,128)}), f32[4,8,1024]{2,1,0:T(8,128)S(1)}, u32[]{:S(2)}, u32[]{:S(2)}) async-start(f32[4,8,1024]{2,1,0:T(8,128)} %convert_reduce_fusion), calls=%async_computation.4 | async-start | bytes 262144 | tf_op jit(solution)/shard_map/all_to_all | solution.py:188
  214.2 3.8 %collective-permute-start.12 = (f32[256,448]{1,0:T(8,128)S(1)}, f32[256,448]{1,0:T(8,128)S(1)}, u32[]{:S(2)}, u32[]{:S(2)}) collective-permute-start(f32[256,448]{1,0:T(8,128)S(1)} %copy.42), channel_id=1, source_target_pairs={{0,16},{16,0},{1,17},{17,1},{2,18},{18,2},{3,19},{19,3},{4,20},{20... | collective-permute-start | bytes 1376264 | tf_op jit(solution)/shard_map/ppermute | solution.py:186
  219.3 20.4 %all-to-all-start.5 = ((bf16[4,64,448]{2,1,0:T(8,128)(2,1)}), bf16[4,64,448]{2,1,0:T(8,128)(2,1)S(1)}, u32[]{:S(2)}, u32[]{:S(2)}) async-start(bf16[4,64,448]{2,1,0:T(8,128)(2,1)} %bitcast.38), calls=%async_computation.5 | async-start | bytes 524288 | tf_op jit(solution)/shard_map/all_to_all | solution.py:193
  224.6 14.5 %collective-permute-start.13 = (bf16[8,1024]{1,0:T(8,128)(2,1)S(1)}, bf16[8,1024]{1,0:T(8,128)(2,1)S(1)}, u32[]{:S(2)}, u32[]{:S(2)}) collective-permute-start(bf16[8,1024]{1,0:T(8,128)(2,1)S(1)} %reduce_sum.19), channel_id=1, source_target_pairs={{0,512},{256,768},{512,0},{768,256},{1,513},{257,769},{513,1},{769... | collective-permute-start | bytes 49160 | tf_op jit(solution)/shard_map/ppermute | solution.py:191

commit v4 on v3

--- a/solution.py
+++ b/solution.py
@@ -7,9 +7,12 @@
 F32 = jnp.float32
 
 TEAM = 4
+TURNS = 16
+TURNS0 = 8
 GROUPS = 16 // TEAM
 PLACES = 2 * GROUPS
 STEPS = PLACES // 2
+DP = ("group", "member")
 Z = ("group", "member", "half", "core")
 
 
@@ -66,27 +69,6 @@
         )
 
     return lax.fori_loop(0, turns, turn, total)
-
-
-def spread_over_dp(x, group, member):
-    blocks, held, block = x.shape
-    x = x.reshape(blocks, 1, held, block)
-    bit = blocks // 2
-    while bit:
-        up = (group & bit) != 0
-        low, high = x[:bit], x[bit:]
-        theirs = lax.ppermute(jnp.where(up, low, high), "group", [(i, i ^ bit) for i in range(GROUPS)])
-        x = ordered(~up, jnp.where(up, high, low), theirs, axis=1)
-        bit //= 2
-    bits = GROUPS.bit_length() - 1
-    x = x.reshape(*(2,) * bits, held, block).transpose(*range(bits - 1, -1, -1), bits, bits + 1)
-    x = x.reshape(GROUPS, 1, held, block)
-    bit = 1
-    while bit < TEAM:
-        theirs = lax.ppermute(x, "member", [(i, i ^ bit) for i in range(TEAM)])
-        x = ordered((member & bit) == 0, x, theirs, axis=1)
-        bit *= 2
-    return x.reshape(16, held, block)
 
 
 def body(tokens, gate_weight, up_weight, mask_gate, mask_up, grad_hidden):
@@ -102,7 +84,7 @@
     replica = gather_col(tokens, columns).reshape(2, 2, columns // 4 * held, features)
 
     spread = tokens.reshape(held, GROUPS, block).transpose(1, 0, 2)
-    spread = spread_over_dp(spread, group, member)
+    spread = jnp.broadcast_to(spread[:, None], (GROUPS, TEAM, held, block)).reshape(16, held, block)
 
     both_weights = jnp.concatenate([masked(gate_weight, mask_gate), masked(up_weight, mask_up)], axis=1)
     replica = jnp.where(half == 0, replica, replica[::-1])
@@ -117,10 +99,10 @@
     summed, spread, both_weights = lax.optimization_barrier((summed, spread, both_weights))
 
     arrived = lax.ppermute(summed[rows:].astype(BF16), "half", SWAP)
-    spread = in_turns(spread, summed[:1, :1])
-    everyone = gather_col(spread, columns)
-    masked_share = in_turns(lax.dynamic_slice_in_dim(both_weights, member * share, share, axis=1), summed[:1, :1], 16)
-    arrived, everyone, masked_share = lax.optimization_barrier((arrived, everyone, masked_share))
+    spread = lax.all_to_all(in_turns(spread, summed[:1, :1], 16), DP, 0, 0)
+    chosen = lax.dynamic_slice_in_dim(both_weights, member * share, share, axis=1)
+    masked_share = in_turns(chosen, summed[:1, :1], TURNS0)
+    arrived, spread, masked_share = lax.optimization_barrier((arrived, spread, masked_share))
     proj = summed[:rows] + arrived.astype(F32)
     gate_proj, up_proj = proj[:, :units], proj[:, units:]
 
@@ -135,9 +117,13 @@
     shares = jnp.broadcast_to(shares[:, None], (TEAM, 2, rows, share)).reshape(2 * TEAM, rows, share)
     own = lax.all_to_all(shares, ("member", "core"), 0, 0).reshape(TEAM, 2, rows, share)
     own = own.transpose(1, 0, 2, 3).reshape(2 * TEAM * rows, share)
-    own, everyone = lax.optimization_barrier((own, everyone))
+    own, spread = lax.optimization_barrier((own, spread))
 
     first = lax.ppermute(own, Z, RING)
+    everyone = gather_col(in_turns(spread, own[:1, :1]), columns)
+    own = in_turns(own, own[:1, :1], TURNS)
+    first, everyone, own = lax.optimization_barrier((first, everyone, own))
+
     everyone = everyone.reshape(2, 2, columns // 4, GROUPS, TEAM, held, block)
     everyone = everyone.transpose(0, 3, 1, 4, 2, 5, 6).reshape(PLACES, 2 * TEAM * rows, block)
     twice = jnp.concatenate([everyone, everyone], axis=0)
@@ -145,7 +131,6 @@
     after = lax.dynamic_slice_in_dim(twice, place, STEPS, axis=0)
     after = jnp.concatenate([after[1:], after[:1]], axis=0)
     my_rows, their_rows = jnp.where(core == 0, before, after), jnp.where(core == 0, after, before)
-    first, my_rows, their_rows = lax.optimization_barrier((first, my_rows, their_rows))
 
     def add(step, tokens_of, met, *total):
         start = total[0] if total else jnp.zeros((tokens_of.shape[2], share), F32)
@@ -161,9 +146,8 @@
 
     third = lax.ppermute(second, Z, RING)
     my_total = add(1, my_rows, second, my_total)
-    my_total, passing = lax.optimization_barrier((my_total, second))
-    across = lax.ppermute(passing, "core", SWAP)
-    far = jnp.where((group < PLACES // 4) == (core == 0), passing, across)
+    across = lax.ppermute(second, "core", SWAP)
+    far = jnp.where((group < PLACES // 4) == (core == 0), second, across)
     part = lax.dot_general(
         jnp.concatenate([own, far], axis=0),
         masked_share,
@@ -173,12 +157,13 @@
     part = part.reshape(2, 2, TEAM, columns // 4, held, features)
     part = jnp.where(half == 0, part, part[::-1]).transpose(0, 1, 3, 2, 4, 5)
     part = part.reshape(columns, TEAM, held, features)
+    part, their_rows = lax.optimization_barrier((part, their_rows))
+    part = lax.all_to_all(part, "col", 0, 0)
     their_total = add(1, their_rows, second, add(0, their_rows, first))
     third, my_total, their_total = lax.optimization_barrier((third, my_total, their_total))
 
     fourth = lax.ppermute(third, Z, RING)
     my_total = add(2, my_rows, third, my_total)
-    part = lax.all_to_all(part, "col", 0, 0)
     their_total = add(2, their_rows, third, their_total)
     fourth, my_total, their_total, part = lax.optimization_barrier((fourth, my_total, their_total, part))
 
@@ -187,8 +172,8 @@
     reduced = jnp.sum(part.astype(F32), axis=0)
     reduced = jnp.sum(lax.all_to_all(reduced, "member", 0, 0), axis=0).astype(BF16)
     full = add(3, my_rows, last, my_total) + got
-    full, reduced = lax.optimization_barrier((full, reduced))
     swapped = lax.ppermute(reduced, "group", FAR_GROUP)
+    full, swapped = lax.optimization_barrier((full, swapped))
     grad_tokens = jnp.where((col < columns // 2) == (half == 0), reduced, swapped)
     traded = lax.all_to_all(full.astype(BF16).reshape(TEAM, block // TEAM, share), "member", 0, 0)
     grads = traded.transpose(1, 0, 2).reshape(block // TEAM, 2 * units).astype(F32)

time: 245 us -> 239 us (0.976)
  starting transfers between devices: 109 us -> 102 us
  waiting for transfers between devices: 70 us -> 66 us
  local copies, waits for them, and re-layouts: 21.3 us -> 25.1 us
    all_to_all x0 -> x1, waiting for transfers between devices: none -> 17.3 us  [body(): spread = lax.all_to_all(in_turns(spread, summed[:1, :1], 16), DP, 0, 0)]
    ppermute x5 -> x1, waiting for transfers between devices: 16.6 us -> 0.01 us  [body(): across = lax.ppermute(second, 'core', SWAP)]
    ppermute x1, waiting for transfers between devices: 16.4 us -> 0.01 us  [body(): first = lax.ppermute(own, Z, RING)]
    ppermute x5 -> x1, starting transfers between devices: 15.5 us -> 1.91 us  [body(): across = lax.ppermute(second, 'core', SWAP)]
    all_to_all x0 -> x1, starting transfers between devices: none -> 8.78 us  [body(): spread = lax.all_to_all(in_turns(spread, summed[:1, :1], 16), DP, 0, 0)]
    ppermute x1, starting transfers between devices: 1.91 us -> 7.4 us  [body(): third = lax.ppermute(second, Z, RING)]
    all_to_all x1, waiting for transfers between devices: 0.01 us -> 5.24 us  [body(): lax.all_to_all(full.astype(BF16).reshape(TEAM, block // TEAM, share), 'me...]
    all_to_all x2, waiting for transfers between devices: 0.27 us -> 4.91 us  [gather_col(): lax.all_to_all(jnp.broadcast_to(x[None], (count, *x.shape)), 'col', 0, 0)]
  transfers between devices with their start and end apart: 20 -> 17, of which waited for: 13 -> 10; matrix products, arithmetic and copies ran while one was open for 20% -> 21% of each run, Pallas kernels for 0% -> 0%
where the time goes in v4:
time: 239 us; the launch traced here: 235 us
  starting transfers between devices  102 us (43%)
  waiting for transfers between devices  66 us (28%)
  matrix products  25.6 us (11%)
  local copies, waits for them, and re-layouts  25.1 us (11%)
  other arithmetic  14.2 us (6%)
    all_to_all x2, starting transfers between devices, gather_col(): lax.all_to_all(jnp.broadcast_to(x[None], (count, *x.shape)), 'col', 0, 0)  23.6 us
    ppermute x1, starting transfers between devices, body(): arrived = lax.ppermute(summed[rows:].astype(BF16), 'half', SWAP)  19.9 us
    dot_general x18, matrix products, turn(): lax.dot_general(lax.dynamic_slice_in_dim(rows, i * part, part, axis=0), l...  18.3 us
    all_to_all x1, waiting for transfers between devices, body(): spread = lax.all_to_all(in_turns(spread, summed[:1, :1], 16), DP, 0, 0)  17.3 us
    all_to_all x1, waiting for transfers between devices, body(): part = lax.all_to_all(part, 'col', 0, 0)  12 us
    dynamic_update_slice x26, local copies, waits for them, and re-layouts, turn(): return lax.dynamic_update_slice_in_dim(y, piece, i * part, axis=0)  11.7 us
    all_to_all x1, waiting for transfers between devices, body(): lax.all_to_all(shares, ('member', 'core'), 0, 0)  9.61 us
    all_to_all x1, starting transfers between devices, body(): spread = lax.all_to_all(in_turns(spread, summed[:1, :1], 16), DP, 0, 0)  8.78 us
  transfers between devices with their start and end apart: 17, of which 10 were waited for; matrix products, arithmetic and copies ran while one was open for 21% of the time, Pallas kernels for 0%

profile of v4, /device:TPU:6, one launch (start us, length us, event | category | flops | bytes accessed | tf_op | source)
XLA Modules:
  0.0 235.3 jit_solution(14504516058247071538)
XLA Ops:
  0.6 1.4 broadcast_in_dim.55
  2.1 16.5 %all-to-all-start = ((bf16[16,8,1024]{2,1,0:T(8,128)(2,1)}), bf16[16,8,1024]{2,1,0:T(8,128)(2,1)S(1)}, u32[]{:S(2)}, u32[]{:S(2)}) async-start(bf16[16,8,1024]{2,1,0:T(8,128)(2,1)} %broadcast_in_dim.55), calls=%async_computation | async-start | bytes 524288 | tf_op jit(solution)/shard_map/all_to_all | solution.py:47
  20.3 2.4 %bitcast_multiply_fusion = (bf16[1024,896]{1,0:T(8,128)(2,1)S(1)}, bf16[1024,896]{1,0:T(8,128)(2,1)S(1)}) fusion(bf16[1024,896]{1,0:T(8,128)(2,1)} %param.34, bf16[8,896]{1,0:T(8,128)(2,1)S(1)} %broadcast_bitcast_fusion, bf16[1024,896]{1,0:T(8,128)(2,1)} %param.33, bf16[8,896]{1,0:T(8,128)(2,1)S(1)} %broadcast_bitcast_fusion.1), kind=kLoop, calls=%fused_computation.46 | loop fusion | flops 1835008 | bytes 7368704 | tf_op jit(solution)/shard_map/mul | solution.py:43
  22.8 2.1 pad_maximum_fusion
  25.1 2.8 %fusion.43 = f32[64,1792]{1,0:T(8,128)S(1)} fusion(bf16[64,1024]{1,0:T(8,128)(2,1)S(1)} %bitcast.71, bf16[1024,1792]{1,0:T(8,128)(2,1)} %pad_maximum_fusion), kind=kOutput, calls=%fused_computation.100 | convolution fusion | flops 234881024 | bytes 4259840 | tf_op jit(solution)/shard_map/dot_general | solution.py:95
  27.9 1.9 collective-permute-start
  29.8 1.8 collective-permute-done
  31.6 2.8 %convolution_add_fusion.9 = f32[64,1792]{1,0:T(8,128)S(1)} fusion(f32[64,1792]{1,0:T(8,128)S(1)} %collective-permute-done, bf16[64,1024]{1,0:T(8,128)(2,1)S(1)} %bitcast.70, bf16[1024,1792]{1,0:T(8,128)(2,1)} %pad_maximum_fusion), kind=kOutput, calls=%fused_computation.44 | convolution fusion | flops 234995712 | bytes 4718592 | tf_op jit(solution)/shard_map/dot_general | solution.py:95
  35.6 19.9 %collective-permute-start.1 = (bf16[32,1792]{1,0:T(8,128)(2,1)S(1)}, bf16[32,1792]{1,0:T(8,128)(2,1)S(1)}, u32[]{:S(2)}, u32[]{:S(2)}) collective-permute-start(bf16[32,1792]{1,0:T(8,128)(2,1)S(1)} %slice.90), channel_id=1, source_target_pairs={{0,32},{32,0},{1,33},{33,1},{2,34},{34,2},{3,35},{35,3},{4,36},{36... | collective-permute-start | bytes 344072 | tf_op jit(solution)/shard_map/ppermute | solution.py:101
  55.5 8.8 %all-to-all-start.1 = ((bf16[16,8,256]{2,1,0:T(8,128)(2,1)}), bf16[16,8,256]{2,1,0:T(8,128)(2,1)S(1)}, u32[]{:S(2)}, u32[]{:S(2)}) async-start(bf16[16,8,256]{2,1,0:T(8,128)(2,1)} %bitcast.9), calls=%async_computation.1 | async-start | bytes 131072 | tf_op jit(solution)/shard_map/all_to_all | solution.py:102
  64.3 1.8 constant_dynamic-slice_fusion.2
  67.2 17.3 %all-to-all-done.1 = bf16[16,8,256]{2,1,0:T(8,128)(2,1)S(1)} async-done(((bf16[16,8,256]{2,1,0:T(8,128)(2,1)}), bf16[16,8,256]{2,1,0:T(8,128)(2,1)S(1)}, u32[]{:S(2)}, u32[]{:S(2)}) %all-to-all-start.1) | async-done | bytes 65568 | tf_op jit(solution)/shard_map/all_to_all | solution.py:102
  86.2 3.4 %all-to-all-start.2 = ((bf16[8,32,448]{2,1,0:T(8,128)(2,1)}), bf16[8,32,448]{2,1,0:T(8,128)(2,1)S(1)}, u32[]{:S(2)}, u32[]{:S(2)}) async-start(bf16[8,32,448]{2,1,0:T(8,128)(2,1)} %bitcast.12), calls=%async_computation.2 | async-start | bytes 524288 | tf_op jit(solution)/shard_map/all_to_all | solution.py:118
  89.7 9.6 %all-to-all-done.2 = bf16[8,32,448]{2,1,0:T(8,128)(2,1)S(1)} async-done(((bf16[8,32,448]{2,1,0:T(8,128)(2,1)}), bf16[8,32,448]{2,1,0:T(8,128)(2,1)S(1)}, u32[]{:S(2)}, u32[]{:S(2)}) %all-to-all-start.2) | async-done | bytes 229408 | tf_op jit(solution)/shard_map/all_to_all | solution.py:118
  100.0 1.1 slice.74
  101.2 2.5 %collective-permute-start.2 = (bf16[256,448]{1,0:T(8,128)(2,1)}, bf16[256,448]{1,0:T(8,128)(2,1)}, u32[]{:S(2)}, u32[]{:S(2)}) collective-permute-start(bf16[256,448]{1,0:T(8,128)(2,1)} %bitcast.15), channel_id=1, source_target_pairs={{0,256},{16,816},{64,320},{80,880},{128,384},{144,944},{192,448},{... | collective-permute-start | bytes 688136 | tf_op jit(solution)/shard_map/ppermute | solution.py:122
  104.5 1.1 broadcast_in_dim.63
  105.5 7.0 %all-to-all-start.3 = ((bf16[16,16,8,256]{3,2,1,0:T(8,128)(2,1)}), bf16[16,16,8,256]{3,2,1,0:T(8,128)(2,1)S(1)}, u32[]{:S(2)}, u32[]{:S(2)}) async-start(bf16[16,16,8,256]{3,2,1,0:T(8,128)(2,1)} %broadcast_in_dim.63), calls=%async_computation.3 | async-start | bytes 2097152 | tf_op jit(solution)/shard_map/all_to_all | solution.py:47
  113.3 11.5 %while.174 = (s32[]{:T(128)}, bf16[256,448]{1,0:T(8,128)(2,1)S(1)}, bf16[256,448]{1,0:T(8,128)(2,1)}, s32[]{:T(128)}, s32[]{:T(128)}, /*index=5*/s32[]{:T(128)}, s32[]{:T(128)}) while((s32[]{:T(128)}, bf16[256,448]{1,0:T(8,128)(2,1)S(1)}, bf16[256,448]{1,0:T(8,128)(2,1)}, s32[]{:T(128)}, s32[]{:T(128)}, /*index=5*/s32[]{:T(128)}, ...), condition=%wide.region_7.8_spmd, body=%wide.region_6.7_spmd.sunk | while | flops 6 | bytes 30847 | solution.py:57
  124.8 4.7 %all-to-all-done.3 = bf16[16,16,8,256]{3,2,1,0:T(8,128)(2,1)S(1)} async-done(((bf16[16,16,8,256]{3,2,1,0:T(8,128)(2,1)}), bf16[16,16,8,256]{3,2,1,0:T(8,128)(2,1)S(1)}, u32[]{:S(2)}, u32[]{:S(2)}) %all-to-all-start.3) | async-done | bytes 1048608 | tf_op jit(solution)/shard_map/all_to_all | solution.py:47
  130.1 1.0 broadcast_select_fusion
  131.2 4.8 %collective-permute-start.3 = (bf16[256,448]{1,0:T(8,128)(2,1)}, bf16[256,448]{1,0:T(8,128)(2,1)}, u32[]{:S(2)}, u32[]{:S(2)}) collective-permute-start(bf16[256,448]{1,0:T(8,128)(2,1)} %collective-permute-done.2), channel_id=1, source_target_pairs={{0,256},{16,816},{64,320},{80,880},{128,384},{144,944},{192,448},{... | collective-permute-start | bytes 688136 | tf_op jit(solution)/shard_map/ppermute | solution.py:139
  136.0 2.4 %while.181 = (s32[]{:T(128)}, f32[128,448]{0,1:T(8,128)S(1)}, bf16[256,128]{1,0:T(8,128)(2,1)S(1)}, bf16[256,448]{1,0:T(8,128)(2,1)}, s32[]{:T(128)}, /*index=5*/s32[]{:T(128)}, s32[]{:T(128)}, s32[]{:T(128)}) while((s32[]{:T(128)}, f32[128,448]{0,1:T(8,128)S(1)}, bf16[256,128]{1,0:T(8,128)(2,1)S(1)}, bf16[256,448]{1,0:T(8,128)(2,1)}, ...), condition=%wide.region_9.10_spmd.clone, body=%wide.region_8.9_spmd.clone.sunk | while | flops 14794759 | bytes 624268 | solution.py:71
  136.0 1.2 convolution_add_fusion.25
  137.2 1.2 convolution_add_fusion.25
  138.4 1.9 collective-permute-start.4
  140.4 2.4 %while.182 = (s32[]{:T(128)}, f32[128,448]{0,1:T(8,128)S(1)}, bf16[256,128]{1,0:T(8,128)(2,1)S(1)}, bf16[256,448]{1,0:T(8,128)(2,1)}, s32[]{:T(128)}, /*index=5*/s32[]{:T(128)}, s32[]{:T(128)}, s32[]{:T(128)}) while((s32[]{:T(128)}, f32[128,448]{0,1:T(8,128)S(1)}, bf16[256,128]{1,0:T(8,128)(2,1)S(1)}, ...), condition=%wide.region_11.12_spmd.clone, body=%wide.region_10.11_spmd.clone.sunk | while | flops 14794759 | bytes 624268 | solution.py:71
  140.4 1.2 convolution_add_fusion.26
  141.6 1.2 convolution_add_fusion.26
  142.8 4.0 %collective-permute-done.3 = bf16[256,448]{1,0:T(8,128)(2,1)} collective-permute-done((bf16[256,448]{1,0:T(8,128)(2,1)}, bf16[256,448]{1,0:T(8,128)(2,1)}, u32[]{:S(2)}, u32[]{:S(2)}) %collective-permute-start.3) | collective-permute-done | bytes 229408 | tf_op jit(solution)/shard_map/ppermute | solution.py:139
  146.9 1.9 collective-permute-start.6
  148.8 7.4 %collective-permute-start.5 = (bf16[256,448]{1,0:T(8,128)(2,1)}, bf16[256,448]{1,0:T(8,128)(2,1)}, u32[]{:S(2)}, u32[]{:S(2)}) collective-permute-start(bf16[256,448]{1,0:T(8,128)(2,1)} %collective-permute-done.3), channel_id=1, source_target_pairs={{0,256},{16,816},{64,320},{80,880},{128,384},{144,944},{192,448},{... | collective-permute-start | bytes 688136 | tf_op jit(solution)/shard_map/ppermute | solution.py:147
  156.2 2.5 %while.175 = (s32[]{:T(128)}, f32[256,448]{0,1:T(8,128)S(1)}, bf16[256,256]{1,0:T(8,128)(2,1)S(1)}, bf16[256,448]{1,0:T(8,128)(2,1)}, s32[]{:T(128)}, /*index=5*/s32[]{:T(128)}, s32[]{:T(128)}, s32[]{:T(128)}) while((s32[]{:T(128)}, f32[256,448]{0,1:T(8,128)S(1)}, bf16[256,256]{1,0:T(8,128)(2,1)S(1)}, bf16[256,448]{1,0:T(8,128)(2,1)}, ...), condition=%wide.region_13.14_spmd, body=%wide.region_12.13_spmd.sunk | while | flops 29474820 | bytes 1115267 | solution.py:71
  156.2 1.2 convolution_add_fusion.19
  157.5 1.2 convolution_add_fusion.19
  158.7 1.0 broadcast_select_fusion.3
  159.7 1.7 convolution_convert_fusion
  161.5 1.3 reverse_select_fusion
  162.8 1.1 slice_bitcast_fusion.3
  163.9 2.5 %while.183 = (s32[]{:T(128)}, f32[256,448]{0,1:T(8,128)S(1)}, bf16[256,256]{1,0:T(8,128)(2,1)S(1)}, bf16[256,448]{1,0:T(8,128)(2,1)}, s32[]{:T(128)}, /*index=5*/s32[]{:T(128)}, s32[]{:T(128)}, s32[]{:T(128)}) while((s32[]{:T(128)}, f32[256,448]{0,1:T(8,128)S(1)}, bf16[256,256]{1,0:T(8,128)(2,1)S(1)}, ...), condition=%wide.region_15.16_spmd.clone, body=%wide.region_14.15_spmd.clone.sunk | while | flops 29589512 | bytes 1115788 | solution.py:71
  164.0 1.2 convolution_add_fusion.27
  165.2 1.2 convolution_add_fusion.27
  166.5 2.5 %while.176 = (s32[]{:T(128)}, f32[256,448]{0,1:T(8,128)S(1)}, bf16[256,256]{1,0:T(8,128)(2,1)S(1)}, bf16[256,448]{1,0:T(8,128)(2,1)}, s32[]{:T(128)}, /*index=5*/s32[]{:T(128)}, s32[]{:T(128)}, s32[]{:T(128)}) while((s32[]{:T(128)}, f32[256,448]{0,1:T(8,128)S(1)}, bf16[256,256]{1,0:T(8,128)(2,1)S(1)}, bf16[256,448]{1,0:T(8,128)(2,1)}, ...), condition=%wide.region_17.18_spmd, body=%wide.region_16.17_spmd.sunk | while | flops 29474820 | bytes 1115267 | solution.py:71
  166.5 1.2 convolution_add_fusion.20
  167.8 1.2 convolution_add_fusion.20
  169.0 6.3 %collective-permute-start.7 = (bf16[256,448]{1,0:T(8,128)(2,1)}, bf16[256,448]{1,0:T(8,128)(2,1)S(1)}, u32[]{:S(2)}, u32[]{:S(2)}) collective-permute-start(bf16[256,448]{1,0:T(8,128)(2,1)} %collective-permute-done.5), channel_id=1, source_target_pairs={{0,256},{16,816},{64,320},{80,880},{128,384},{144,944},{192,448},{... | collective-permute-start | bytes 688136 | tf_op jit(solution)/shard_map/ppermute | solution.py:165
  175.3 6.5 %all-to-all-start.4 = ((bf16[16,4,8,1024]{3,2,1,0:T(8,128)(2,1)}), bf16[16,4,8,1024]{3,2,1,0:T(8,128)(2,1)S(1)}, u32[]{:S(2)}, u32[]{:S(2)}) async-start(bf16[16,4,8,1024]{3,2,1,0:T(8,128)(2,1)} %bitcast.25), calls=%async_computation.4 | async-start | bytes 2097152 | tf_op jit(solution)/shard_map/all_to_all | solution.py:161
  181.9 2.5 %while.178 = (s32[]{:T(128)}, f32[256,448]{0,1:T(8,128)S(1)}, bf16[256,256]{1,0:T(8,128)(2,1)S(1)}, bf16[256,448]{1,0:T(8,128)(2,1)}, s32[]{:T(128)}, /*index=5*/s32[]{:T(128)}, s32[]{:T(128)}, s32[]{:T(128)}) while((s32[]{:T(128)}, f32[256,448]{0,1:T(8,128)S(1)}, bf16[256,256]{1,0:T(8,128)(2,1)S(1)}, bf16[256,448]{1,0:T(8,128)(2,1)}, ...), condition=%wide.region_21.22_spmd, body=%wide.region_20.21_spmd.sunk | while | flops 29474820 | bytes 1115267 | solution.py:71
  181.9 1.2 convolution_add_fusion.22
  183.1 1.2 convolution_add_fusion.22
  184.4 2.5 %while.177 = (s32[]{:T(128)}, f32[256,448]{0,1:T(8,128)S(1)}, bf16[256,256]{1,0:T(8,128)(2,1)S(1)}, bf16[256,448]{1,0:T(8,128)(2,1)}, s32[]{:T(128)}, /*index=5*/s32[]{:T(128)}, s32[]{:T(128)}, s32[]{:T(128)}) while((s32[]{:T(128)}, f32[256,448]{0,1:T(8,128)S(1)}, bf16[256,256]{1,0:T(8,128)(2,1)S(1)}, bf16[256,448]{1,0:T(8,128)(2,1)}, ...), condition=%wide.region_19.20_spmd, body=%wide.region_18.19_spmd.sunk | while | flops 29474820 | bytes 1115267 | solution.py:71
  184.4 1.3 convolution_add_fusion.21
  185.7 1.2 convolution_add_fusion.21
  186.9 12.0 %all-to-all-done.4 = bf16[16,4,8,1024]{3,2,1,0:T(8,128)(2,1)S(1)} async-done(((bf16[16,4,8,1024]{3,2,1,0:T(8,128)(2,1)}), bf16[16,4,8,1024]{3,2,1,0:T(8,128)(2,1)S(1)}, u32[]{:S(2)}, u32[]{:S(2)}) %all-to-all-start.4) | async-done | bytes 1048608 | tf_op jit(solution)/shard_map/all_to_all | solution.py:161
  198.9 0.8 convert_reduce_fusion
  199.7 3.3 %all-to-all-start.5 = ((f32[4,8,1024]{2,1,0:T(8,128)}), f32[4,8,1024]{2,1,0:T(8,128)S(1)}, u32[]{:S(2)}, u32[]{:S(2)}) async-start(f32[4,8,1024]{2,1,0:T(8,128)} %convert_reduce_fusion), calls=%async_computation.5 | async-start | bytes 262144 | tf_op jit(solution)/shard_map/all_to_all | solution.py:173
  204.0 1.9 collective-permute-start.8
  205.9 3.2 %all-to-all-done.5 = f32[4,8,1024]{2,1,0:T(8,128)S(1)} async-done(((f32[4,8,1024]{2,1,0:T(8,128)}), f32[4,8,1024]{2,1,0:T(8,128)S(1)}, u32[]{:S(2)}, u32[]{:S(2)}) %all-to-all-start.5) | async-done | bytes 131104 | tf_op jit(solution)/shard_map/all_to_all | solution.py:173
  209.1 4.7 %collective-permute-start.9 = (bf16[8,1024]{1,0:T(8,128)(2,1)S(1)}, bf16[8,1024]{1,0:T(8,128)(2,1)S(1)}, u32[]{:S(2)}, u32[]{:S(2)}) collective-permute-start(bf16[8,1024]{1,0:T(8,128)(2,1)S(1)} %reduce_sum.19), channel_id=1, source_target_pairs={{0,512},{256,768},{512,0},{768,256},{1,513},{257,769},{513,1},{769... | collective-permute-start | bytes 49160 | tf_op jit(solution)/shard_map/ppermute | solution.py:175
  214.7 0.8 add.423
  215.4 8.0 %collective-permute-done.9 = bf16[8,1024]{1,0:T(8,128)(2,1)S(1)} collective-permute-done((bf16[8,1024]{1,0:T(8,128)(2,1)S(1)}, bf16[8,1024]{1,0:T(8,128)(2,1)S(1)}, u32[]{:S(2)}, u32[]{:S(2)}) %collective-permute-start.9) | collective-permute-done | bytes 16416 | tf_op jit(solution)/shard_map/ppermute | solution.py:175
  223.4 3.4 %all-to-all-start.6 = ((bf16[4,64,448]{2,1,0:T(8,128)(2,1)}), bf16[4,64,448]{2,1,0:T(8,128)(2,1)S(1)}, u32[]{:S(2)}, u32[]{:S(2)}) async-start(bf16[4,64,448]{2,1,0:T(8,128)(2,1)} %bitcast.32), calls=%async_computation.6 | async-start | bytes 524288 | tf_op jit(solution)/shard_map/all_to_all | solution.py:178
  228.4 5.2 %all-to-all-done.6 = bf16[4,64,448]{2,1,0:T(8,128)(2,1)S(1)} async-done(((bf16[4,64,448]{2,1,0:T(8,128)(2,1)}), bf16[4,64,448]{2,1,0:T(8,128)(2,1)S(1)}, u32[]{:S(2)}, u32[]{:S(2)}) %all-to-all-start.6) | async-done | bytes 229408 | tf_op jit(solution)/shard_map/all_to_all | solution.py:178
  234.5 0.8 slice_multiply_fusion
  (95 shorter events, 25.9 us)
Async XLA Ops:
  2.1 22.9 %all-to-all-start = ((bf16[16,8,1024]{2,1,0:T(8,128)(2,1)}), bf16[16,8,1024]{2,1,0:T(8,128)(2,1)S(1)}, u32[]{:S(2)}, u32[]{:S(2)}) async-start(bf16[16,8,1024]{2,1,0:T(8,128)(2,1)} %broadcast_in_dim.55), calls=%async_computation | async-start | bytes 524288 | tf_op jit(solution)/shard_map/all_to_all | solution.py:47
  27.9 3.7 %collective-permute-start = (f32[64,1792]{1,0:T(8,128)S(1)}, f32[64,1792]{1,0:T(8,128)S(1)}, u32[]{:S(2)}, u32[]{:S(2)}) collective-permute-start(f32[64,1792]{1,0:T(8,128)S(1)} %fusion.43), channel_id=1, source_target_pairs={{0,16},{16,0},{1,17},{17,1},{2,18},{18,2},{3,19},{19,3},{4,20},{20... | collective-permute-start | bytes 1376264 | tf_op jit(solution)/shard_map/ppermute | solution.py:97
  31.6 2.8 %copy-start.2 = (bf16[8,1024]{1,0:T(8,128)(2,1)S(1)}, bf16[8,1024]{1,0:T(8,128)(2,1)}, u32[]{:S(2)}) copy-start(bf16[8,1024]{1,0:T(8,128)(2,1)} %param.32) | copy-start | bytes 49156
  35.6 31.6 %collective-permute-start.1 = (bf16[32,1792]{1,0:T(8,128)(2,1)S(1)}, bf16[32,1792]{1,0:T(8,128)(2,1)S(1)}, u32[]{:S(2)}, u32[]{:S(2)}) collective-permute-start(bf16[32,1792]{1,0:T(8,128)(2,1)S(1)} %slice.90), channel_id=1, source_target_pairs={{0,32},{32,0},{1,33},{33,1},{2,34},{34,2},{3,35},{35,3},{4,36},{36... | collective-permute-start | bytes 344072 | tf_op jit(solution)/shard_map/ppermute | solution.py:101
  55.5 29.0 %all-to-all-start.1 = ((bf16[16,8,256]{2,1,0:T(8,128)(2,1)}), bf16[16,8,256]{2,1,0:T(8,128)(2,1)S(1)}, u32[]{:S(2)}, u32[]{:S(2)}) async-start(bf16[16,8,256]{2,1,0:T(8,128)(2,1)} %bitcast.9), calls=%async_computation.1 | async-start | bytes 131072 | tf_op jit(solution)/shard_map/all_to_all | solution.py:102
  64.3 20.2 %copy-start.3 = (bf16[32,896]{1,0:T(8,128)(2,1)S(1)}, bf16[32,896]{1,0:T(8,128)(2,1)}, u32[]{:S(2)}) copy-start(bf16[32,896]{1,0:T(8,128)(2,1)} %param.37) | copy-start | bytes 172036
  86.2 13.1 %all-to-all-start.2 = ((bf16[8,32,448]{2,1,0:T(8,128)(2,1)}), bf16[8,32,448]{2,1,0:T(8,128)(2,1)S(1)}, u32[]{:S(2)}, u32[]{:S(2)}) async-start(bf16[8,32,448]{2,1,0:T(8,128)(2,1)} %bitcast.12), calls=%async_computation.2 | async-start | bytes 524288 | tf_op jit(solution)/shard_map/all_to_all | solution.py:118
  101.2 23.6 %collective-permute-start.2 = (bf16[256,448]{1,0:T(8,128)(2,1)}, bf16[256,448]{1,0:T(8,128)(2,1)}, u32[]{:S(2)}, u32[]{:S(2)}) collective-permute-start(bf16[256,448]{1,0:T(8,128)(2,1)} %bitcast.15), channel_id=1, source_target_pairs={{0,256},{16,816},{64,320},{80,880},{128,384},{144,944},{192,448},{... | collective-permute-start | bytes 688136 | tf_op jit(solution)/shard_map/ppermute | solution.py:122
  105.5 24.0 %all-to-all-start.3 = ((bf16[16,16,8,256]{3,2,1,0:T(8,128)(2,1)}), bf16[16,16,8,256]{3,2,1,0:T(8,128)(2,1)S(1)}, u32[]{:S(2)}, u32[]{:S(2)}) async-start(bf16[16,16,8,256]{3,2,1,0:T(8,128)(2,1)} %broadcast_in_dim.63), calls=%async_computation.3 | async-start | bytes 2097152 | tf_op jit(solution)/shard_map/all_to_all | solution.py:47
  124.8 5.3 %copy-start = (bf16[256,448]{1,0:T(8,128)(2,1)}, bf16[256,448]{1,0:T(8,128)(2,1)S(1)}, u32[]{:S(2)}) copy-start(bf16[256,448]{1,0:T(8,128)(2,1)S(1)} %get-tuple-element.1020) | copy-start | bytes 688132
  131.2 15.7 %collective-permute-start.3 = (bf16[256,448]{1,0:T(8,128)(2,1)}, bf16[256,448]{1,0:T(8,128)(2,1)}, u32[]{:S(2)}, u32[]{:S(2)}) collective-permute-start(bf16[256,448]{1,0:T(8,128)(2,1)} %collective-permute-done.2), channel_id=1, source_target_pairs={{0,256},{16,816},{64,320},{80,880},{128,384},{144,944},{192,448},{... | collective-permute-start | bytes 688136 | tf_op jit(solution)/shard_map/ppermute | solution.py:139
  138.4 8.4 %collective-permute-start.4 = (bf16[4,256,256]{2,1,0:T(8,128)(2,1)}, bf16[4,256,256]{2,1,0:T(8,128)(2,1)}, u32[]{:S(2)}, u32[]{:S(2)}) collective-permute-start(bf16[4,256,256]{2,1,0:T(8,128)(2,1)} %get-tuple-element.1015), channel_id=1, source_target_pairs={{0,16},{16,0},{1,17},{17,1},{2,18},{18,2},{3,19},{19,3},{4,20},{20... | collective-permute-start | bytes 1572872 | tf_op jit(solution)/shard_map/ppermute | solution.py:142
  146.9 11.9 %collective-permute-start.6 = (bf16[256,448]{1,0:T(8,128)(2,1)}, bf16[256,448]{1,0:T(8,128)(2,1)S(1)}, u32[]{:S(2)}, u32[]{:S(2)}) collective-permute-start(bf16[256,448]{1,0:T(8,128)(2,1)} %collective-permute-done.3), channel_id=1, source_target_pairs={{0,16},{16,0},{1,17},{17,1},{2,18},{18,2},{3,19},{19,3},{4,20},{20... | collective-permute-start | bytes 688136 | tf_op jit(solution)/shard_map/ppermute | solution.py:149
  148.8 20.2 %collective-permute-start.5 = (bf16[256,448]{1,0:T(8,128)(2,1)}, bf16[256,448]{1,0:T(8,128)(2,1)}, u32[]{:S(2)}, u32[]{:S(2)}) collective-permute-start(bf16[256,448]{1,0:T(8,128)(2,1)} %collective-permute-done.3), channel_id=1, source_target_pairs={{0,256},{16,816},{64,320},{80,880},{128,384},{144,944},{192,448},{... | collective-permute-start | bytes 688136 | tf_op jit(solution)/shard_map/ppermute | solution.py:147
  169.0 17.9 %collective-permute-start.7 = (bf16[256,448]{1,0:T(8,128)(2,1)}, bf16[256,448]{1,0:T(8,128)(2,1)S(1)}, u32[]{:S(2)}, u32[]{:S(2)}) collective-permute-start(bf16[256,448]{1,0:T(8,128)(2,1)} %collective-permute-done.5), channel_id=1, source_target_pairs={{0,256},{16,816},{64,320},{80,880},{128,384},{144,944},{192,448},{... | collective-permute-start | bytes 688136 | tf_op jit(solution)/shard_map/ppermute | solution.py:165
  175.3 23.5 %all-to-all-start.4 = ((bf16[16,4,8,1024]{3,2,1,0:T(8,128)(2,1)}), bf16[16,4,8,1024]{3,2,1,0:T(8,128)(2,1)S(1)}, u32[]{:S(2)}, u32[]{:S(2)}) async-start(bf16[16,4,8,1024]{3,2,1,0:T(8,128)(2,1)} %bitcast.25), calls=%async_computation.4 | async-start | bytes 2097152 | tf_op jit(solution)/shard_map/all_to_all | solution.py:161
  184.3 18.7 %copy-start.1 = (bf16[256,448]{1,0:T(8,128)(2,1)S(1)}, bf16[256,448]{1,0:T(8,128)(2,1)}, u32[]{:S(2)}) copy-start(bf16[256,448]{1,0:T(8,128)(2,1)} %copy-done) | copy-start | bytes 688132
  199.7 9.4 %all-to-all-start.5 = ((f32[4,8,1024]{2,1,0:T(8,128)}), f32[4,8,1024]{2,1,0:T(8,128)S(1)}, u32[]{:S(2)}, u32[]{:S(2)}) async-start(f32[4,8,1024]{2,1,0:T(8,128)} %convert_reduce_fusion), calls=%async_computation.5 | async-start | bytes 262144 | tf_op jit(solution)/shard_map/all_to_all | solution.py:173
  204.0 10.7 %collective-permute-start.8 = (f32[256,448]{1,0:T(8,128)S(1)}, f32[256,448]{1,0:T(8,128)S(1)}, u32[]{:S(2)}, u32[]{:S(2)}) collective-permute-start(f32[256,448]{1,0:T(8,128)S(1)} %copy.38), channel_id=1, source_target_pairs={{0,16},{16,0},{1,17},{17,1},{2,18},{18,2},{3,19},{19,3},{4,20},{20... | collective-permute-start | bytes 1376264 | tf_op jit(solution)/shard_map/ppermute | solution.py:171
  209.1 14.3 %collective-permute-start.9 = (bf16[8,1024]{1,0:T(8,128)(2,1)S(1)}, bf16[8,1024]{1,0:T(8,128)(2,1)S(1)}, u32[]{:S(2)}, u32[]{:S(2)}) collective-permute-start(bf16[8,1024]{1,0:T(8,128)(2,1)S(1)} %reduce_sum.19), channel_id=1, source_target_pairs={{0,512},{256,768},{512,0},{768,256},{1,513},{257,769},{513,1},{769... | collective-permute-start | bytes 49160 | tf_op jit(solution)/shard_map/ppermute | solution.py:175
  223.4 10.2 %all-to-all-start.6 = ((bf16[4,64,448]{2,1,0:T(8,128)(2,1)}), bf16[4,64,448]{2,1,0:T(8,128)(2,1)S(1)}, u32[]{:S(2)}, u32[]{:S(2)}) async-start(bf16[4,64,448]{2,1,0:T(8,128)(2,1)} %bitcast.32), calls=%async_computation.6 | async-start | bytes 524288 | tf_op jit(solution)/shard_map/all_to_all | solution.py:178

commit v5 on v4

--- a/solution.py
+++ b/solution.py
@@ -95,7 +95,8 @@
         return jnp.dot(x.reshape(2 * rows, features), both_weights, preferred_element_type=F32)
 
     others = lax.ppermute(project(replica[:, 1]), "core", SWAP)
-    summed = project(replica[:, 0]) + others
+    summed, others = lax.optimization_barrier((project(replica[:, 0]), others))
+    summed = summed + others
     summed, spread, both_weights = lax.optimization_barrier((summed, spread, both_weights))
 
     arrived = lax.ppermute(summed[rows:].astype(BF16), "half", SWAP)
@@ -122,7 +123,7 @@
     first = lax.ppermute(own, Z, RING)
     everyone = gather_col(in_turns(spread, own[:1, :1]), columns)
     own = in_turns(own, own[:1, :1], TURNS)
-    first, everyone, own = lax.optimization_barrier((first, everyone, own))
+    first, own = lax.optimization_barrier((first, own))
 
     everyone = everyone.reshape(2, 2, columns // 4, GROUPS, TEAM, held, block)
     everyone = everyone.transpose(0, 3, 1, 4, 2, 5, 6).reshape(PLACES, 2 * TEAM * rows, block)
@@ -132,20 +133,15 @@
     after = jnp.concatenate([after[1:], after[:1]], axis=0)
     my_rows, their_rows = jnp.where(core == 0, before, after), jnp.where(core == 0, after, before)
 
-    def add(step, tokens_of, met, *total):
+    def add(step, tokens_of, met, *total, turns=2):
         start = total[0] if total else jnp.zeros((tokens_of.shape[2], share), F32)
-        return add_term(start, tokens_of[step], met)
+        return add_term(start, tokens_of[step], met, turns)
 
     second = lax.ppermute(first, Z, RING)
-    low = add(0, my_rows[:1, :, : block // 2], first)
-    low, their_rows = lax.optimization_barrier((low, their_rows))
-    their_rows = lax.ppermute(their_rows, "core", SWAP)
-    high = add(0, my_rows[:1, :, block // 2 :], first)
-    second, low, high, their_rows = lax.optimization_barrier((second, low, high, their_rows))
-    my_total = jnp.concatenate([low, high], axis=0)
+    my_total = add(0, my_rows, first)
+    second, my_total = lax.optimization_barrier((second, my_total))
 
     third = lax.ppermute(second, Z, RING)
-    my_total = add(1, my_rows, second, my_total)
     across = lax.ppermute(second, "core", SWAP)
     far = jnp.where((group < PLACES // 4) == (core == 0), second, across)
     part = lax.dot_general(
@@ -157,23 +153,24 @@
     part = part.reshape(2, 2, TEAM, columns // 4, held, features)
     part = jnp.where(half == 0, part, part[::-1]).transpose(0, 1, 3, 2, 4, 5)
     part = part.reshape(columns, TEAM, held, features)
-    part, their_rows = lax.optimization_barrier((part, their_rows))
+    part, my_total, my_rows, their_rows = lax.optimization_barrier((part, my_total, my_rows, their_rows))
     part = lax.all_to_all(part, "col", 0, 0)
-    their_total = add(1, their_rows, second, add(0, their_rows, first))
-    third, my_total, their_total = lax.optimization_barrier((third, my_total, their_total))
+    their_rows = lax.ppermute(their_rows, "core", SWAP)
+    my_total = add(1, my_rows, second, my_total, turns=4)
+    third, my_total = lax.optimization_barrier((third, my_total))
 
     fourth = lax.ppermute(third, Z, RING)
+    my_total, part, their_rows = lax.optimization_barrier((my_total, part, their_rows))
     my_total = add(2, my_rows, third, my_total)
-    their_total = add(2, their_rows, third, their_total)
-    fourth, my_total, their_total, part = lax.optimization_barrier((fourth, my_total, their_total, part))
+    their_total = add(2, their_rows, third, add(1, their_rows, second, add(0, their_rows, first)))
+    reduced = jnp.sum(part.astype(F32), axis=0)
+    reduced = jnp.sum(lax.all_to_all(reduced, "member", 0, 0), axis=0).astype(BF16)
+    swapped = lax.ppermute(reduced, "group", FAR_GROUP)
+    fourth, my_total, their_total, swapped = lax.optimization_barrier((fourth, my_total, their_total, swapped))
 
     last = jnp.where(core == 0, fourth, own)
     got = lax.ppermute(add(3, their_rows, last, their_total), "core", SWAP)
-    reduced = jnp.sum(part.astype(F32), axis=0)
-    reduced = jnp.sum(lax.all_to_all(reduced, "member", 0, 0), axis=0).astype(BF16)
     full = add(3, my_rows, last, my_total) + got
-    swapped = lax.ppermute(reduced, "group", FAR_GROUP)
-    full, swapped = lax.optimization_barrier((full, swapped))
     grad_tokens = jnp.where((col < columns // 2) == (half == 0), reduced, swapped)
     traded = lax.all_to_all(full.astype(BF16).reshape(TEAM, block // TEAM, share), "member", 0, 0)
     grads = traded.transpose(1, 0, 2).reshape(block // TEAM, 2 * units).astype(F32)

time: 239 us -> 234 us (0.979)
  waiting for transfers between devices: 66 us -> 55.2 us
  starting transfers between devices: 102 us -> 109 us
    ppermute x1, waiting for transfers between devices: 8 us -> 2.14 us  [body(): swapped = lax.ppermute(reduced, 'group', FAR_GROUP)]
    all_to_all x1, waiting for transfers between devices: 12 us -> 6.55 us  [body(): part = lax.all_to_all(part, 'col', 0, 0)]
    ppermute x1, waiting for transfers between devices: 4.03 us -> 9.24 us  [body(): second = lax.ppermute(first, Z, RING)]
    ppermute x1, starting transfers between devices: 4.66 us -> 9.68 us  [body(): swapped = lax.ppermute(reduced, 'group', FAR_GROUP)]
    all_to_all x2, waiting for transfers between devices: 4.91 us -> 0.2 us  [gather_col(): lax.all_to_all(jnp.broadcast_to(x[None], (count, *x.shape)), 'col', 0, 0)]
    all_to_all x1, waiting for transfers between devices: 5.24 us -> 7.76 us  [body(): lax.all_to_all(full.astype(BF16).reshape(TEAM, block // TEAM, share), 'me...]
  transfers between devices with their start and end apart: 17 -> 17, of which waited for: 10 -> 9; matrix products, arithmetic and copies ran while one was open for 21% -> 22% of each run, Pallas kernels for 0% -> 0%
where the time goes in v5:
time: 234 us; the launch traced here: 230 us
  starting transfers between devices  109 us (47%)
  waiting for transfers between devices  55.2 us (24%)
  local copies, waits for them, and re-layouts  25.1 us (11%)
  matrix products  24.5 us (10%)
  other arithmetic  14.4 us (6%)
    all_to_all x2, starting transfers between devices, gather_col(): lax.all_to_all(jnp.broadcast_to(x[None], (count, *x.shape)), 'col', 0, 0)  23.5 us
    ppermute x1, starting transfers between devices, body(): arrived = lax.ppermute(summed[rows:].astype(BF16), 'half', SWAP)  19.9 us
    dot_general x18, matrix products, turn(): lax.dot_general(lax.dynamic_slice_in_dim(rows, i * part, part, axis=0), l...  18.2 us
    all_to_all x1, waiting for transfers between devices, body(): spread = lax.all_to_all(in_turns(spread, summed[:1, :1], 16), DP, 0, 0)  17.8 us
    dynamic_update_slice x26, local copies, waits for them, and re-layouts, turn(): return lax.dynamic_update_slice_in_dim(y, piece, i * part, axis=0)  11.7 us
    ppermute x1, starting transfers between devices, body(): swapped = lax.ppermute(reduced, 'group', FAR_GROUP)  9.68 us
    all_to_all x1, waiting for transfers between devices, body(): lax.all_to_all(shares, ('member', 'core'), 0, 0)  9.64 us
    ppermute x1, waiting for transfers between devices, body(): second = lax.ppermute(first, Z, RING)  9.24 us
  transfers between devices with their start and end apart: 17, of which 9 were waited for; matrix products, arithmetic and copies ran while one was open for 22% of the time, Pallas kernels for 0%

profile of v5, /device:TPU:6, one launch (start us, length us, event | category | flops | bytes accessed | tf_op | source)
XLA Modules:
  0.0 230.4 jit_solution(4630332144022031193)
XLA Ops:
  0.6 1.4 broadcast_in_dim.52
  2.1 16.5 %all-to-all-start = ((bf16[16,8,1024]{2,1,0:T(8,128)(2,1)}), bf16[16,8,1024]{2,1,0:T(8,128)(2,1)S(1)}, u32[]{:S(2)}, u32[]{:S(2)}) async-start(bf16[16,8,1024]{2,1,0:T(8,128)(2,1)} %broadcast_in_dim.52), calls=%async_computation | async-start | bytes 524288 | tf_op jit(solution)/shard_map/all_to_all | solution.py:47
  20.3 2.4 %bitcast_multiply_fusion = (bf16[1024,896]{1,0:T(8,128)(2,1)S(1)}, bf16[1024,896]{1,0:T(8,128)(2,1)S(1)}) fusion(bf16[1024,896]{1,0:T(8,128)(2,1)} %param.32, bf16[8,896]{1,0:T(8,128)(2,1)S(1)} %broadcast_bitcast_fusion, bf16[1024,896]{1,0:T(8,128)(2,1)} %param.31, bf16[8,896]{1,0:T(8,128)(2,1)S(1)} %broadcast_bitcast_fusion.1), kind=kLoop, calls=%fused_computation.41 | loop fusion | flops 1835008 | bytes 7368704 | tf_op jit(solution)/shard_map/mul | solution.py:43
  22.8 2.0 pad_maximum_fusion
  25.1 2.8 %fusion.41 = f32[64,1792]{1,0:T(8,128)S(1)} fusion(bf16[64,1024]{1,0:T(8,128)(2,1)S(1)} %bitcast.69, bf16[1024,1792]{1,0:T(8,128)(2,1)} %pad_maximum_fusion), kind=kOutput, calls=%fused_computation.95 | convolution fusion | flops 234881024 | bytes 4259840 | tf_op jit(solution)/shard_map/dot_general | solution.py:95
  27.9 1.9 collective-permute-start
  29.9 2.8 %fusion.40 = f32[64,1792]{1,0:T(8,128)S(1)} fusion(bf16[64,1024]{1,0:T(8,128)(2,1)S(1)} %bitcast.68, bf16[1024,1792]{1,0:T(8,128)(2,1)} %pad_maximum_fusion), kind=kOutput, calls=%fused_computation.94 | convolution fusion | flops 234881024 | bytes 4259840 | tf_op jit(solution)/shard_map/dot_general | solution.py:95
  33.9 19.9 %collective-permute-start.1 = (bf16[32,1792]{1,0:T(8,128)(2,1)S(1)}, bf16[32,1792]{1,0:T(8,128)(2,1)S(1)}, u32[]{:S(2)}, u32[]{:S(2)}) collective-permute-start(bf16[32,1792]{1,0:T(8,128)(2,1)S(1)} %slice.86), channel_id=1, source_target_pairs={{0,32},{32,0},{1,33},{33,1},{2,34},{34,2},{3,35},{35,3},{4,36},{36... | collective-permute-start | bytes 344072 | tf_op jit(solution)/shard_map/ppermute | solution.py:102
  53.8 8.8 %all-to-all-start.1 = ((bf16[16,8,256]{2,1,0:T(8,128)(2,1)}), bf16[16,8,256]{2,1,0:T(8,128)(2,1)S(1)}, u32[]{:S(2)}, u32[]{:S(2)}) async-start(bf16[16,8,256]{2,1,0:T(8,128)(2,1)} %bitcast.9), calls=%async_computation.1 | async-start | bytes 131072 | tf_op jit(solution)/shard_map/all_to_all | solution.py:103
  62.6 1.8 constant_dynamic-slice_fusion.2
  65.5 17.8 %all-to-all-done.1 = bf16[16,8,256]{2,1,0:T(8,128)(2,1)S(1)} async-done(((bf16[16,8,256]{2,1,0:T(8,128)(2,1)}), bf16[16,8,256]{2,1,0:T(8,128)(2,1)S(1)}, u32[]{:S(2)}, u32[]{:S(2)}) %all-to-all-start.1) | async-done | bytes 65568 | tf_op jit(solution)/shard_map/all_to_all | solution.py:103
  84.3 0.7 broadcast_in_dim.58
  85.0 3.4 %all-to-all-start.2 = ((bf16[8,32,448]{2,1,0:T(8,128)(2,1)}), bf16[8,32,448]{2,1,0:T(8,128)(2,1)S(1)}, u32[]{:S(2)}, u32[]{:S(2)}) async-start(bf16[8,32,448]{2,1,0:T(8,128)(2,1)} %bitcast.12), calls=%async_computation.2 | async-start | bytes 524288 | tf_op jit(solution)/shard_map/all_to_all | solution.py:119
  88.4 9.6 %all-to-all-done.2 = bf16[8,32,448]{2,1,0:T(8,128)(2,1)S(1)} async-done(((bf16[8,32,448]{2,1,0:T(8,128)(2,1)}), bf16[8,32,448]{2,1,0:T(8,128)(2,1)S(1)}, u32[]{:S(2)}, u32[]{:S(2)}) %all-to-all-start.2) | async-done | bytes 229408 | tf_op jit(solution)/shard_map/all_to_all | solution.py:119
  98.8 1.2 slice.71
  100.0 2.1 collective-permute-start.2
  102.8 1.1 broadcast_in_dim.61
  103.9 7.0 %all-to-all-start.3 = ((bf16[16,16,8,256]{3,2,1,0:T(8,128)(2,1)}), bf16[16,16,8,256]{3,2,1,0:T(8,128)(2,1)S(1)}, u32[]{:S(2)}, u32[]{:S(2)}) async-start(bf16[16,16,8,256]{3,2,1,0:T(8,128)(2,1)} %broadcast_in_dim.61), calls=%async_computation.3 | async-start | bytes 2097152 | tf_op jit(solution)/shard_map/all_to_all | solution.py:47
  111.6 11.5 %while.159 = (s32[]{:T(128)}, bf16[256,448]{1,0:T(8,128)(2,1)S(1)}, bf16[256,448]{1,0:T(8,128)(2,1)}, s32[]{:T(128)}, s32[]{:T(128)}, /*index=5*/s32[]{:T(128)}, s32[]{:T(128)}) while((s32[]{:T(128)}, bf16[256,448]{1,0:T(8,128)(2,1)S(1)}, bf16[256,448]{1,0:T(8,128)(2,1)}, s32[]{:T(128)}, s32[]{:T(128)}, /*index=5*/s32[]{:T(128)}, ...), condition=%wide.region_5.6_spmd, body=%wide.region_4.5_spmd.sunk | while | flops 6 | bytes 30847 | solution.py:57
  111.6 0.7 dynamic-slice_dynamic-update-slice_fusion.7
  123.1 6.8 %collective-permute-start.3 = (bf16[256,448]{1,0:T(8,128)(2,1)}, bf16[256,448]{1,0:T(8,128)(2,1)}, u32[]{:S(2)}, u32[]{:S(2)}) collective-permute-start(bf16[256,448]{1,0:T(8,128)(2,1)} %collective-permute-done.2), channel_id=1, source_target_pairs={{0,256},{16,816},{64,320},{80,880},{128,384},{144,944},{192,448},{... | collective-permute-start | bytes 688136 | tf_op jit(solution)/shard_map/ppermute | solution.py:140
  130.8 2.5 %while.167 = (s32[]{:T(128)}, f32[256,448]{0,1:T(8,128)S(1)}, bf16[256,256]{1,0:T(8,128)(2,1)S(1)}, bf16[256,448]{1,0:T(8,128)(2,1)}, s32[]{:T(128)}, /*index=5*/s32[]{:T(128)}, s32[]{:T(128)}, s32[]{:T(128)}) while((s32[]{:T(128)}, f32[256,448]{0,1:T(8,128)S(1)}, bf16[256,256]{1,0:T(8,128)(2,1)S(1)}, bf16[256,448]{1,0:T(8,128)(2,1)}, ...), condition=%wide.region_9.10_spmd.clone, body=%wide.region_8.9_spmd.clone.sunk | while | flops 29589512 | bytes 1115788 | solution.py:71
  130.8 1.2 convolution_add_fusion.22
  132.1 1.2 convolution_add_fusion.22
  133.3 9.2 %collective-permute-done.3 = bf16[256,448]{1,0:T(8,128)(2,1)} collective-permute-done((bf16[256,448]{1,0:T(8,128)(2,1)}, bf16[256,448]{1,0:T(8,128)(2,1)}, u32[]{:S(2)}, u32[]{:S(2)}) %collective-permute-start.3) | collective-permute-done | bytes 229408 | tf_op jit(solution)/shard_map/ppermute | solution.py:140
  142.6 2.0 collective-permute-start.5
  144.6 6.0 %collective-permute-start.4 = (bf16[256,448]{1,0:T(8,128)(2,1)}, bf16[256,448]{1,0:T(8,128)(2,1)}, u32[]{:S(2)}, u32[]{:S(2)}) collective-permute-start(bf16[256,448]{1,0:T(8,128)(2,1)} %collective-permute-done.3), channel_id=1, source_target_pairs={{0,256},{16,816},{64,320},{80,880},{128,384},{144,944},{192,448},{... | collective-permute-start | bytes 688136 | tf_op jit(solution)/shard_map/ppermute | solution.py:144
  150.7 1.0 broadcast_select_fusion.3
  151.7 0.8 convolution_convert_fusion
  152.5 1.3 reverse_select_fusion
  153.8 4.2 %collective-permute-start.6 = (bf16[4,256,256]{2,1,0:T(8,128)(2,1)S(1)}, bf16[4,256,256]{2,1,0:T(8,128)(2,1)}, u32[]{:S(2)}, u32[]{:S(2)}) collective-permute-start(bf16[4,256,256]{2,1,0:T(8,128)(2,1)S(1)} %get-tuple-element.943), channel_id=1, source_target_pairs={{0,16},{16,0},{1,17},{17,1},{2,18},{18,2},{3,19},{19,3},{4,20},{20... | collective-permute-start | bytes 1572872 | tf_op jit(solution)/shard_map/ppermute | solution.py:158
  158.1 7.2 %all-to-all-start.4 = ((bf16[16,4,8,1024]{3,2,1,0:T(8,128)(2,1)}), bf16[16,4,8,1024]{3,2,1,0:T(8,128)(2,1)S(1)}, u32[]{:S(2)}, u32[]{:S(2)}) async-start(bf16[16,4,8,1024]{3,2,1,0:T(8,128)(2,1)} %bitcast.23), calls=%async_computation.4 | async-start | bytes 2097152 | tf_op jit(solution)/shard_map/all_to_all | solution.py:157
  165.3 4.7 %while.161 = (s32[]{:T(128)}, f32[256,448]{0,1:T(8,128)S(1)}, bf16[256,256]{1,0:T(8,128)(2,1)S(1)}, bf16[256,448]{1,0:T(8,128)(2,1)}, s32[]{:T(128)}, /*index=5*/s32[]{:T(128)}, s32[]{:T(128)}, s32[]{:T(128)}) while((s32[]{:T(128)}, f32[256,448]{0,1:T(8,128)S(1)}, bf16[256,256]{1,0:T(8,128)(2,1)S(1)}, bf16[256,448]{1,0:T(8,128)(2,1)}, ...), condition=%wide.region_11.12_spmd, body=%wide.region_10.11_spmd.sunk | while | flops 14794758 | bytes 1016963 | solution.py:71
  165.3 1.2 convolution_add_fusion.16
  166.5 1.2 convolution_add_fusion.16
  167.7 1.2 convolution_add_fusion.16
  168.9 1.2 convolution_add_fusion.16
  170.1 4.1 %collective-permute-start.7 = (bf16[256,448]{1,0:T(8,128)(2,1)}, bf16[256,448]{1,0:T(8,128)(2,1)}, u32[]{:S(2)}, u32[]{:S(2)}) collective-permute-start(bf16[256,448]{1,0:T(8,128)(2,1)} %collective-permute-done.4), channel_id=1, source_target_pairs={{0,256},{16,816},{64,320},{80,880},{128,384},{144,944},{192,448},{... | collective-permute-start | bytes 688136 | tf_op jit(solution)/shard_map/ppermute | solution.py:162
  174.2 6.5 %all-to-all-done.4 = bf16[16,4,8,1024]{3,2,1,0:T(8,128)(2,1)S(1)} async-done(((bf16[16,4,8,1024]{3,2,1,0:T(8,128)(2,1)}), bf16[16,4,8,1024]{3,2,1,0:T(8,128)(2,1)S(1)}, u32[]{:S(2)}, u32[]{:S(2)}) %all-to-all-start.4) | async-done | bytes 1048608 | tf_op jit(solution)/shard_map/all_to_all | solution.py:157
  180.8 1.1 slice_bitcast_fusion.1
  181.9 2.5 %while.168 = (s32[]{:T(128)}, f32[256,448]{0,1:T(8,128)S(1)}, bf16[256,256]{1,0:T(8,128)(2,1)S(1)}, bf16[256,448]{1,0:T(8,128)(2,1)}, s32[]{:T(128)}, /*index=5*/s32[]{:T(128)}, s32[]{:T(128)}, s32[]{:T(128)}) while((s32[]{:T(128)}, f32[256,448]{0,1:T(8,128)S(1)}, bf16[256,256]{1,0:T(8,128)(2,1)S(1)}, ...), condition=%wide.region_17.18_spmd.clone, body=%wide.region_16.17_spmd.clone.sunk | while | flops 29589512 | bytes 1115788 | solution.py:71
  181.9 1.2 convolution_add_fusion.23
  183.2 1.2 convolution_add_fusion.23
  184.5 0.8 convert_reduce_fusion
  185.3 3.3 %all-to-all-start.5 = ((f32[4,8,1024]{2,1,0:T(8,128)}), f32[4,8,1024]{2,1,0:T(8,128)S(1)}, u32[]{:S(2)}, u32[]{:S(2)}) async-start(f32[4,8,1024]{2,1,0:T(8,128)} %convert_reduce_fusion), calls=%async_computation.5 | async-start | bytes 262144 | tf_op jit(solution)/shard_map/all_to_all | solution.py:167
  188.6 2.5 %while.163 = (s32[]{:T(128)}, f32[256,448]{0,1:T(8,128)S(1)}, bf16[256,256]{1,0:T(8,128)(2,1)S(1)}, bf16[256,448]{1,0:T(8,128)(2,1)}, s32[]{:T(128)}, /*index=5*/s32[]{:T(128)}, s32[]{:T(128)}, s32[]{:T(128)}) while((s32[]{:T(128)}, f32[256,448]{0,1:T(8,128)S(1)}, bf16[256,256]{1,0:T(8,128)(2,1)S(1)}, bf16[256,448]{1,0:T(8,128)(2,1)}, ...), condition=%wide.region_19.20_spmd, body=%wide.region_18.19_spmd.sunk | while | flops 29474820 | bytes 1115267 | solution.py:71
  188.7 1.2 convolution_add_fusion.18
  189.9 1.2 convolution_add_fusion.18
  191.1 2.5 %while.164 = (s32[]{:T(128)}, f32[256,448]{0,1:T(8,128)S(1)}, bf16[256,256]{1,0:T(8,128)(2,1)S(1)}, bf16[256,448]{1,0:T(8,128)(2,1)}, s32[]{:T(128)}, /*index=5*/s32[]{:T(128)}, s32[]{:T(128)}, s32[]{:T(128)}) while((s32[]{:T(128)}, f32[256,448]{0,1:T(8,128)S(1)}, bf16[256,256]{1,0:T(8,128)(2,1)S(1)}, bf16[256,448]{1,0:T(8,128)(2,1)}, ...), condition=%wide.region_21.22_spmd, body=%wide.region_20.21_spmd.sunk | while | flops 29474820 | bytes 1115267 | solution.py:71
  191.2 1.2 convolution_add_fusion.19
  192.4 1.2 convolution_add_fusion.19
  193.7 0.9 all-to-all-done.5
  194.5 9.7 %collective-permute-start.8 = (bf16[8,1024]{1,0:T(8,128)(2,1)S(1)}, bf16[8,1024]{1,0:T(8,128)(2,1)S(1)}, u32[]{:S(2)}, u32[]{:S(2)}) collective-permute-start(bf16[8,1024]{1,0:T(8,128)(2,1)S(1)} %reduce_sum.19), channel_id=1, source_target_pairs={{0,512},{256,768},{512,0},{768,256},{1,513},{257,769},{513,1},{769... | collective-permute-start | bytes 49160 | tf_op jit(solution)/shard_map/ppermute | solution.py:168
  204.2 2.5 %while.162 = (s32[]{:T(128)}, f32[256,448]{0,1:T(8,128)S(1)}, bf16[256,256]{1,0:T(8,128)(2,1)S(1)}, bf16[256,448]{1,0:T(8,128)(2,1)}, s32[]{:T(128)}, /*index=5*/s32[]{:T(128)}, s32[]{:T(128)}, s32[]{:T(128)}) while((s32[]{:T(128)}, f32[256,448]{0,1:T(8,128)S(1)}, bf16[256,256]{1,0:T(8,128)(2,1)S(1)}, bf16[256,448]{1,0:T(8,128)(2,1)}, ...), condition=%wide.region_15.16_spmd, body=%wide.region_14.15_spmd.sunk | while | flops 29474820 | bytes 1115267 | solution.py:71
  204.3 1.2 convolution_add_fusion.17
  205.5 1.2 convolution_add_fusion.17
  206.7 2.1 collective-permute-done.8
  208.9 1.0 broadcast_select_fusion.2
  210.8 1.9 collective-permute-start.9
  213.6 1.0 collective-permute-done.9
  214.6 0.8 add_convert_fusion
  215.4 4.2 %all-to-all-start.6 = ((bf16[4,64,448]{2,1,0:T(8,128)(2,1)}), bf16[4,64,448]{2,1,0:T(8,128)(2,1)S(1)}, u32[]{:S(2)}, u32[]{:S(2)}) async-start(bf16[4,64,448]{2,1,0:T(8,128)(2,1)} %bitcast.31), calls=%async_computation.6 | async-start | bytes 524288 | tf_op jit(solution)/shard_map/all_to_all | solution.py:175
  221.0 7.8 %all-to-all-done.6 = bf16[4,64,448]{2,1,0:T(8,128)(2,1)S(1)} async-done(((bf16[4,64,448]{2,1,0:T(8,128)(2,1)}), bf16[4,64,448]{2,1,0:T(8,128)(2,1)S(1)}, u32[]{:S(2)}, u32[]{:S(2)}) %all-to-all-start.6) | async-done | bytes 229408 | tf_op jit(solution)/shard_map/all_to_all | solution.py:175
  229.6 0.8 slice_multiply_fusion
  (89 shorter events, 24.6 us)
Async XLA Ops:
  2.1 22.9 %all-to-all-start = ((bf16[16,8,1024]{2,1,0:T(8,128)(2,1)}), bf16[16,8,1024]{2,1,0:T(8,128)(2,1)S(1)}, u32[]{:S(2)}, u32[]{:S(2)}) async-start(bf16[16,8,1024]{2,1,0:T(8,128)(2,1)} %broadcast_in_dim.52), calls=%async_computation | async-start | bytes 524288 | tf_op jit(solution)/shard_map/all_to_all | solution.py:47
  27.9 4.7 %collective-permute-start = (f32[64,1792]{1,0:T(8,128)S(1)}, f32[64,1792]{1,0:T(8,128)S(1)}, u32[]{:S(2)}, u32[]{:S(2)}) collective-permute-start(f32[64,1792]{1,0:T(8,128)S(1)} %fusion.41), channel_id=1, source_target_pairs={{0,16},{16,0},{1,17},{17,1},{2,18},{18,2},{3,19},{19,3},{4,20},{20... | collective-permute-start | bytes 1376264 | tf_op jit(solution)/shard_map/ppermute | solution.py:97
  29.8 2.9 %copy-start = (bf16[8,1024]{1,0:T(8,128)(2,1)S(1)}, bf16[8,1024]{1,0:T(8,128)(2,1)}, u32[]{:S(2)}) copy-start(bf16[8,1024]{1,0:T(8,128)(2,1)} %param.30) | copy-start | bytes 49156
  33.9 31.6 %collective-permute-start.1 = (bf16[32,1792]{1,0:T(8,128)(2,1)S(1)}, bf16[32,1792]{1,0:T(8,128)(2,1)S(1)}, u32[]{:S(2)}, u32[]{:S(2)}) collective-permute-start(bf16[32,1792]{1,0:T(8,128)(2,1)S(1)} %slice.86), channel_id=1, source_target_pairs={{0,32},{32,0},{1,33},{33,1},{2,34},{34,2},{3,35},{35,3},{4,36},{36... | collective-permute-start | bytes 344072 | tf_op jit(solution)/shard_map/ppermute | solution.py:102
  53.8 29.5 %all-to-all-start.1 = ((bf16[16,8,256]{2,1,0:T(8,128)(2,1)}), bf16[16,8,256]{2,1,0:T(8,128)(2,1)S(1)}, u32[]{:S(2)}, u32[]{:S(2)}) async-start(bf16[16,8,256]{2,1,0:T(8,128)(2,1)} %bitcast.9), calls=%async_computation.1 | async-start | bytes 131072 | tf_op jit(solution)/shard_map/all_to_all | solution.py:103
  62.6 20.7 %copy-start.1 = (bf16[32,896]{1,0:T(8,128)(2,1)S(1)}, bf16[32,896]{1,0:T(8,128)(2,1)}, u32[]{:S(2)}) copy-start(bf16[32,896]{1,0:T(8,128)(2,1)} %param.35) | copy-start | bytes 172036
  85.0 13.1 %all-to-all-start.2 = ((bf16[8,32,448]{2,1,0:T(8,128)(2,1)}), bf16[8,32,448]{2,1,0:T(8,128)(2,1)S(1)}, u32[]{:S(2)}, u32[]{:S(2)}) async-start(bf16[8,32,448]{2,1,0:T(8,128)(2,1)} %bitcast.12), calls=%async_computation.2 | async-start | bytes 524288 | tf_op jit(solution)/shard_map/all_to_all | solution.py:119
  100.0 23.1 %collective-permute-start.2 = (bf16[256,448]{1,0:T(8,128)(2,1)}, bf16[256,448]{1,0:T(8,128)(2,1)}, u32[]{:S(2)}, u32[]{:S(2)}) collective-permute-start(bf16[256,448]{1,0:T(8,128)(2,1)} %bitcast.15), channel_id=1, source_target_pairs={{0,256},{16,816},{64,320},{80,880},{128,384},{144,944},{192,448},{... | collective-permute-start | bytes 688136 | tf_op jit(solution)/shard_map/ppermute | solution.py:123
  103.9 26.1 %all-to-all-start.3 = ((bf16[16,16,8,256]{3,2,1,0:T(8,128)(2,1)}), bf16[16,16,8,256]{3,2,1,0:T(8,128)(2,1)S(1)}, u32[]{:S(2)}, u32[]{:S(2)}) async-start(bf16[16,16,8,256]{3,2,1,0:T(8,128)(2,1)} %broadcast_in_dim.61), calls=%async_computation.3 | async-start | bytes 2097152 | tf_op jit(solution)/shard_map/all_to_all | solution.py:47
  123.1 19.5 %collective-permute-start.3 = (bf16[256,448]{1,0:T(8,128)(2,1)}, bf16[256,448]{1,0:T(8,128)(2,1)}, u32[]{:S(2)}, u32[]{:S(2)}) collective-permute-start(bf16[256,448]{1,0:T(8,128)(2,1)} %collective-permute-done.2), channel_id=1, source_target_pairs={{0,256},{16,816},{64,320},{80,880},{128,384},{144,944},{192,448},{... | collective-permute-start | bytes 688136 | tf_op jit(solution)/shard_map/ppermute | solution.py:140
  142.6 8.1 %collective-permute-start.5 = (bf16[256,448]{1,0:T(8,128)(2,1)}, bf16[256,448]{1,0:T(8,128)(2,1)}, u32[]{:S(2)}, u32[]{:S(2)}) collective-permute-start(bf16[256,448]{1,0:T(8,128)(2,1)} %collective-permute-done.3), channel_id=1, source_target_pairs={{0,16},{16,0},{1,17},{17,1},{2,18},{18,2},{3,19},{19,3},{4,20},{20... | collective-permute-start | bytes 688136 | tf_op jit(solution)/shard_map/ppermute | solution.py:145
  144.6 25.4 %collective-permute-start.4 = (bf16[256,448]{1,0:T(8,128)(2,1)}, bf16[256,448]{1,0:T(8,128)(2,1)}, u32[]{:S(2)}, u32[]{:S(2)}) collective-permute-start(bf16[256,448]{1,0:T(8,128)(2,1)} %collective-permute-done.3), channel_id=1, source_target_pairs={{0,256},{16,816},{64,320},{80,880},{128,384},{144,944},{192,448},{... | collective-permute-start | bytes 688136 | tf_op jit(solution)/shard_map/ppermute | solution.py:144
  153.8 20.4 %collective-permute-start.6 = (bf16[4,256,256]{2,1,0:T(8,128)(2,1)S(1)}, bf16[4,256,256]{2,1,0:T(8,128)(2,1)}, u32[]{:S(2)}, u32[]{:S(2)}) collective-permute-start(bf16[4,256,256]{2,1,0:T(8,128)(2,1)S(1)} %get-tuple-element.943), channel_id=1, source_target_pairs={{0,16},{16,0},{1,17},{17,1},{2,18},{18,2},{3,19},{19,3},{4,20},{20... | collective-permute-start | bytes 1572872 | tf_op jit(solution)/shard_map/ppermute | solution.py:158
  158.1 22.7 %all-to-all-start.4 = ((bf16[16,4,8,1024]{3,2,1,0:T(8,128)(2,1)}), bf16[16,4,8,1024]{3,2,1,0:T(8,128)(2,1)S(1)}, u32[]{:S(2)}, u32[]{:S(2)}) async-start(bf16[16,4,8,1024]{3,2,1,0:T(8,128)(2,1)} %bitcast.23), calls=%async_computation.4 | async-start | bytes 2097152 | tf_op jit(solution)/shard_map/all_to_all | solution.py:157
  170.1 36.7 %collective-permute-start.7 = (bf16[256,448]{1,0:T(8,128)(2,1)}, bf16[256,448]{1,0:T(8,128)(2,1)}, u32[]{:S(2)}, u32[]{:S(2)}) collective-permute-start(bf16[256,448]{1,0:T(8,128)(2,1)} %collective-permute-done.4), channel_id=1, source_target_pairs={{0,256},{16,816},{64,320},{80,880},{128,384},{144,944},{192,448},{... | collective-permute-start | bytes 688136 | tf_op jit(solution)/shard_map/ppermute | solution.py:162
  185.3 9.2 %all-to-all-start.5 = ((f32[4,8,1024]{2,1,0:T(8,128)}), f32[4,8,1024]{2,1,0:T(8,128)S(1)}, u32[]{:S(2)}, u32[]{:S(2)}) async-start(f32[4,8,1024]{2,1,0:T(8,128)} %convert_reduce_fusion), calls=%async_computation.5 | async-start | bytes 262144 | tf_op jit(solution)/shard_map/all_to_all | solution.py:167
  194.5 14.3 %collective-permute-start.8 = (bf16[8,1024]{1,0:T(8,128)(2,1)S(1)}, bf16[8,1024]{1,0:T(8,128)(2,1)S(1)}, u32[]{:S(2)}, u32[]{:S(2)}) collective-permute-start(bf16[8,1024]{1,0:T(8,128)(2,1)S(1)} %reduce_sum.19), channel_id=1, source_target_pairs={{0,512},{256,768},{512,0},{768,256},{1,513},{257,769},{513,1},{769... | collective-permute-start | bytes 49160 | tf_op jit(solution)/shard_map/ppermute | solution.py:168
  210.8 3.8 %collective-permute-start.9 = (f32[256,448]{1,0:T(8,128)S(1)}, f32[256,448]{1,0:T(8,128)S(1)}, u32[]{:S(2)}, u32[]{:S(2)}) collective-permute-start(f32[256,448]{1,0:T(8,128)S(1)} %copy.38), channel_id=1, source_target_pairs={{0,16},{16,0},{1,17},{17,1},{2,18},{18,2},{3,19},{19,3},{4,20},{20... | collective-permute-start | bytes 1376264 | tf_op jit(solution)/shard_map/ppermute | solution.py:172
  215.4 13.4 %all-to-all-start.6 = ((bf16[4,64,448]{2,1,0:T(8,128)(2,1)}), bf16[4,64,448]{2,1,0:T(8,128)(2,1)S(1)}, u32[]{:S(2)}, u32[]{:S(2)}) async-start(bf16[4,64,448]{2,1,0:T(8,128)(2,1)} %bitcast.31), calls=%async_computation.6 | async-start | bytes 524288 | tf_op jit(solution)/shard_map/all_to_all | solution.py:175

commit v6 on v5

--- a/solution.py
+++ b/solution.py
@@ -7,12 +7,12 @@
 F32 = jnp.float32
 
 TEAM = 4
-TURNS = 16
+TURNS = 12
 TURNS0 = 8
+TURNS1 = 4
 GROUPS = 16 // TEAM
 PLACES = 2 * GROUPS
 STEPS = PLACES // 2
-DP = ("group", "member")
 Z = ("group", "member", "half", "core")
 
 
@@ -48,7 +48,7 @@
 
 
 def in_turns(x, after, turns=2):
-    part = x.shape[0] // turns
+    part = -(-x.shape[0] // turns)
 
     def turn(i, y):
         piece = lax.dynamic_slice_in_dim(x, i * part, part, axis=0)
@@ -84,7 +84,6 @@
     replica = gather_col(tokens, columns).reshape(2, 2, columns // 4 * held, features)
 
     spread = tokens.reshape(held, GROUPS, block).transpose(1, 0, 2)
-    spread = jnp.broadcast_to(spread[:, None], (GROUPS, TEAM, held, block)).reshape(16, held, block)
 
     both_weights = jnp.concatenate([masked(gate_weight, mask_gate), masked(up_weight, mask_up)], axis=1)
     replica = jnp.where(half == 0, replica, replica[::-1])
@@ -100,7 +99,7 @@
     summed, spread, both_weights = lax.optimization_barrier((summed, spread, both_weights))
 
     arrived = lax.ppermute(summed[rows:].astype(BF16), "half", SWAP)
-    spread = lax.all_to_all(in_turns(spread, summed[:1, :1], 16), DP, 0, 0)
+    spread = lax.all_to_all(in_turns(spread, summed[:1, :1], TURNS1), "group", 0, 0)
     chosen = lax.dynamic_slice_in_dim(both_weights, member * share, share, axis=1)
     masked_share = in_turns(chosen, summed[:1, :1], TURNS0)
     arrived, spread, masked_share = lax.optimization_barrier((arrived, spread, masked_share))
@@ -115,9 +114,15 @@
     grad_up_act = (cotangent * activation).astype(BF16)
 
     shares = jnp.concatenate([grad_gate_act, grad_up_act], axis=1).reshape(rows, TEAM, share).transpose(1, 0, 2)
-    shares = jnp.broadcast_to(shares[:, None], (TEAM, 2, rows, share)).reshape(2 * TEAM, rows, share)
-    own = lax.all_to_all(shares, ("member", "core"), 0, 0).reshape(TEAM, 2, rows, share)
-    own = own.transpose(1, 0, 2, 3).reshape(2 * TEAM * rows, share)
+    spread = spread.reshape(rows, GROUPS * held * block // rows)
+    begin = -(-share // 128) * 128
+    shares = jnp.pad(shares, ((0, 0), (0, 0), (0, begin - share)))
+    shares = jnp.concatenate([shares, jnp.broadcast_to(spread, (TEAM, *spread.shape))], axis=2)
+    shares = jnp.broadcast_to(shares[:, None], (TEAM, 2, *shares.shape[1:])).reshape(2 * TEAM, rows, shares.shape[2])
+    own = lax.all_to_all(shares, ("member", "core"), 0, 0).reshape(TEAM, 2, rows, shares.shape[2])
+    spread = jnp.where(core == 0, own[:, 0, :, begin:], own[:, 1, :, begin:])
+    spread = spread.reshape(TEAM, GROUPS, held, block).transpose(1, 0, 2, 3).reshape(16, held, block)
+    own = own[..., :share].transpose(1, 0, 2, 3).reshape(2 * TEAM * rows, share)
     own, spread = lax.optimization_barrier((own, spread))
 
     first = lax.ppermute(own, Z, RING)
@@ -162,7 +167,10 @@
     fourth = lax.ppermute(third, Z, RING)
     my_total, part, their_rows = lax.optimization_barrier((my_total, part, their_rows))
     my_total = add(2, my_rows, third, my_total)
-    their_total = add(2, their_rows, third, add(1, their_rows, second, add(0, their_rows, first)))
+    their_total = sum(
+        lax.dot_general(their_rows[step], met, (((0,), (0,)), ((), ())), preferred_element_type=F32)
+        for step, met in enumerate((first, second, third))
+    )
     reduced = jnp.sum(part.astype(F32), axis=0)
     reduced = jnp.sum(lax.all_to_all(reduced, "member", 0, 0), axis=0).astype(BF16)
     swapped = lax.ppermute(reduced, "group", FAR_GROUP)

time: 234 us -> 231 us (0.987)
  starting transfers between devices: 109 us -> 115 us
  waiting for transfers between devices: 55.2 us -> 49.2 us
  matrix products: 24.5 us -> 21 us
    dynamic_slice x0 -> x12, local copies, waits for them, and re-layouts: none -> 9.29 us  [turn(): piece = lax.dynamic_slice_in_dim(x, i * part, part, axis=0)]
    dot_general x18 -> x12, matrix products: 18.2 us -> 10.8 us  [turn(): lax.dot_general(lax.dynamic_slice_in_dim(rows, i * part, part, axis=0), l...]
    dynamic_update_slice x26 -> x22, local copies, waits for them, and re-layouts: 11.7 us -> 4.85 us  [turn(): return lax.dynamic_update_slice_in_dim(y, piece, i * part, axis=0)]
    ppermute x1, starting transfers between devices: 2.01 us -> 8.21 us  [body(): across = lax.ppermute(second, 'core', SWAP)]
    ppermute x1, waiting for transfers between devices: 9.24 us -> 5.34 us  [body(): second = lax.ppermute(first, Z, RING)]
    dot_general x0 -> x3, matrix products: none -> 3.87 us  [body(): lax.dot_general(their_rows[step], met, (((0,), (0,)), ((), ())), preferre...]
    ppermute x1, starting transfers between devices: 6.01 us -> 2.41 us  [body(): third = lax.ppermute(second, Z, RING)]
    all_to_all x1, waiting for transfers between devices: 17.8 us -> 14.5 us  [body(): lax.all_to_all(in_turns(spread, summed[:1, :1], TURNS1), 'group', 0, 0)]
where the time goes in v6:
time: 231 us; the launch traced here: 228 us
  starting transfers between devices  115 us (50%)
  waiting for transfers between devices  49.2 us (21%)
  local copies, waits for them, and re-layouts  26.9 us (12%)
  matrix products  21 us (9%)
  other arithmetic  13.6 us (6%)
    all_to_all x2, starting transfers between devices, gather_col(): lax.all_to_all(jnp.broadcast_to(x[None], (count, *x.shape)), 'col', 0, 0)  23.5 us
    ppermute x1, starting transfers between devices, body(): arrived = lax.ppermute(summed[rows:].astype(BF16), 'half', SWAP)  19.9 us
    all_to_all x1, waiting for transfers between devices, body(): lax.all_to_all(in_turns(spread, summed[:1, :1], TURNS1), 'group', 0, 0)  14.5 us
    all_to_all x1, waiting for transfers between devices, body(): lax.all_to_all(shares, ('member', 'core'), 0, 0)  12.5 us
    ppermute x1, starting transfers between devices, body(): swapped = lax.ppermute(reduced, 'group', FAR_GROUP)  11.4 us
    dot_general x12, matrix products, turn(): lax.dot_general(lax.dynamic_slice_in_dim(rows, i * part, part, axis=0), l...  10.8 us
    dynamic_slice x12, local copies, waits for them, and re-layouts, turn(): piece = lax.dynamic_slice_in_dim(x, i * part, part, axis=0)  9.29 us
    ppermute x1, starting transfers between devices, body(): across = lax.ppermute(second, 'core', SWAP)  8.21 us
  transfers between devices with their start and end apart: 17, of which 9 were waited for; matrix products, arithmetic and copies ran while one was open for 22% of the time, Pallas kernels for 0%

profile of v6, /device:TPU:6, one launch (start us, length us, event | category | flops | bytes accessed | tf_op | source)
XLA Modules:
  0.0 227.6 jit_solution(8378740199455605715)
XLA Ops:
  0.6 1.4 broadcast_in_dim.52
  2.1 16.5 %all-to-all-start = ((bf16[16,8,1024]{2,1,0:T(8,128)(2,1)}), bf16[16,8,1024]{2,1,0:T(8,128)(2,1)S(1)}, u32[]{:S(2)}, u32[]{:S(2)}) async-start(bf16[16,8,1024]{2,1,0:T(8,128)(2,1)} %broadcast_in_dim.52), calls=%async_computation | async-start | bytes 524288 | tf_op jit(solution)/shard_map/all_to_all | solution.py:47
  20.3 2.4 %bitcast_multiply_fusion = (bf16[1024,896]{1,0:T(8,128)(2,1)S(1)}, bf16[1024,896]{1,0:T(8,128)(2,1)S(1)}) fusion(bf16[1024,896]{1,0:T(8,128)(2,1)} %param.26, bf16[8,896]{1,0:T(8,128)(2,1)S(1)} %broadcast_bitcast_fusion, bf16[1024,896]{1,0:T(8,128)(2,1)} %param.25, bf16[8,896]{1,0:T(8,128)(2,1)S(1)} %broadcast_bitcast_fusion.1), kind=kLoop, calls=%fused_computation.29 | loop fusion | flops 1835008 | bytes 7368704 | tf_op jit(solution)/shard_map/mul | solution.py:43
  22.7 2.0 pad_maximum_fusion
  25.1 2.8 %fusion.44 = f32[64,1792]{1,0:T(8,128)S(1)} fusion(bf16[64,1024]{1,0:T(8,128)(2,1)S(1)} %bitcast.83, bf16[1024,1792]{1,0:T(8,128)(2,1)} %pad_maximum_fusion), kind=kOutput, calls=%fused_computation.96 | convolution fusion | flops 234881024 | bytes 4259840 | tf_op jit(solution)/shard_map/dot_general | solution.py:94
  27.9 1.9 collective-permute-start
  29.8 2.8 %fusion.43 = f32[64,1792]{1,0:T(8,128)S(1)} fusion(bf16[64,1024]{1,0:T(8,128)(2,1)S(1)} %bitcast.82, bf16[1024,1792]{1,0:T(8,128)(2,1)} %pad_maximum_fusion), kind=kOutput, calls=%fused_computation.95 | convolution fusion | flops 234881024 | bytes 4259840 | tf_op jit(solution)/shard_map/dot_general | solution.py:94
  33.3 19.9 %collective-permute-start.1 = (bf16[32,1792]{1,0:T(8,128)(2,1)S(1)}, bf16[32,1792]{1,0:T(8,128)(2,1)S(1)}, u32[]{:S(2)}, u32[]{:S(2)}) collective-permute-start(bf16[32,1792]{1,0:T(8,128)(2,1)S(1)} %slice.98), channel_id=1, source_target_pairs={{0,32},{32,0},{1,33},{33,1},{2,34},{34,2},{3,35},{35,3},{4,36},{36... | collective-permute-start | bytes 344072 | tf_op jit(solution)/shard_map/ppermute | solution.py:101
  53.2 7.3 %all-to-all-start.1 = ((bf16[4,8,256]{2,1,0:T(8,128)(2,1)}), bf16[4,8,256]{2,1,0:T(8,128)(2,1)S(1)}, u32[]{:S(2)}, u32[]{:S(2)}) async-start(bf16[4,8,256]{2,1,0:T(8,128)(2,1)} %bitcast.8), calls=%async_computation.1 | async-start | bytes 32768 | tf_op jit(solution)/shard_map/all_to_all | solution.py:102
  60.5 1.8 constant_dynamic-slice_fusion.3
  63.3 14.5 %all-to-all-done.1 = bf16[4,8,256]{2,1,0:T(8,128)(2,1)S(1)} async-done(((bf16[4,8,256]{2,1,0:T(8,128)(2,1)}), bf16[4,8,256]{2,1,0:T(8,128)(2,1)S(1)}, u32[]{:S(2)}, u32[]{:S(2)}) %all-to-all-start.1) | async-done | bytes 16416 | tf_op jit(solution)/shard_map/all_to_all | solution.py:102
  78.9 0.8 broadcast_in_dim.58
  79.7 3.5 %all-to-all-start.2 = ((bf16[8,32,768]{2,1,0:T(8,128)(2,1)}), bf16[8,32,768]{2,1,0:T(8,128)(2,1)S(1)}, u32[]{:S(2)}, u32[]{:S(2)}) async-start(bf16[8,32,768]{2,1,0:T(8,128)(2,1)} %bitcast.12), calls=%async_computation.2 | async-start | bytes 786432 | tf_op jit(solution)/shard_map/all_to_all | solution.py:122
  83.2 12.5 %all-to-all-done.2 = bf16[8,32,768]{2,1,0:T(8,128)(2,1)S(1)} async-done(((bf16[8,32,768]{2,1,0:T(8,128)(2,1)}), bf16[8,32,768]{2,1,0:T(8,128)(2,1)S(1)}, u32[]{:S(2)}, u32[]{:S(2)}) %all-to-all-start.2) | async-done | bytes 393248 | tf_op jit(solution)/shard_map/all_to_all | solution.py:122
  96.4 1.2 slice.83
  97.6 2.5 %collective-permute-start.2 = (bf16[256,448]{1,0:T(8,128)(2,1)}, bf16[256,448]{1,0:T(8,128)(2,1)}, u32[]{:S(2)}, u32[]{:S(2)}) collective-permute-start(bf16[256,448]{1,0:T(8,128)(2,1)} %bitcast.15), channel_id=1, source_target_pairs={{0,256},{16,816},{64,320},{80,880},{128,384},{144,944},{192,448},{... | collective-permute-start | bytes 688136 | tf_op jit(solution)/shard_map/ppermute | solution.py:128
  100.9 1.1 broadcast_in_dim.62
  102.0 7.0 %all-to-all-start.3 = ((bf16[16,16,8,256]{3,2,1,0:T(8,128)(2,1)}), bf16[16,16,8,256]{3,2,1,0:T(8,128)(2,1)S(1)}, u32[]{:S(2)}, u32[]{:S(2)}) async-start(bf16[16,16,8,256]{3,2,1,0:T(8,128)(2,1)} %broadcast_in_dim.62), calls=%async_computation.3 | async-start | bytes 2097152 | tf_op jit(solution)/shard_map/all_to_all | solution.py:47
  109.7 14.4 %while.119 = (s32[]{:T(128)}, bf16[256,448]{1,0:T(8,128)(2,1)S(1)}, bf16[256,448]{1,0:T(8,128)(2,1)}, s32[]{:T(128)}, s32[]{:T(128)}, /*index=5*/s32[]{:T(128)}, s32[]{:T(128)}) while((s32[]{:T(128)}, bf16[256,448]{1,0:T(8,128)(2,1)S(1)}, bf16[256,448]{1,0:T(8,128)(2,1)}, s32[]{:T(128)}, s32[]{:T(128)}, /*index=5*/s32[]{:T(128)}, ...), condition=%wide.region_5.6_spmd, body=%wide.region_4.5_spmd.sunk | while | flops 6 | bytes 78979 | solution.py:57
  109.7 0.8 constant_dynamic-slice_fusion.5
  110.9 0.8 constant_dynamic-slice_fusion.5
  112.1 0.8 constant_dynamic-slice_fusion.5
  113.3 0.8 constant_dynamic-slice_fusion.5
  114.5 0.8 constant_dynamic-slice_fusion.5
  115.7 0.8 constant_dynamic-slice_fusion.5
  116.9 0.8 constant_dynamic-slice_fusion.5
  118.2 0.8 constant_dynamic-slice_fusion.5
  119.4 0.8 constant_dynamic-slice_fusion.5
  120.6 0.8 constant_dynamic-slice_fusion.5
  124.1 7.3 %collective-permute-start.3 = (bf16[256,448]{1,0:T(8,128)(2,1)}, bf16[256,448]{1,0:T(8,128)(2,1)}, u32[]{:S(2)}, u32[]{:S(2)}) collective-permute-start(bf16[256,448]{1,0:T(8,128)(2,1)} %collective-permute-done.2), channel_id=1, source_target_pairs={{0,256},{16,816},{64,320},{80,880},{128,384},{144,944},{192,448},{... | collective-permute-start | bytes 688136 | tf_op jit(solution)/shard_map/ppermute | solution.py:145
  132.2 2.6 %while.125 = (s32[]{:T(128)}, f32[256,448]{0,1:T(8,128)S(1)}, bf16[256,256]{1,0:T(8,128)(2,1)S(1)}, bf16[256,448]{1,0:T(8,128)(2,1)}, s32[]{:T(128)}, /*index=5*/s32[]{:T(128)}, s32[]{:T(128)}, s32[]{:T(128)}) while((s32[]{:T(128)}, f32[256,448]{0,1:T(8,128)S(1)}, bf16[256,256]{1,0:T(8,128)(2,1)S(1)}, bf16[256,448]{1,0:T(8,128)(2,1)}, ...), condition=%wide.region_9.10_spmd.clone, body=%wide.region_8.9_spmd.clone.sunk | while | flops 29589512 | bytes 1115788 | solution.py:71
  132.2 1.2 convolution_add_fusion.15
  133.5 1.2 convolution_add_fusion.15
  134.7 5.3 %collective-permute-done.3 = bf16[256,448]{1,0:T(8,128)(2,1)} collective-permute-done((bf16[256,448]{1,0:T(8,128)(2,1)}, bf16[256,448]{1,0:T(8,128)(2,1)}, u32[]{:S(2)}, u32[]{:S(2)}) %collective-permute-start.3) | collective-permute-done | bytes 229408 | tf_op jit(solution)/shard_map/ppermute | solution.py:145
  140.1 8.2 %collective-permute-start.5 = (bf16[256,448]{1,0:T(8,128)(2,1)}, bf16[256,448]{1,0:T(8,128)(2,1)S(1)}, u32[]{:S(2)}, u32[]{:S(2)}) collective-permute-start(bf16[256,448]{1,0:T(8,128)(2,1)} %collective-permute-done.3), channel_id=1, source_target_pairs={{0,16},{16,0},{1,17},{17,1},{2,18},{18,2},{3,19},{19,3},{4,20},{20... | collective-permute-start | bytes 688136 | tf_op jit(solution)/shard_map/ppermute | solution.py:150
  148.3 2.4 %collective-permute-start.4 = (bf16[256,448]{1,0:T(8,128)(2,1)}, bf16[256,448]{1,0:T(8,128)(2,1)}, u32[]{:S(2)}, u32[]{:S(2)}) collective-permute-start(bf16[256,448]{1,0:T(8,128)(2,1)} %collective-permute-done.3), channel_id=1, source_target_pairs={{0,256},{16,816},{64,320},{80,880},{128,384},{144,944},{192,448},{... | collective-permute-start | bytes 688136 | tf_op jit(solution)/shard_map/ppermute | solution.py:149
  150.7 1.0 broadcast_select_fusion.3
  152.6 1.3 reverse_select_fusion
  153.9 2.2 collective-permute-start.6
  156.1 7.2 %all-to-all-start.4 = ((bf16[16,4,8,1024]{3,2,1,0:T(8,128)(2,1)}), bf16[16,4,8,1024]{3,2,1,0:T(8,128)(2,1)S(1)}, u32[]{:S(2)}, u32[]{:S(2)}) async-start(bf16[16,4,8,1024]{3,2,1,0:T(8,128)(2,1)} %bitcast.26), calls=%async_computation.4 | async-start | bytes 2097152 | tf_op jit(solution)/shard_map/all_to_all | solution.py:162
  163.4 4.7 %while.121 = (s32[]{:T(128)}, f32[256,448]{0,1:T(8,128)S(1)}, bf16[256,256]{1,0:T(8,128)(2,1)S(1)}, bf16[256,448]{1,0:T(8,128)(2,1)}, s32[]{:T(128)}, /*index=5*/s32[]{:T(128)}, s32[]{:T(128)}, s32[]{:T(128)}) while((s32[]{:T(128)}, f32[256,448]{0,1:T(8,128)S(1)}, bf16[256,256]{1,0:T(8,128)(2,1)S(1)}, bf16[256,448]{1,0:T(8,128)(2,1)}, ...), condition=%wide.region_11.12_spmd, body=%wide.region_10.11_spmd.sunk | while | flops 14794758 | bytes 1016963 | solution.py:71
  163.4 1.2 convolution_add_fusion.11
  164.5 1.2 convolution_add_fusion.11
  165.7 1.2 convolution_add_fusion.11
  166.9 1.2 convolution_add_fusion.11
  168.1 5.8 %collective-permute-start.7 = (bf16[256,448]{1,0:T(8,128)(2,1)}, bf16[256,448]{1,0:T(8,128)(2,1)S(1)}, u32[]{:S(2)}, u32[]{:S(2)}) collective-permute-start(bf16[256,448]{1,0:T(8,128)(2,1)} %collective-permute-done.4), channel_id=1, source_target_pairs={{0,256},{16,816},{64,320},{80,880},{128,384},{144,944},{192,448},{... | collective-permute-start | bytes 688136 | tf_op jit(solution)/shard_map/ppermute | solution.py:167
  173.9 5.2 %all-to-all-done.4 = bf16[16,4,8,1024]{3,2,1,0:T(8,128)(2,1)S(1)} async-done(((bf16[16,4,8,1024]{3,2,1,0:T(8,128)(2,1)}), bf16[16,4,8,1024]{3,2,1,0:T(8,128)(2,1)S(1)}, u32[]{:S(2)}, u32[]{:S(2)}) %all-to-all-start.4) | async-done | bytes 1048608 | tf_op jit(solution)/shard_map/all_to_all | solution.py:162
  179.1 1.3 fusion.25
  180.4 0.8 convert_reduce_fusion
  181.2 5.4 %all-to-all-start.5 = ((f32[4,8,1024]{2,1,0:T(8,128)}), f32[4,8,1024]{2,1,0:T(8,128)S(1)}, u32[]{:S(2)}, u32[]{:S(2)}) async-start(f32[4,8,1024]{2,1,0:T(8,128)} %convert_reduce_fusion), calls=%async_computation.5 | async-start | bytes 262144 | tf_op jit(solution)/shard_map/all_to_all | solution.py:175
  186.6 1.3 fusion.23
  187.9 1.3 fusion.15
  189.2 2.5 %while.122 = (s32[]{:T(128)}, f32[256,448]{0,1:T(8,128)S(1)}, bf16[256,256]{1,0:T(8,128)(2,1)S(1)}, bf16[256,448]{1,0:T(8,128)(2,1)}, s32[]{:T(128)}, /*index=5*/s32[]{:T(128)}, s32[]{:T(128)}, s32[]{:T(128)}) while((s32[]{:T(128)}, f32[256,448]{0,1:T(8,128)S(1)}, bf16[256,256]{1,0:T(8,128)(2,1)S(1)}, bf16[256,448]{1,0:T(8,128)(2,1)}, ...), condition=%wide.region_15.16_spmd, body=%wide.region_14.15_spmd.sunk | while | flops 29474820 | bytes 1115267 | solution.py:71
  189.2 1.2 convolution_add_fusion.12
  190.5 1.2 convolution_add_fusion.12
  191.7 0.8 all-to-all-done.5
  192.6 11.4 %collective-permute-start.8 = (bf16[8,1024]{1,0:T(8,128)(2,1)S(1)}, bf16[8,1024]{1,0:T(8,128)(2,1)S(1)}, u32[]{:S(2)}, u32[]{:S(2)}) collective-permute-start(bf16[8,1024]{1,0:T(8,128)(2,1)S(1)} %reduce_sum.19), channel_id=1, source_target_pairs={{0,512},{256,768},{512,0},{768,256},{1,513},{257,769},{513,1},{769... | collective-permute-start | bytes 49160 | tf_op jit(solution)/shard_map/ppermute | solution.py:176
  204.0 0.9 slice_bitcast_fusion.2
  204.9 2.0 collective-permute-done.8
  207.8 1.9 collective-permute-start.9
  210.7 1.0 collective-permute-done.9
  212.4 4.3 %all-to-all-start.6 = ((bf16[4,64,448]{2,1,0:T(8,128)(2,1)}), bf16[4,64,448]{2,1,0:T(8,128)(2,1)S(1)}, u32[]{:S(2)}, u32[]{:S(2)}) async-start(bf16[4,64,448]{2,1,0:T(8,128)(2,1)} %bitcast.34), calls=%async_computation.6 | async-start | bytes 524288 | tf_op jit(solution)/shard_map/all_to_all | solution.py:183
  218.2 7.8 %all-to-all-done.6 = bf16[4,64,448]{2,1,0:T(8,128)(2,1)S(1)} async-done(((bf16[4,64,448]{2,1,0:T(8,128)(2,1)}), bf16[4,64,448]{2,1,0:T(8,128)(2,1)S(1)}, u32[]{:S(2)}, u32[]{:S(2)}) %all-to-all-start.6) | async-done | bytes 229408 | tf_op jit(solution)/shard_map/all_to_all | solution.py:183
  226.8 0.8 slice_multiply_fusion
  (92 shorter events, 21.1 us)
Async XLA Ops:
  2.1 22.9 %all-to-all-start = ((bf16[16,8,1024]{2,1,0:T(8,128)(2,1)}), bf16[16,8,1024]{2,1,0:T(8,128)(2,1)S(1)}, u32[]{:S(2)}, u32[]{:S(2)}) async-start(bf16[16,8,1024]{2,1,0:T(8,128)(2,1)} %broadcast_in_dim.52), calls=%async_computation | async-start | bytes 524288 | tf_op jit(solution)/shard_map/all_to_all | solution.py:47
  27.9 4.7 %collective-permute-start = (f32[64,1792]{1,0:T(8,128)S(1)}, f32[64,1792]{1,0:T(8,128)S(1)}, u32[]{:S(2)}, u32[]{:S(2)}) collective-permute-start(f32[64,1792]{1,0:T(8,128)S(1)} %fusion.44), channel_id=1, source_target_pairs={{0,16},{16,0},{1,17},{17,1},{2,18},{18,2},{3,19},{19,3},{4,20},{20... | collective-permute-start | bytes 1376264 | tf_op jit(solution)/shard_map/ppermute | solution.py:96
  33.3 44.5 %collective-permute-start.1 = (bf16[32,1792]{1,0:T(8,128)(2,1)S(1)}, bf16[32,1792]{1,0:T(8,128)(2,1)S(1)}, u32[]{:S(2)}, u32[]{:S(2)}) collective-permute-start(bf16[32,1792]{1,0:T(8,128)(2,1)S(1)} %slice.98), channel_id=1, source_target_pairs={{0,32},{32,0},{1,33},{33,1},{2,34},{34,2},{3,35},{35,3},{4,36},{36... | collective-permute-start | bytes 344072 | tf_op jit(solution)/shard_map/ppermute | solution.py:101
  53.2 24.6 %all-to-all-start.1 = ((bf16[4,8,256]{2,1,0:T(8,128)(2,1)}), bf16[4,8,256]{2,1,0:T(8,128)(2,1)S(1)}, u32[]{:S(2)}, u32[]{:S(2)}) async-start(bf16[4,8,256]{2,1,0:T(8,128)(2,1)} %bitcast.8), calls=%async_computation.1 | async-start | bytes 32768 | tf_op jit(solution)/shard_map/all_to_all | solution.py:102
  60.5 17.4 %copy-start = (bf16[32,896]{1,0:T(8,128)(2,1)S(1)}, bf16[32,896]{1,0:T(8,128)(2,1)}, u32[]{:S(2)}) copy-start(bf16[32,896]{1,0:T(8,128)(2,1)} %param.29) | copy-start | bytes 172036
  79.7 15.9 %all-to-all-start.2 = ((bf16[8,32,768]{2,1,0:T(8,128)(2,1)}), bf16[8,32,768]{2,1,0:T(8,128)(2,1)S(1)}, u32[]{:S(2)}, u32[]{:S(2)}) async-start(bf16[8,32,768]{2,1,0:T(8,128)(2,1)} %bitcast.12), calls=%async_computation.2 | async-start | bytes 786432 | tf_op jit(solution)/shard_map/all_to_all | solution.py:122
  97.6 26.5 %collective-permute-start.2 = (bf16[256,448]{1,0:T(8,128)(2,1)}, bf16[256,448]{1,0:T(8,128)(2,1)}, u32[]{:S(2)}, u32[]{:S(2)}) collective-permute-start(bf16[256,448]{1,0:T(8,128)(2,1)} %bitcast.15), channel_id=1, source_target_pairs={{0,256},{16,816},{64,320},{80,880},{128,384},{144,944},{192,448},{... | collective-permute-start | bytes 688136 | tf_op jit(solution)/shard_map/ppermute | solution.py:128
  102.0 29.4 %all-to-all-start.3 = ((bf16[16,16,8,256]{3,2,1,0:T(8,128)(2,1)}), bf16[16,16,8,256]{3,2,1,0:T(8,128)(2,1)S(1)}, u32[]{:S(2)}, u32[]{:S(2)}) async-start(bf16[16,16,8,256]{3,2,1,0:T(8,128)(2,1)} %broadcast_in_dim.62), calls=%async_computation.3 | async-start | bytes 2097152 | tf_op jit(solution)/shard_map/all_to_all | solution.py:47
  124.1 16.0 %collective-permute-start.3 = (bf16[256,448]{1,0:T(8,128)(2,1)}, bf16[256,448]{1,0:T(8,128)(2,1)}, u32[]{:S(2)}, u32[]{:S(2)}) collective-permute-start(bf16[256,448]{1,0:T(8,128)(2,1)} %collective-permute-done.2), channel_id=1, source_target_pairs={{0,256},{16,816},{64,320},{80,880},{128,384},{144,944},{192,448},{... | collective-permute-start | bytes 688136 | tf_op jit(solution)/shard_map/ppermute | solution.py:145
  140.1 10.6 %collective-permute-start.5 = (bf16[256,448]{1,0:T(8,128)(2,1)}, bf16[256,448]{1,0:T(8,128)(2,1)S(1)}, u32[]{:S(2)}, u32[]{:S(2)}) collective-permute-start(bf16[256,448]{1,0:T(8,128)(2,1)} %collective-permute-done.3), channel_id=1, source_target_pairs={{0,16},{16,0},{1,17},{17,1},{2,18},{18,2},{3,19},{19,3},{4,20},{20... | collective-permute-start | bytes 688136 | tf_op jit(solution)/shard_map/ppermute | solution.py:150
  148.3 19.8 %collective-permute-start.4 = (bf16[256,448]{1,0:T(8,128)(2,1)}, bf16[256,448]{1,0:T(8,128)(2,1)}, u32[]{:S(2)}, u32[]{:S(2)}) collective-permute-start(bf16[256,448]{1,0:T(8,128)(2,1)} %collective-permute-done.3), channel_id=1, source_target_pairs={{0,256},{16,816},{64,320},{80,880},{128,384},{144,944},{192,448},{... | collective-permute-start | bytes 688136 | tf_op jit(solution)/shard_map/ppermute | solution.py:149
  153.9 20.0 %collective-permute-start.6 = (bf16[4,256,256]{2,1,0:T(8,128)(2,1)S(1)}, bf16[4,256,256]{2,1,0:T(8,128)(2,1)}, u32[]{:S(2)}, u32[]{:S(2)}) collective-permute-start(bf16[4,256,256]{2,1,0:T(8,128)(2,1)S(1)} %get-tuple-element.706), channel_id=1, source_target_pairs={{0,16},{16,0},{1,17},{17,1},{2,18},{18,2},{3,19},{19,3},{4,20},{20... | collective-permute-start | bytes 1572872 | tf_op jit(solution)/shard_map/ppermute | solution.py:163
  156.1 23.0 %all-to-all-start.4 = ((bf16[16,4,8,1024]{3,2,1,0:T(8,128)(2,1)}), bf16[16,4,8,1024]{3,2,1,0:T(8,128)(2,1)S(1)}, u32[]{:S(2)}, u32[]{:S(2)}) async-start(bf16[16,4,8,1024]{3,2,1,0:T(8,128)(2,1)} %bitcast.26), calls=%async_computation.4 | async-start | bytes 2097152 | tf_op jit(solution)/shard_map/all_to_all | solution.py:162
  168.1 36.8 %collective-permute-start.7 = (bf16[256,448]{1,0:T(8,128)(2,1)}, bf16[256,448]{1,0:T(8,128)(2,1)S(1)}, u32[]{:S(2)}, u32[]{:S(2)}) collective-permute-start(bf16[256,448]{1,0:T(8,128)(2,1)} %collective-permute-done.4), channel_id=1, source_target_pairs={{0,256},{16,816},{64,320},{80,880},{128,384},{144,944},{192,448},{... | collective-permute-start | bytes 688136 | tf_op jit(solution)/shard_map/ppermute | solution.py:167
  181.2 11.3 %all-to-all-start.5 = ((f32[4,8,1024]{2,1,0:T(8,128)}), f32[4,8,1024]{2,1,0:T(8,128)S(1)}, u32[]{:S(2)}, u32[]{:S(2)}) async-start(f32[4,8,1024]{2,1,0:T(8,128)} %convert_reduce_fusion), calls=%async_computation.5 | async-start | bytes 262144 | tf_op jit(solution)/shard_map/all_to_all | solution.py:175
  192.6 14.3 %collective-permute-start.8 = (bf16[8,1024]{1,0:T(8,128)(2,1)S(1)}, bf16[8,1024]{1,0:T(8,128)(2,1)S(1)}, u32[]{:S(2)}, u32[]{:S(2)}) collective-permute-start(bf16[8,1024]{1,0:T(8,128)(2,1)S(1)} %reduce_sum.19), channel_id=1, source_target_pairs={{0,512},{256,768},{512,0},{768,256},{1,513},{257,769},{513,1},{769... | collective-permute-start | bytes 49160 | tf_op jit(solution)/shard_map/ppermute | solution.py:176
  207.8 3.8 %collective-permute-start.9 = (f32[256,448]{1,0:T(8,128)S(1)}, f32[256,448]{1,0:T(8,128)S(1)}, u32[]{:S(2)}, u32[]{:S(2)}) collective-permute-start(f32[256,448]{1,0:T(8,128)S(1)} %copy.42), channel_id=1, source_target_pairs={{0,16},{16,0},{1,17},{17,1},{2,18},{18,2},{3,19},{19,3},{4,20},{20... | collective-permute-start | bytes 1376264 | tf_op jit(solution)/shard_map/ppermute | solution.py:180
  212.4 13.5 %all-to-all-start.6 = ((bf16[4,64,448]{2,1,0:T(8,128)(2,1)}), bf16[4,64,448]{2,1,0:T(8,128)(2,1)S(1)}, u32[]{:S(2)}, u32[]{:S(2)}) async-start(bf16[4,64,448]{2,1,0:T(8,128)(2,1)} %bitcast.34), calls=%async_computation.6 | async-start | bytes 524288 | tf_op jit(solution)/shard_map/all_to_all | solution.py:183

commit v7 on v6

--- a/solution.py
+++ b/solution.py
@@ -7,7 +7,7 @@
 F32 = jnp.float32
 
 TEAM = 4
-TURNS = 12
+TURNS = 14
 TURNS0 = 8
 TURNS1 = 4
 GROUPS = 16 // TEAM
@@ -112,6 +112,11 @@
     cotangent = grad_hidden.astype(F32)
     grad_gate_act = (cotangent * up_proj * sigmoid_gate * (1.0 + gate_proj * (1.0 - sigmoid_gate))).astype(BF16)
     grad_up_act = (cotangent * activation).astype(BF16)
+
+    def kept_blocks(mask):
+        line = (group * TEAM + member) * mask.shape[0] // 16
+        line = lax.dynamic_index_in_dim(mask, line, 0, keepdims=False).astype(F32)
+        return jnp.repeat(line, units // mask.shape[1])
 
     shares = jnp.concatenate([grad_gate_act, grad_up_act], axis=1).reshape(rows, TEAM, share).transpose(1, 0, 2)
     spread = spread.reshape(rows, GROUPS * held * block // rows)
@@ -127,8 +132,9 @@
 
     first = lax.ppermute(own, Z, RING)
     everyone = gather_col(in_turns(spread, own[:1, :1]), columns)
-    own = in_turns(own, own[:1, :1], TURNS)
-    first, own = lax.optimization_barrier((first, own))
+    lines = jnp.stack([kept_blocks(mask_gate), kept_blocks(mask_up)])
+    lines = in_turns(lines.reshape(2 * TURNS, units // TURNS), own[:1, :1], TURNS).reshape(2, units)
+    first, lines = lax.optimization_barrier((first, lines))
 
     everyone = everyone.reshape(2, 2, columns // 4, GROUPS, TEAM, held, block)
     everyone = everyone.transpose(0, 3, 1, 4, 2, 5, 6).reshape(PLACES, 2 * TEAM * rows, block)
@@ -173,8 +179,8 @@
     )
     reduced = jnp.sum(part.astype(F32), axis=0)
     reduced = jnp.sum(lax.all_to_all(reduced, "member", 0, 0), axis=0).astype(BF16)
+    fourth, my_total, their_total, reduced = lax.optimization_barrier((fourth, my_total, their_total, reduced))
     swapped = lax.ppermute(reduced, "group", FAR_GROUP)
-    fourth, my_total, their_total, swapped = lax.optimization_barrier((fourth, my_total, their_total, swapped))
 
     last = jnp.where(core == 0, fourth, own)
     got = lax.ppermute(add(3, their_rows, last, their_total), "core", SWAP)
@@ -183,12 +189,7 @@
     traded = lax.all_to_all(full.astype(BF16).reshape(TEAM, block // TEAM, share), "member", 0, 0)
     grads = traded.transpose(1, 0, 2).reshape(block // TEAM, 2 * units).astype(F32)
 
-    def kept_blocks(mask):
-        line = (group * TEAM + member) * mask.shape[0] // 16
-        line = lax.dynamic_slice_in_dim(mask, line, 1, axis=0).astype(F32)
-        return jnp.repeat(line, units // mask.shape[1], axis=1)
-
-    return (hidden, grad_tokens, grads[:, :units] * kept_blocks(mask_gate), grads[:, units:] * kept_blocks(mask_up))
+    return (hidden, grad_tokens, grads[:, :units] * lines[0], grads[:, units:] * lines[1])
 
 
 def solution(mesh):

time: 231 us -> 213 us (0.922)
  local copies, waits for them, and re-layouts: 26.9 us -> 11.9 us
  starting transfers between devices: 115 us -> 101 us
  waiting for transfers between devices: 49.2 us -> 58.7 us
    dynamic_slice x12 -> x0, local copies, waits for them, and re-layouts: 9.29 us -> none  [turn(): piece = lax.dynamic_slice_in_dim(x, i * part, part, axis=0)]
    all_to_all x1, waiting for transfers between devices: 7.76 us -> 0.01 us  [body(): lax.all_to_all(full.astype(BF16).reshape(TEAM, block // TEAM, share), 'me...]
    ppermute x1, starting transfers between devices: 8.21 us -> 1.91 us  [body(): across = lax.ppermute(second, 'core', SWAP)]
    ppermute x1, starting transfers between devices: 7.29 us -> 1.98 us  [body(): second = lax.ppermute(first, Z, RING)]
    ppermute x1, waiting for transfers between devices: 0.01 us -> 5.31 us  [body(): first = lax.ppermute(own, Z, RING)]
    dynamic_update_slice x22 -> x24, local copies, waits for them, and re-layouts: 4.85 us -> 0.38 us  [turn(): return lax.dynamic_update_slice_in_dim(y, piece, i * part, axis=0)]
    ppermute x1, waiting for transfers between devices: 5.34 us -> 9.47 us  [body(): second = lax.ppermute(first, Z, RING)]
    all_to_all x2, waiting for transfers between devices: 0.19 us -> 4.06 us  [gather_col(): lax.all_to_all(jnp.broadcast_to(x[None], (count, *x.shape)), 'col', 0, 0)]
  transfers between devices with their start and end apart: 17 -> 17, of which waited for: 9 -> 10; matrix products, arithmetic and copies ran while one was open for 22% -> 17% of each run, Pallas kernels for 0% -> 0%
where the time goes in v7:
time: 213 us; the launch traced here: 209 us
  starting transfers between devices  101 us (47%)
  waiting for transfers between devices  58.7 us (28%)
  matrix products  21 us (10%)
  other arithmetic  14.5 us (7%)
  local copies, waits for them, and re-layouts  11.9 us (6%)
    all_to_all x2, starting transfers between devices, gather_col(): lax.all_to_all(jnp.broadcast_to(x[None], (count, *x.shape)), 'col', 0, 0)  23.5 us
    ppermute x1, starting transfers between devices, body(): arrived = lax.ppermute(summed[rows:].astype(BF16), 'half', SWAP)  19.9 us
    all_to_all x1, waiting for transfers between devices, body(): lax.all_to_all(in_turns(spread, summed[:1, :1], TURNS1), 'group', 0, 0)  14.5 us
    all_to_all x1, waiting for transfers between devices, body(): lax.all_to_all(shares, ('member', 'core'), 0, 0)  11.5 us
    dot_general x12, matrix products, turn(): lax.dot_general(lax.dynamic_slice_in_dim(rows, i * part, part, axis=0), l...  10.8 us
    all_to_all x1, starting transfers between devices, body(): part = lax.all_to_all(part, 'col', 0, 0)  9.75 us
    ppermute x1, waiting for transfers between devices, body(): second = lax.ppermute(first, Z, RING)  9.47 us
    ppermute x1, starting transfers between devices, body(): swapped = lax.ppermute(reduced, 'group', FAR_GROUP)  9 us
  transfers between devices with their start and end apart: 17, of which 10 were waited for; matrix products, arithmetic and copies ran while one was open for 17% of the time, Pallas kernels for 0%

profile of v7, /device:TPU:6, one launch (start us, length us, event | category | flops | bytes accessed | tf_op | source)
XLA Modules:
  0.0 209.5 jit_solution(15643780142786389148)
XLA Ops:
  0.6 1.4 broadcast_in_dim.48
  2.1 16.5 %all-to-all-start = ((bf16[16,8,1024]{2,1,0:T(8,128)(2,1)}), bf16[16,8,1024]{2,1,0:T(8,128)(2,1)S(1)}, u32[]{:S(2)}, u32[]{:S(2)}) async-start(bf16[16,8,1024]{2,1,0:T(8,128)(2,1)} %broadcast_in_dim.48), calls=%async_computation | async-start | bytes 524288 | tf_op jit(solution)/shard_map/all_to_all | solution.py:47
  18.6 0.7 convert_element_type.66
  19.4 0.7 convert_element_type.65
  20.3 2.4 %bitcast_multiply_fusion = (bf16[1024,896]{1,0:T(8,128)(2,1)S(1)}, bf16[1024,896]{1,0:T(8,128)(2,1)S(1)}) fusion(bf16[1024,896]{1,0:T(8,128)(2,1)} %param.26, bf16[8,896]{1,0:T(8,128)(2,1)S(1)} %broadcast_bitcast_fusion, bf16[1024,896]{1,0:T(8,128)(2,1)} %param.25, bf16[8,896]{1,0:T(8,128)(2,1)S(1)} %broadcast_bitcast_fusion.1), kind=kLoop, calls=%fused_computation.29 | loop fusion | flops 1835008 | bytes 7368704 | tf_op jit(solution)/shard_map/mul | solution.py:43
  22.7 2.0 pad_maximum_fusion
  25.1 2.8 %fusion.44 = f32[64,1792]{1,0:T(8,128)S(1)} fusion(bf16[64,1024]{1,0:T(8,128)(2,1)S(1)} %bitcast.95, bf16[1024,1792]{1,0:T(8,128)(2,1)} %pad_maximum_fusion), kind=kOutput, calls=%fused_computation.101 | convolution fusion | flops 234881024 | bytes 4259840 | tf_op jit(solution)/shard_map/dot_general | solution.py:94
  27.9 1.9 collective-permute-start
  29.8 2.8 %fusion.43 = f32[64,1792]{1,0:T(8,128)S(1)} fusion(bf16[64,1024]{1,0:T(8,128)(2,1)S(1)} %bitcast.94, bf16[1024,1792]{1,0:T(8,128)(2,1)} %pad_maximum_fusion), kind=kOutput, calls=%fused_computation.100 | convolution fusion | flops 234881024 | bytes 4259840 | tf_op jit(solution)/shard_map/dot_general | solution.py:94
  33.3 19.9 %collective-permute-start.1 = (bf16[32,1792]{1,0:T(8,128)(2,1)S(1)}, bf16[32,1792]{1,0:T(8,128)(2,1)S(1)}, u32[]{:S(2)}, u32[]{:S(2)}) collective-permute-start(bf16[32,1792]{1,0:T(8,128)(2,1)S(1)} %slice.106), channel_id=1, source_target_pairs={{0,32},{32,0},{1,33},{33,1},{2,34},{34,2},{3,35},{35,3},{4,36},{36... | collective-permute-start | bytes 344072 | tf_op jit(solution)/shard_map/ppermute | solution.py:101
  53.2 7.3 %all-to-all-start.1 = ((bf16[4,8,256]{2,1,0:T(8,128)(2,1)}), bf16[4,8,256]{2,1,0:T(8,128)(2,1)S(1)}, u32[]{:S(2)}, u32[]{:S(2)}) async-start(bf16[4,8,256]{2,1,0:T(8,128)(2,1)} %bitcast.8), calls=%async_computation.1 | async-start | bytes 32768 | tf_op jit(solution)/shard_map/all_to_all | solution.py:102
  60.5 1.8 constant_dynamic-slice_fusion.2
  62.3 0.7 broadcast_in_dim.52
  63.3 14.5 %all-to-all-done.1 = bf16[4,8,256]{2,1,0:T(8,128)(2,1)S(1)} async-done(((bf16[4,8,256]{2,1,0:T(8,128)(2,1)}), bf16[4,8,256]{2,1,0:T(8,128)(2,1)S(1)}, u32[]{:S(2)}, u32[]{:S(2)}) %all-to-all-start.1) | async-done | bytes 16416 | tf_op jit(solution)/shard_map/all_to_all | solution.py:102
  77.8 0.7 fusion.33
  78.9 0.8 broadcast_in_dim.54
  79.7 3.5 %all-to-all-start.2 = ((bf16[8,32,768]{2,1,0:T(8,128)(2,1)}), bf16[8,32,768]{2,1,0:T(8,128)(2,1)S(1)}, u32[]{:S(2)}, u32[]{:S(2)}) async-start(bf16[8,32,768]{2,1,0:T(8,128)(2,1)} %bitcast.12), calls=%async_computation.2 | async-start | bytes 786432 | tf_op jit(solution)/shard_map/all_to_all | solution.py:127
  83.2 0.7 fusion.38
  84.2 11.5 %all-to-all-done.2 = bf16[8,32,768]{2,1,0:T(8,128)(2,1)S(1)} async-done(((bf16[8,32,768]{2,1,0:T(8,128)(2,1)}), bf16[8,32,768]{2,1,0:T(8,128)(2,1)S(1)}, u32[]{:S(2)}, u32[]{:S(2)}) %all-to-all-start.2) | async-done | bytes 393248 | tf_op jit(solution)/shard_map/all_to_all | solution.py:127
  96.2 2.5 %collective-permute-start.2 = (bf16[256,448]{1,0:T(8,128)(2,1)S(1)}, bf16[256,448]{1,0:T(8,128)(2,1)}, u32[]{:S(2)}, u32[]{:S(2)}) collective-permute-start(bf16[256,448]{1,0:T(8,128)(2,1)S(1)} %bitcast.89), channel_id=1, source_target_pairs={{0,256},{16,816},{64,320},{80,880},{128,384},{144,944},{192,448},{... | collective-permute-start | bytes 688136 | tf_op jit(solution)/shard_map/ppermute | solution.py:133
  98.8 0.7 broadcast_in_dim.59
  99.5 1.1 broadcast_in_dim.60
  100.6 7.0 %all-to-all-start.3 = ((bf16[16,16,8,256]{3,2,1,0:T(8,128)(2,1)}), bf16[16,16,8,256]{3,2,1,0:T(8,128)(2,1)S(1)}, u32[]{:S(2)}, u32[]{:S(2)}) async-start(bf16[16,16,8,256]{3,2,1,0:T(8,128)(2,1)} %broadcast_in_dim.60), calls=%async_computation.3 | async-start | bytes 2097152 | tf_op jit(solution)/shard_map/all_to_all | solution.py:47
  108.9 5.3 %collective-permute-done.2 = bf16[256,448]{1,0:T(8,128)(2,1)} collective-permute-done((bf16[256,448]{1,0:T(8,128)(2,1)S(1)}, bf16[256,448]{1,0:T(8,128)(2,1)}, u32[]{:S(2)}, u32[]{:S(2)}) %collective-permute-start.2) | collective-permute-done | bytes 229408 | tf_op jit(solution)/shard_map/ppermute | solution.py:133
  114.2 2.0 collective-permute-start.3
  116.2 3.9 %all-to-all-done.3 = bf16[16,16,8,256]{3,2,1,0:T(8,128)(2,1)S(1)} async-done(((bf16[16,16,8,256]{3,2,1,0:T(8,128)(2,1)}), bf16[16,16,8,256]{3,2,1,0:T(8,128)(2,1)S(1)}, u32[]{:S(2)}, u32[]{:S(2)}) %all-to-all-start.3) | async-done | bytes 1048608 | tf_op jit(solution)/shard_map/all_to_all | solution.py:47
  120.9 2.5 %while.125 = (s32[]{:T(128)}, f32[256,448]{0,1:T(8,128)S(1)}, bf16[256,256]{1,0:T(8,128)(2,1)S(1)}, bf16[256,448]{1,0:T(8,128)(2,1)}, s32[]{:T(128)}, /*index=5*/s32[]{:T(128)}, s32[]{:T(128)}, s32[]{:T(128)}) while((s32[]{:T(128)}, f32[256,448]{0,1:T(8,128)S(1)}, bf16[256,256]{1,0:T(8,128)(2,1)S(1)}, bf16[256,448]{1,0:T(8,128)(2,1)}, ...), condition=%wide.region_9.10_spmd.clone, body=%wide.region_8.9_spmd.clone.sunk | while | flops 29589512 | bytes 1115788 | solution.py:71
  120.9 1.2 convolution_add_fusion.15
  122.2 1.2 convolution_add_fusion.15
  123.4 9.5 %collective-permute-done.3 = bf16[256,448]{1,0:T(8,128)(2,1)} collective-permute-done((bf16[256,448]{1,0:T(8,128)(2,1)}, bf16[256,448]{1,0:T(8,128)(2,1)}, u32[]{:S(2)}, u32[]{:S(2)}) %collective-permute-start.3) | collective-permute-done | bytes 229408 | tf_op jit(solution)/shard_map/ppermute | solution.py:151
  132.9 1.9 collective-permute-start.5
  134.8 1.9 collective-permute-start.4
  136.8 1.0 broadcast_select_fusion.3
  137.8 0.7 convolution_convert_fusion
  138.7 1.3 reverse_select_fusion
  140.0 2.7 %collective-permute-start.7 = (bf16[4,256,256]{2,1,0:T(8,128)(2,1)S(1)}, bf16[4,256,256]{2,1,0:T(8,128)(2,1)}, u32[]{:S(2)}, u32[]{:S(2)}) collective-permute-start(bf16[4,256,256]{2,1,0:T(8,128)(2,1)S(1)} %get-tuple-element.706), channel_id=1, source_target_pairs={{0,16},{16,0},{1,17},{17,1},{2,18},{18,2},{3,19},{19,3},{4,20},{20... | collective-permute-start | bytes 1572872 | tf_op jit(solution)/shard_map/ppermute | solution.py:169
  142.7 9.8 %all-to-all-start.4 = ((bf16[16,4,8,1024]{3,2,1,0:T(8,128)(2,1)}), bf16[16,4,8,1024]{3,2,1,0:T(8,128)(2,1)S(1)}, u32[]{:S(2)}, u32[]{:S(2)}) async-start(bf16[16,4,8,1024]{3,2,1,0:T(8,128)(2,1)} %bitcast.28), calls=%async_computation.4 | async-start | bytes 2097152 | tf_op jit(solution)/shard_map/all_to_all | solution.py:168
  152.4 4.7 %while.121 = (s32[]{:T(128)}, f32[256,448]{0,1:T(8,128)S(1)}, bf16[256,256]{1,0:T(8,128)(2,1)S(1)}, bf16[256,448]{1,0:T(8,128)(2,1)}, s32[]{:T(128)}, /*index=5*/s32[]{:T(128)}, s32[]{:T(128)}, s32[]{:T(128)}) while((s32[]{:T(128)}, f32[256,448]{0,1:T(8,128)S(1)}, bf16[256,256]{1,0:T(8,128)(2,1)S(1)}, bf16[256,448]{1,0:T(8,128)(2,1)}, ...), condition=%wide.region_11.12_spmd, body=%wide.region_10.11_spmd.sunk | while | flops 14794758 | bytes 1016963 | solution.py:71
  152.4 1.2 convolution_add_fusion.11
  153.6 1.2 convolution_add_fusion.11
  154.8 1.2 convolution_add_fusion.11
  156.0 1.2 convolution_add_fusion.11
  157.2 4.4 %collective-permute-start.6 = (bf16[256,448]{1,0:T(8,128)(2,1)}, bf16[256,448]{1,0:T(8,128)(2,1)}, u32[]{:S(2)}, u32[]{:S(2)}) collective-permute-start(bf16[256,448]{1,0:T(8,128)(2,1)} %collective-permute-done.4), channel_id=1, source_target_pairs={{0,256},{16,816},{64,320},{80,880},{128,384},{144,944},{192,448},{... | collective-permute-start | bytes 688136 | tf_op jit(solution)/shard_map/ppermute | solution.py:173
  161.6 6.3 %all-to-all-done.4 = bf16[16,4,8,1024]{3,2,1,0:T(8,128)(2,1)S(1)} async-done(((bf16[16,4,8,1024]{3,2,1,0:T(8,128)(2,1)}), bf16[16,4,8,1024]{3,2,1,0:T(8,128)(2,1)S(1)}, u32[]{:S(2)}, u32[]{:S(2)}) %all-to-all-start.4) | async-done | bytes 1048608 | tf_op jit(solution)/shard_map/all_to_all | solution.py:168
  167.9 1.3 fusion.25
  169.2 1.3 fusion.23
  170.5 0.8 convert_reduce_fusion
  171.3 5.0 %all-to-all-start.5 = ((f32[4,8,1024]{2,1,0:T(8,128)}), f32[4,8,1024]{2,1,0:T(8,128)S(1)}, u32[]{:S(2)}, u32[]{:S(2)}) async-start(f32[4,8,1024]{2,1,0:T(8,128)} %convert_reduce_fusion), calls=%async_computation.5 | async-start | bytes 262144 | tf_op jit(solution)/shard_map/all_to_all | solution.py:181
  176.4 1.3 fusion.15
  177.7 2.5 %while.122 = (s32[]{:T(128)}, f32[256,448]{0,1:T(8,128)S(1)}, bf16[256,256]{1,0:T(8,128)(2,1)S(1)}, bf16[256,448]{1,0:T(8,128)(2,1)}, s32[]{:T(128)}, /*index=5*/s32[]{:T(128)}, s32[]{:T(128)}, s32[]{:T(128)}) while((s32[]{:T(128)}, f32[256,448]{0,1:T(8,128)S(1)}, bf16[256,256]{1,0:T(8,128)(2,1)S(1)}, bf16[256,448]{1,0:T(8,128)(2,1)}, ...), condition=%wide.region_13.14_spmd, body=%wide.region_12.13_spmd.sunk | while | flops 29474820 | bytes 1115267 | solution.py:71
  177.7 1.2 convolution_add_fusion.12
  178.9 1.2 convolution_add_fusion.12
  180.2 0.9 slice_bitcast_fusion.2
  181.1 1.2 all-to-all-done.5
  182.3 1.0 broadcast_select_fusion.2
  183.3 0.7 while.124
  184.2 1.9 collective-permute-start.9
  186.1 0.7 while.123
  187.0 1.0 collective-permute-done.9
  188.0 0.8 add_convert_fusion
  188.8 3.9 %all-to-all-start.6 = ((bf16[4,64,448]{2,1,0:T(8,128)(2,1)}), bf16[4,64,448]{2,1,0:T(8,128)(2,1)S(1)}, u32[]{:S(2)}, u32[]{:S(2)}) async-start(bf16[4,64,448]{2,1,0:T(8,128)(2,1)} %bitcast.36), calls=%async_computation.6 | async-start | bytes 524288 | tf_op jit(solution)/shard_map/all_to_all | solution.py:189
  192.7 9.0 %collective-permute-start.8 = (bf16[8,1024]{1,0:T(8,128)(2,1)S(1)}, bf16[8,1024]{1,0:T(8,128)(2,1)S(1)}, u32[]{:S(2)}, u32[]{:S(2)}) collective-permute-start(bf16[8,1024]{1,0:T(8,128)(2,1)S(1)} %reduce_sum.19), channel_id=1, source_target_pairs={{0,512},{256,768},{512,0},{768,256},{1,513},{257,769},{513,1},{769... | collective-permute-start | bytes 49160 | tf_op jit(solution)/shard_map/ppermute | solution.py:183
  201.7 5.4 %collective-permute-done.8 = bf16[8,1024]{1,0:T(8,128)(2,1)S(1)} collective-permute-done((bf16[8,1024]{1,0:T(8,128)(2,1)S(1)}, bf16[8,1024]{1,0:T(8,128)(2,1)S(1)}, u32[]{:S(2)}, u32[]{:S(2)}) %collective-permute-start.8) | collective-permute-done | bytes 16416 | tf_op jit(solution)/shard_map/ppermute | solution.py:183
  208.7 0.8 slice_multiply_fusion
  (88 shorter events, 8.6 us)
Async XLA Ops:
  2.1 22.9 %all-to-all-start = ((bf16[16,8,1024]{2,1,0:T(8,128)(2,1)}), bf16[16,8,1024]{2,1,0:T(8,128)(2,1)S(1)}, u32[]{:S(2)}, u32[]{:S(2)}) async-start(bf16[16,8,1024]{2,1,0:T(8,128)(2,1)} %broadcast_in_dim.48), calls=%async_computation | async-start | bytes 524288 | tf_op jit(solution)/shard_map/all_to_all | solution.py:47
  27.9 4.7 %collective-permute-start = (f32[64,1792]{1,0:T(8,128)S(1)}, f32[64,1792]{1,0:T(8,128)S(1)}, u32[]{:S(2)}, u32[]{:S(2)}) collective-permute-start(f32[64,1792]{1,0:T(8,128)S(1)} %fusion.44), channel_id=1, source_target_pairs={{0,16},{16,0},{1,17},{17,1},{2,18},{18,2},{3,19},{19,3},{4,20},{20... | collective-permute-start | bytes 1376264 | tf_op jit(solution)/shard_map/ppermute | solution.py:96
  33.3 44.5 %collective-permute-start.1 = (bf16[32,1792]{1,0:T(8,128)(2,1)S(1)}, bf16[32,1792]{1,0:T(8,128)(2,1)S(1)}, u32[]{:S(2)}, u32[]{:S(2)}) collective-permute-start(bf16[32,1792]{1,0:T(8,128)(2,1)S(1)} %slice.106), channel_id=1, source_target_pairs={{0,32},{32,0},{1,33},{33,1},{2,34},{34,2},{3,35},{35,3},{4,36},{36... | collective-permute-start | bytes 344072 | tf_op jit(solution)/shard_map/ppermute | solution.py:101
  53.2 24.6 %all-to-all-start.1 = ((bf16[4,8,256]{2,1,0:T(8,128)(2,1)}), bf16[4,8,256]{2,1,0:T(8,128)(2,1)S(1)}, u32[]{:S(2)}, u32[]{:S(2)}) async-start(bf16[4,8,256]{2,1,0:T(8,128)(2,1)} %bitcast.8), calls=%async_computation.1 | async-start | bytes 32768 | tf_op jit(solution)/shard_map/all_to_all | solution.py:102
  60.5 17.4 %copy-start = (bf16[32,896]{1,0:T(8,128)(2,1)S(1)}, bf16[32,896]{1,0:T(8,128)(2,1)}, u32[]{:S(2)}) copy-start(bf16[32,896]{1,0:T(8,128)(2,1)} %param.29) | copy-start | bytes 172036
  79.7 15.9 %all-to-all-start.2 = ((bf16[8,32,768]{2,1,0:T(8,128)(2,1)}), bf16[8,32,768]{2,1,0:T(8,128)(2,1)S(1)}, u32[]{:S(2)}, u32[]{:S(2)}) async-start(bf16[8,32,768]{2,1,0:T(8,128)(2,1)} %bitcast.12), calls=%async_computation.2 | async-start | bytes 786432 | tf_op jit(solution)/shard_map/all_to_all | solution.py:127
  96.2 18.0 %collective-permute-start.2 = (bf16[256,448]{1,0:T(8,128)(2,1)S(1)}, bf16[256,448]{1,0:T(8,128)(2,1)}, u32[]{:S(2)}, u32[]{:S(2)}) collective-permute-start(bf16[256,448]{1,0:T(8,128)(2,1)S(1)} %bitcast.89), channel_id=1, source_target_pairs={{0,256},{16,816},{64,320},{80,880},{128,384},{144,944},{192,448},{... | collective-permute-start | bytes 688136 | tf_op jit(solution)/shard_map/ppermute | solution.py:133
  100.6 19.5 %all-to-all-start.3 = ((bf16[16,16,8,256]{3,2,1,0:T(8,128)(2,1)}), bf16[16,16,8,256]{3,2,1,0:T(8,128)(2,1)S(1)}, u32[]{:S(2)}, u32[]{:S(2)}) async-start(bf16[16,16,8,256]{3,2,1,0:T(8,128)(2,1)} %broadcast_in_dim.60), calls=%async_computation.3 | async-start | bytes 2097152 | tf_op jit(solution)/shard_map/all_to_all | solution.py:47
  114.2 18.7 %collective-permute-start.3 = (bf16[256,448]{1,0:T(8,128)(2,1)}, bf16[256,448]{1,0:T(8,128)(2,1)}, u32[]{:S(2)}, u32[]{:S(2)}) collective-permute-start(bf16[256,448]{1,0:T(8,128)(2,1)} %collective-permute-done.2), channel_id=1, source_target_pairs={{0,256},{16,816},{64,320},{80,880},{128,384},{144,944},{192,448},{... | collective-permute-start | bytes 688136 | tf_op jit(solution)/shard_map/ppermute | solution.py:151
  132.9 3.9 %collective-permute-start.5 = (bf16[256,448]{1,0:T(8,128)(2,1)}, bf16[256,448]{1,0:T(8,128)(2,1)S(1)}, u32[]{:S(2)}, u32[]{:S(2)}) collective-permute-start(bf16[256,448]{1,0:T(8,128)(2,1)} %collective-permute-done.3), channel_id=1, source_target_pairs={{0,16},{16,0},{1,17},{17,1},{2,18},{18,2},{3,19},{19,3},{4,20},{20... | collective-permute-start | bytes 688136 | tf_op jit(solution)/shard_map/ppermute | solution.py:156
  134.8 22.3 %collective-permute-start.4 = (bf16[256,448]{1,0:T(8,128)(2,1)}, bf16[256,448]{1,0:T(8,128)(2,1)}, u32[]{:S(2)}, u32[]{:S(2)}) collective-permute-start(bf16[256,448]{1,0:T(8,128)(2,1)} %collective-permute-done.3), channel_id=1, source_target_pairs={{0,256},{16,816},{64,320},{80,880},{128,384},{144,944},{192,448},{... | collective-permute-start | bytes 688136 | tf_op jit(solution)/shard_map/ppermute | solution.py:155
  140.0 21.6 %collective-permute-start.7 = (bf16[4,256,256]{2,1,0:T(8,128)(2,1)S(1)}, bf16[4,256,256]{2,1,0:T(8,128)(2,1)}, u32[]{:S(2)}, u32[]{:S(2)}) collective-permute-start(bf16[4,256,256]{2,1,0:T(8,128)(2,1)S(1)} %get-tuple-element.706), channel_id=1, source_target_pairs={{0,16},{16,0},{1,17},{17,1},{2,18},{18,2},{3,19},{19,3},{4,20},{20... | collective-permute-start | bytes 1572872 | tf_op jit(solution)/shard_map/ppermute | solution.py:169
  142.7 25.2 %all-to-all-start.4 = ((bf16[16,4,8,1024]{3,2,1,0:T(8,128)(2,1)}), bf16[16,4,8,1024]{3,2,1,0:T(8,128)(2,1)S(1)}, u32[]{:S(2)}, u32[]{:S(2)}) async-start(bf16[16,4,8,1024]{3,2,1,0:T(8,128)(2,1)} %bitcast.28), calls=%async_computation.4 | async-start | bytes 2097152 | tf_op jit(solution)/shard_map/all_to_all | solution.py:168
  157.2 25.1 %collective-permute-start.6 = (bf16[256,448]{1,0:T(8,128)(2,1)}, bf16[256,448]{1,0:T(8,128)(2,1)}, u32[]{:S(2)}, u32[]{:S(2)}) collective-permute-start(bf16[256,448]{1,0:T(8,128)(2,1)} %collective-permute-done.4), channel_id=1, source_target_pairs={{0,256},{16,816},{64,320},{80,880},{128,384},{144,944},{192,448},{... | collective-permute-start | bytes 688136 | tf_op jit(solution)/shard_map/ppermute | solution.py:173
  171.3 10.9 %all-to-all-start.5 = ((f32[4,8,1024]{2,1,0:T(8,128)}), f32[4,8,1024]{2,1,0:T(8,128)S(1)}, u32[]{:S(2)}, u32[]{:S(2)}) async-start(f32[4,8,1024]{2,1,0:T(8,128)} %convert_reduce_fusion), calls=%async_computation.5 | async-start | bytes 262144 | tf_op jit(solution)/shard_map/all_to_all | solution.py:181
  184.2 3.8 %collective-permute-start.9 = (f32[256,448]{1,0:T(8,128)S(1)}, f32[256,448]{1,0:T(8,128)S(1)}, u32[]{:S(2)}, u32[]{:S(2)}) collective-permute-start(f32[256,448]{1,0:T(8,128)S(1)} %copy.42), channel_id=1, source_target_pairs={{0,16},{16,0},{1,17},{17,1},{2,18},{18,2},{3,19},{19,3},{4,20},{20... | collective-permute-start | bytes 1376264 | tf_op jit(solution)/shard_map/ppermute | solution.py:186
  188.8 19.0 %all-to-all-start.6 = ((bf16[4,64,448]{2,1,0:T(8,128)(2,1)}), bf16[4,64,448]{2,1,0:T(8,128)(2,1)S(1)}, u32[]{:S(2)}, u32[]{:S(2)}) async-start(bf16[4,64,448]{2,1,0:T(8,128)(2,1)} %bitcast.36), calls=%async_computation.6 | async-start | bytes 524288 | tf_op jit(solution)/shard_map/all_to_all | solution.py:189
  192.7 14.5 %collective-permute-start.8 = (bf16[8,1024]{1,0:T(8,128)(2,1)S(1)}, bf16[8,1024]{1,0:T(8,128)(2,1)S(1)}, u32[]{:S(2)}, u32[]{:S(2)}) collective-permute-start(bf16[8,1024]{1,0:T(8,128)(2,1)S(1)} %reduce_sum.19), channel_id=1, source_target_pairs={{0,512},{256,768},{512,0},{768,256},{1,513},{257,769},{513,1},{769... | collective-permute-start | bytes 49160 | tf_op jit(solution)/shard_map/ppermute | solution.py:183
